TPU v7x, 128 devices: a whole 4x4x4 slice. The times are simulated.
128 devices in a mesh: gx: 16 (over x, y), gz: 8 (over z, core).
Axes of the slice: x: 4, y: 4, z: 4, core: 2. Of those that a mesh axis runs over, the one named last changes fastest.
Arguments:
- pressure_now: float32 [256, 256, 512], P('gz', 'gx'), may hold values from -6 to 6
- pressure_prev: float32 [256, 256, 512], P('gz', 'gx'), may hold values from -6 to 6
- adjoint_now: float32 [256, 256, 512], P('gz', 'gx'), may hold values from -6 to 6
- adjoint_prev: float32 [256, 256, 512], P('gz', 'gx'), may hold values from -6 to 6
- speed2: float32 [256, 256, 512], P('gz', 'gx'), may hold values from 0.05 to 0.32
- layer_state: float32 [16384, 64, 128], P(('gx', 'gz')), may hold values from -3 to 3
- layer_maps: float32 [8, 64, 64], replicated, as said below
- send_rows: int32 [128, 128, 1], P(('gx', 'gz')), may hold values from -1 to 2047, as said below
- slot_patch: int32 [16384], P(('gx', 'gz')), may hold values from 0 to 1023
- patch_material: int32 [1024], replicated, may hold values from 0 to 7
Outputs:
- pressure_out: float32 [256, 256, 512], P('gz', 'gx')
- adjoint_out: float32 [256, 256, 512], P('gz', 'gx')
- patch_gradient: float32 [1024, 128], P(('gx', 'gz'))
Inputs may be any that keep to these rules, and one draw needn't show every extreme that they name: `send_rows`: each device's non-negative entries are distinct rows of its tile; -1 marks an unused entry; for one device every entry aimed at it is used. `layer_maps`: each material's matrix has diagonal entries from 0.5 to 0.9.
All inputs are finite; a program needn't handle non-finite values.
Results may differ from a plain program's by a relative error of at most 0.00016.
Values sent between devices are 32-bit elements; how exact they have to be, the bound alone decides.
No kernel may reach another device: no remote copies, remote signals or barrier semaphores. Data moves between devices by JAX's collectives and lax.ppermute only.
A program may use at most 192 MiB of HBM per device.

v0:
```python
import jax
import jax.numpy as jnp
from jax import lax
from jax.sharding import PartitionSpec as P

STEPS = 4


KAPPA = 0.5
BETA = 0.3


def with_halo(block, sides, width):
    for axis, dim in sides:
        count = lax.axis_size(axis)
        forward = [(i, i + 1) for i in range(count - 1)]
        backward = [(target, source) for source, target in forward]
        low = lax.ppermute(
            lax.slice_in_dim(block, block.shape[dim] - width, None, axis=dim), axis, forward
        )
        high = lax.ppermute(lax.slice_in_dim(block, 0, width, axis=dim), axis, backward)
        block = jnp.concatenate([low, block, high], axis=dim)
    return block


def advance(fields, previous, speed2, padded):
    along = jnp.pad(fields, ((0, 0), (0, 0), (0, 0), (1, 1)))
    beside = padded[:, 2:, 1:-1, :] + padded[:, :-2, 1:-1, :]
    beside = beside + padded[:, 1:-1, 2:, :] + padded[:, 1:-1, :-2, :]
    beside = beside + along[:, :, :, 2:] + along[:, :, :, :-2]
    return 2.0 * fields - previous + speed2[None] * (beside - 6.0 * fields)


def pick_rows(fields, sources, width):
    batch = fields.shape[0]
    rows = fields.reshape(batch, -1, width)
    flat = sources.reshape(-1)
    picked = jnp.take(rows, jnp.maximum(flat, 0), axis=1)
    return jnp.where((flat >= 0)[None, :, None], picked, 0.0)


def layer_update(layer, maps, air):
    push = KAPPA * (air - layer[:, :, 0, :])
    fresh = jnp.einsum("bsij,bsjw->bsiw", maps, layer, precision=lax.Precision.HIGHEST)
    return fresh + maps[:, :, :, 0][:, :, :, None] * push[:, :, None, :]


def couple(fields, sources, picked, back):
    batch = fields.shape[0]
    width = picked.shape[-1]
    flat = sources.reshape(-1)
    total = fields.shape[1] * fields.shape[2] * fields.shape[3] // width
    delta = jnp.where((flat >= 0)[None, :, None], BETA * (back - picked), 0.0)
    target = jnp.where(flat >= 0, flat, total)
    coupling = jnp.zeros((batch, total, width), jnp.float32).at[:, target].add(delta, mode="drop")
    return coupling.reshape(fields.shape)


def body(
    pressure_now,
    pressure_prev,
    adjoint_now,
    adjoint_prev,
    speed2,
    layer_state,
    layer_maps,
    send_rows,
    slot_patch,
    patch_material,
):
    slots = layer_state.shape[0]
    width = layer_state.shape[2]
    devices = lax.axis_size(("gx", "gz"))
    sources = send_rows[0]
    cap = sources.shape[1]
    patches = patch_material.shape[0]
    materials = jnp.take(patch_material, slot_patch)
    forward_maps = jnp.take(layer_maps, materials, axis=0)
    adjoint_maps = jnp.swapaxes(forward_maps, 1, 2)
    owners = (slot_patch[:, None] == jnp.arange(patches, dtype=jnp.int32)[None, :]).astype(
        jnp.float32
    )

    def step_pair(fields, previous, layer, maps, halo_fn, out_fn, back_fn):
        batch = fields.shape[0]
        picked = pick_rows(fields, sources, width)
        air = out_fn(picked.reshape(batch, devices, cap, width)).reshape(batch, slots, width)
        fresh = layer_update(layer, maps, air)
        back = back_fn(fresh[:, :, 0, :].reshape(batch, devices, cap, width)).reshape(
            batch, devices * cap, width
        )
        padded = halo_fn(fields)
        following = advance(fields, previous, speed2, padded) + couple(
            fields, sources, picked, back
        )
        return (following, fresh)

    gradient = jnp.zeros((patches // devices, width), jnp.float32)
    summed = jnp.zeros((slots, width), jnp.float32)

    def halo_single(fields):
        return with_halo(fields, (("gx", 2), ("gz", 1)), 1)

    def out_single(picked):
        return lax.all_to_all(picked, ("gx", "gz"), split_axis=1, concat_axis=1, tiled=True)

    def back_single(rims):
        return lax.all_to_all(rims, ("gx", "gz"), split_axis=1, concat_axis=1, tiled=True)

    current, earlier, layer = (pressure_now[None], pressure_prev[None], layer_state[None])
    stored = []
    for step in range(STEPS):
        following, layer = step_pair(
            current, earlier, layer, forward_maps[None], halo_single, out_single, back_single
        )
        earlier, current = (current, following)
        stored.append(layer[0])
    pressure_out = current[0]
    current, earlier = (adjoint_now[None], adjoint_prev[None])
    layer = jnp.zeros_like(layer_state)[None]
    for step in range(STEPS):
        following, layer = step_pair(
            current, earlier, layer, adjoint_maps[None], halo_single, out_single, back_single
        )
        earlier, current = (current, following)
        gather_gradient = gradient
        gather_gradient = gather_gradient + lax.psum_scatter(
            jnp.einsum(
                "sp,sw->pw",
                owners,
                jnp.sum(stored[STEPS - 1 - step] * layer[0], axis=1),
                precision=lax.Precision.HIGHEST,
            ),
            ("gx", "gz"),
            scatter_dimension=0,
            tiled=True,
        )
        gradient, summed = (gather_gradient, summed)
    adjoint_out = current[0]
    return (pressure_out, adjoint_out, gradient)


def solution(mesh):
    in_specs = (
        P("gz", "gx", None),
        P("gz", "gx", None),
        P("gz", "gx", None),
        P("gz", "gx", None),
        P("gz", "gx", None),
        P(("gx", "gz"), None, None),
        P(),
        P(("gx", "gz"), None, None),
        P(("gx", "gz")),
        P(),
    )
    out_specs = (P("gz", "gx", None), P("gz", "gx", None), P(("gx", "gz"), None))
    return jax.shard_map(body, mesh=mesh, in_specs=in_specs, out_specs=out_specs, check_vma=False)
```

profile of v0, /device:TPU:1, one launch (start us, length us, event | category | flops | bytes accessed | tf_op | source)
XLA Modules:
  0.0 688.5 jit_solution(14261502849842861366)
XLA Ops:
  27.6 14.8 %all-to-all-start.8 = ((f32[1,128,1,128]{3,2,0,1:T(1,128)}), f32[1,128,1,128]{3,2,0,1:T(1,128)S(1)}, u32[]{:S(2)}, u32[]{:S(2)}) async-start(f32[1,128,1,128]{3,2,0,1:T(1,128)} %bitcast.57), calls=%async_computation.8 | async-start | bytes 131072 | tf_op jit(solution)/shard_map/all_to_all | solution.py:105
  48.2 10.5 %fusion.17 = f32[128,64,128]{2,1,0:T(8,128)} fusion(f32[128,64,64]{2,1,0:T(8,128)} %gather_fusion.1, pred[128]{0:T(512)(128)(4,1)S(1)} %get-tuple-element.10), kind=kOutput, calls=%fused_computation.49 | convolution fusion | flops 805830656 | bytes 6291584 | tf_op jit(solution)/shard_map/bsij,bsjw->bsiw/dot_general | solution.py:44
  76.7 13.6 %fusion.8 = f32[128,64,128]{2,1,0:T(8,128)} fusion(f32[128,64,128]{2,1,0:T(8,128)} %fusion.17, f32[128,64,64]{2,1,0:T(8,128)} %gather_fusion.1, f32[128,128]{1,0:T(8,128)S(1)} %bitcast.261, f32[128,64]{1,0:T(8,128)S(1)} %bitcast.243, pred[128]{0:T(512)(128)(4,1)S(1)} %get-tuple-element.10), kind=kOutput, calls=%fused_computation.39 | convolution fusion | flops 807927808 | bytes 10584192 | tf_op jit(solution)/shard_map/bsij,bsjw->bsiw/dot_general | solution.py:44
  94.4 9.8 %all-to-all-start.9 = ((f32[1,128,1,128]{3,2,0,1:T(1,128)}), f32[1,128,1,128]{3,2,0,1:T(1,128)S(1)}, u32[]{:S(2)}, u32[]{:S(2)}) async-start(f32[1,128,1,128]{3,2,0,1:T(1,128)} %slice_bitcast_fusion.4), calls=%async_computation.9 | async-start | bytes 131072 | tf_op jit(solution)/shard_map/all_to_all | solution.py:108
  131.1 10.0 %all-to-all-start.10 = ((f32[1,128,1,128]{3,2,0,1:T(1,128)}), f32[1,128,1,128]{3,2,0,1:T(1,128)}, u32[]{:S(2)}, u32[]{:S(2)}) async-start(f32[1,128,1,128]{3,2,0,1:T(1,128)} %bitcast.66), calls=%async_computation.10 | async-start | bytes 131072 | tf_op jit(solution)/shard_map/all_to_all | solution.py:105
  157.9 10.7 %all-to-all-start.11 = ((f32[1,128,1,128]{3,2,0,1:T(1,128)}), f32[1,128,1,128]{3,2,0,1:T(1,128)}, u32[]{:S(2)}, u32[]{:S(2)}) async-start(f32[1,128,1,128]{3,2,0,1:T(1,128)} %slice_bitcast_fusion.3), calls=%async_computation.11 | async-start | bytes 131072 | tf_op jit(solution)/shard_map/all_to_all | solution.py:108
  176.0 13.5 %fusion.10 = f32[128,64,128]{2,1,0:T(8,128)} fusion(f32[128,64,128]{2,1,0:T(8,128)} %fusion.8, f32[128,64,64]{2,1,0:T(8,128)} %gather_fusion.1, f32[128,128]{1,0:T(8,128)S(1)} %bitcast.250, f32[128,64]{1,0:T(8,128)S(1)} %bitcast.246, pred[128]{0:T(512)(128)(4,1)S(1)} %get-tuple-element.10), kind=kOutput, calls=%fused_computation.41 | convolution fusion | flops 807927808 | bytes 10584192 | tf_op jit(solution)/shard_map/bsij,bsjw->bsiw/dot_general | solution.py:44
  203.7 9.5 %all-to-all-start = ((f32[1,128,1,128]{3,2,0,1:T(1,128)}), f32[1,128,1,128]{3,2,0,1:T(1,128)S(1)}, u32[]{:S(2)}, u32[]{:S(2)}) async-start(f32[1,128,1,128]{3,2,0,1:T(1,128)} %bitcast.13), calls=%async_computation | async-start | bytes 131072 | tf_op jit(solution)/shard_map/all_to_all | solution.py:105
  222.5 10.1 %all-to-all-start.12 = ((f32[1,128,1,128]{3,2,0,1:T(1,128)}), f32[1,128,1,128]{3,2,0,1:T(1,128)S(1)}, u32[]{:S(2)}, u32[]{:S(2)}) async-start(f32[1,128,1,128]{3,2,0,1:T(1,128)} %bitcast.75), calls=%async_computation.12 | async-start | bytes 131072 | tf_op jit(solution)/shard_map/all_to_all | solution.py:105
  233.8 10.4 %fusion.2 = f32[128,64,128]{2,1,0:T(8,128)} fusion(f32[128,64,128]{2,1,0:T(8,128)} %fusion.22, f32[128,64,64]{2,1,0:T(8,128)} %gather_fusion.1, f32[128,128]{1,0:T(8,128)S(1)} %bitcast.252, f32[128,64]{1,0:T(8,128)S(1)} %bitcast.236, pred[128]{0:T(512)(128)(4,1)S(1)} %get-tuple-element.10), kind=kOutput, calls=%fused_computation.33 | convolution fusion | flops 807927808 | bytes 10584192 | tf_op jit(solution)/shard_map/bsij,bsjw->bsiw/dot_general | solution.py:44
  255.2 10.2 %all-to-all-start.13 = ((f32[1,128,1,128]{3,2,0,1:T(1,128)}), f32[1,128,1,128]{3,2,0,1:T(1,128)}, u32[]{:S(2)}, u32[]{:S(2)}) async-start(f32[1,128,1,128]{3,2,0,1:T(1,128)} %slice_bitcast_fusion.2), calls=%async_computation.13 | async-start | bytes 131072 | tf_op jit(solution)/shard_map/all_to_all | solution.py:108
  274.7 9.4 %all-to-all-start.1 = ((f32[1,128,1,128]{3,2,0,1:T(1,128)}), f32[1,128,1,128]{3,2,0,1:T(1,128)}, u32[]{:S(2)}, u32[]{:S(2)}) async-start(f32[1,128,1,128]{3,2,0,1:T(1,128)} %slice_bitcast_fusion.7), calls=%async_computation.1 | async-start | bytes 131072 | tf_op jit(solution)/shard_map/all_to_all | solution.py:108
  307.5 9.8 %all-to-all-start.2 = ((f32[1,128,1,128]{3,2,0,1:T(1,128)}), f32[1,128,1,128]{3,2,0,1:T(1,128)S(1)}, u32[]{:S(2)}, u32[]{:S(2)}) async-start(f32[1,128,1,128]{3,2,0,1:T(1,128)} %bitcast.23), calls=%async_computation.2 | async-start | bytes 131072 | tf_op jit(solution)/shard_map/all_to_all | solution.py:105
  330.5 14.1 %all-to-all-start.14 = ((f32[1,128,1,128]{3,2,0,1:T(1,128)}), f32[1,128,1,128]{3,2,0,1:T(1,128)}, u32[]{:S(2)}, u32[]{:S(2)}) async-start(f32[1,128,1,128]{3,2,0,1:T(1,128)} %bitcast.84), calls=%async_computation.14 | async-start | bytes 131072 | tf_op jit(solution)/shard_map/all_to_all | solution.py:105
  345.7 10.5 %fusion.4 = f32[128,64,128]{2,1,0:T(8,128)} fusion(f32[128,64,128]{2,1,0:T(8,128)} %fusion.2, f32[128,64,64]{2,1,0:T(8,128)} %gather_fusion.1, f32[128,128]{1,0:T(8,128)S(1)} %bitcast.255, f32[128,64]{1,0:T(8,128)S(1)} %bitcast.238, pred[128]{0:T(512)(128)(4,1)S(1)} %get-tuple-element.10), kind=kOutput, calls=%fused_computation.35 | convolution fusion | flops 807927808 | bytes 10584192 | tf_op jit(solution)/shard_map/bsij,bsjw->bsiw/dot_general | solution.py:44
  360.4 10.2 %all-to-all-start.3 = ((f32[1,128,1,128]{3,2,0,1:T(1,128)}), f32[1,128,1,128]{3,2,0,1:T(1,128)}, u32[]{:S(2)}, u32[]{:S(2)}) async-start(f32[1,128,1,128]{3,2,0,1:T(1,128)} %slice_bitcast_fusion.6), calls=%async_computation.3 | async-start | bytes 131072 | tf_op jit(solution)/shard_map/all_to_all | solution.py:108
  397.4 9.5 %all-to-all-start.4 = ((f32[1,128,1,128]{3,2,0,1:T(1,128)}), f32[1,128,1,128]{3,2,0,1:T(1,128)S(1)}, u32[]{:S(2)}, u32[]{:S(2)}) async-start(f32[1,128,1,128]{3,2,0,1:T(1,128)} %bitcast.32), calls=%async_computation.4 | async-start | bytes 131072 | tf_op jit(solution)/shard_map/all_to_all | solution.py:105
  424.1 10.6 %all-to-all-start.5 = ((f32[1,128,1,128]{3,2,0,1:T(1,128)}), f32[1,128,1,128]{3,2,0,1:T(1,128)}, u32[]{:S(2)}, u32[]{:S(2)}) async-start(f32[1,128,1,128]{3,2,0,1:T(1,128)} %slice_bitcast_fusion.5), calls=%async_computation.5 | async-start | bytes 131072 | tf_op jit(solution)/shard_map/all_to_all | solution.py:108
  441.6 10.2 %fusion.6 = f32[128,64,128]{2,1,0:T(8,128)} fusion(f32[128,64,128]{2,1,0:T(8,128)} %fusion.4, f32[128,64,64]{2,1,0:T(8,128)} %gather_fusion.1, f32[128,128]{1,0:T(8,128)S(1)} %bitcast.259, f32[128,64]{1,0:T(8,128)S(1)} %bitcast.241, pred[128]{0:T(512)(128)(4,1)S(1)} %get-tuple-element.10), kind=kOutput, calls=%fused_computation.37 | convolution fusion | flops 807927808 | bytes 10584192 | tf_op jit(solution)/shard_map/bsij,bsjw->bsiw/dot_general | solution.py:44
  464.1 9.5 %all-to-all-start.6 = ((f32[1,128,1,128]{3,2,0,1:T(1,128)}), f32[1,128,1,128]{3,2,0,1:T(1,128)S(1)}, u32[]{:S(2)}, u32[]{:S(2)}) async-start(f32[1,128,1,128]{3,2,0,1:T(1,128)} %bitcast.41), calls=%async_computation.6 | async-start | bytes 131072 | tf_op jit(solution)/shard_map/all_to_all | solution.py:105
  484.0 23.3 %multiply_reduce_fusion = (f32[128,128]{1,0:T(8,128)}, f32[128,128]{1,0:T(8,128)}, f32[128,128]{1,0:T(8,128)}, f32[128,128]{1,0:T(8,128)}, f32[1,128,64,128]{3,2,1,0:T(8,128)S(1)}, /*index=5*/f32[1,128,64,128]{3,2,1,0:T(8,128)}) fusion(f32[128,64,128]{2,1,0:T(8,128)} %fusion.22, f32[128,128]{1,0:T(8,128)} %bitcast.266, f32[128,64]{1,0:T(8,128)S(1)} %bitcast.248, ...), kind=kOutput, calls=%fused_computation.19 | convolution fusion | flops 833028096 | bytes 40697984 | tf_op jit(solution)/shard_map/bsij,bsjw->bsiw/dot_general | solution.py:44
  508.0 10.3 %all-to-all-start.7 = ((f32[1,128,1,128]{3,2,0,1:T(1,128)}), f32[1,128,1,128]{3,2,0,1:T(1,128)S(1)}, u32[]{:S(2)}, u32[]{:S(2)}) async-start(f32[1,128,1,128]{3,2,0,1:T(1,128)} %slice_bitcast_fusion.1), calls=%async_computation.7 | async-start | bytes 131072 | tf_op jit(solution)/shard_map/all_to_all | solution.py:108
  533.3 9.5 %all-to-all-start.15 = ((f32[1,128,1,128]{3,2,0,1:T(1,128)}), f32[1,128,1,128]{3,2,0,1:T(1,128)S(1)}, u32[]{:S(2)}, u32[]{:S(2)}) async-start(f32[1,128,1,128]{3,2,0,1:T(1,128)} %slice_bitcast_fusion), calls=%async_computation.15 | async-start | bytes 131072 | tf_op jit(solution)/shard_map/all_to_all | solution.py:108
  561.7 118.5 %all-reduce.11.cloned.1.call-done = f32[1024,128]{1,0:T(8,128)} async-done(((f32[1024,128]{1,0:T(8,128)}), f32[1024,128]{1,0:T(8,128)}) %all-reduce.11.cloned.1.call-update) | async-done | bytes 524304
  (248 shorter events, 295.1 us)
Async XLA Ops:
  9.2 95.0 %collective-permute-start.17 = (f32[1,32,1,512]{3,2,1,0:T(1,128)}, f32[1,32,1,512]{3,2,1,0:T(1,128)}, u32[]{:S(2)}, u32[]{:S(2)}) collective-permute-start(f32[1,32,1,512]{3,2,1,0:T(1,128)} %get-tuple-element.36), channel_id=1, source_target_pairs={{8,0},{16,8},{24,16},{32,24},{40,32},{48,40},{56,48},{64,56},{72,6... | collective-permute-start | bytes 196616 | tf_op jit(solution)/shard_map/ppermute | solution.py:21
  10.5 93.7 %collective-permute-start.16 = (f32[1,32,1,512]{3,2,1,0:T(1,128)}, f32[1,32,1,512]{3,2,1,0:T(1,128)}, u32[]{:S(2)}, u32[]{:S(2)}) collective-permute-start(f32[1,32,1,512]{3,2,1,0:T(1,128)} %get-tuple-element.37), channel_id=1, source_target_pairs={{0,8},{8,16},{16,24},{24,32},{32,40},{40,48},{48,56},{56,64},{64,7... | collective-permute-start | bytes 196616 | tf_op jit(solution)/shard_map/ppermute | solution.py:18
  17.7 93.4 %collective-permute-start.1 = (f32[1,32,1,512]{3,2,1,0:T(1,128)}, f32[1,32,1,512]{3,2,1,0:T(1,128)S(1)}, u32[]{:S(2)}, u32[]{:S(2)}) collective-permute-start(f32[1,32,1,512]{3,2,1,0:T(1,128)} %get-tuple-element.44), channel_id=1, source_target_pairs={{8,0},{16,8},{24,16},{32,24},{40,32},{48,40},{56,48},{64,56},{72,6... | collective-permute-start | bytes 196616 | tf_op jit(solution)/shard_map/ppermute | solution.py:21
  19.0 92.1 %collective-permute-start = (f32[1,32,1,512]{3,2,1,0:T(1,128)}, f32[1,32,1,512]{3,2,1,0:T(1,128)}, u32[]{:S(2)}, u32[]{:S(2)}) collective-permute-start(f32[1,32,1,512]{3,2,1,0:T(1,128)} %get-tuple-element.45), channel_id=1, source_target_pairs={{0,8},{8,16},{16,24},{24,32},{32,40},{40,48},{48,56},{56,64},{64,7... | collective-permute-start | bytes 196616 | tf_op jit(solution)/shard_map/ppermute | solution.py:18
  27.6 49.0 %all-to-all-start.8 = ((f32[1,128,1,128]{3,2,0,1:T(1,128)}), f32[1,128,1,128]{3,2,0,1:T(1,128)S(1)}, u32[]{:S(2)}, u32[]{:S(2)}) async-start(f32[1,128,1,128]{3,2,0,1:T(1,128)} %bitcast.57), calls=%async_computation.8 | async-start | bytes 131072 | tf_op jit(solution)/shard_map/all_to_all | solution.py:105
  112.5 188.6 %collective-permute-start.2 = (f32[1,1,18,512]{3,2,1,0:T(8,128)}, f32[1,1,18,512]{3,2,1,0:T(8,128)}, u32[]{:S(2)}, u32[]{:S(2)}) collective-permute-start(f32[1,1,18,512]{3,2,1,0:T(8,128)} %get-tuple-element.28), channel_id=1, source_target_pairs={{1,0},{2,1},{3,2},{4,3},{5,4},{6,5},{7,6},{9,8},{10,9},{11,10},{12... | collective-permute-start | bytes 110600 | tf_op jit(solution)/shard_map/ppermute | solution.py:21
  114.8 186.3 %collective-permute-start.3 = (f32[1,1,18,512]{3,2,1,0:T(8,128)}, f32[1,1,18,512]{3,2,1,0:T(8,128)}, u32[]{:S(2)}, u32[]{:S(2)}) collective-permute-start(f32[1,1,18,512]{3,2,1,0:T(8,128)} %get-tuple-element.29), channel_id=1, source_target_pairs={{0,1},{1,2},{2,3},{3,4},{4,5},{5,6},{6,7},{8,9},{9,10},{10,11},{11... | collective-permute-start | bytes 110600 | tf_op jit(solution)/shard_map/ppermute | solution.py:18
  143.0 25.6 %collective-permute-start.21 = (f32[1,32,1,512]{3,2,1,0:T(1,128)}, f32[1,32,1,512]{3,2,1,0:T(1,128)S(1)}, u32[]{:S(2)}, u32[]{:S(2)}) collective-permute-start(f32[1,32,1,512]{3,2,1,0:T(1,128)} %get-tuple-element.34), channel_id=1, source_target_pairs={{8,0},{16,8},{24,16},{32,24},{40,32},{48,40},{56,48},{64,56},{72,6... | collective-permute-start | bytes 196616 | tf_op jit(solution)/shard_map/ppermute | solution.py:21
  157.9 31.6 %all-to-all-start.11 = ((f32[1,128,1,128]{3,2,0,1:T(1,128)}), f32[1,128,1,128]{3,2,0,1:T(1,128)}, u32[]{:S(2)}, u32[]{:S(2)}) async-start(f32[1,128,1,128]{3,2,0,1:T(1,128)} %slice_bitcast_fusion.3), calls=%async_computation.11 | async-start | bytes 131072 | tf_op jit(solution)/shard_map/all_to_all | solution.py:108
  215.2 50.2 %collective-permute-start.25 = (f32[1,32,1,512]{3,2,1,0:T(1,128)}, f32[1,32,1,512]{3,2,1,0:T(1,128)S(1)}, u32[]{:S(2)}, u32[]{:S(2)}) collective-permute-start(f32[1,32,1,512]{3,2,1,0:T(1,128)} %get-tuple-element.32), channel_id=1, source_target_pairs={{8,0},{16,8},{24,16},{32,24},{40,32},{48,40},{56,48},{64,56},{72,6... | collective-permute-start | bytes 196616 | tf_op jit(solution)/shard_map/ppermute | solution.py:21
  216.4 49.0 %collective-permute-start.24 = (f32[1,32,1,512]{3,2,1,0:T(1,128)}, f32[1,32,1,512]{3,2,1,0:T(1,128)}, u32[]{:S(2)}, u32[]{:S(2)}) collective-permute-start(f32[1,32,1,512]{3,2,1,0:T(1,128)} %get-tuple-element.33), channel_id=1, source_target_pairs={{0,8},{8,16},{16,24},{24,32},{32,40},{40,48},{48,56},{56,64},{64,7... | collective-permute-start | bytes 196616 | tf_op jit(solution)/shard_map/ppermute | solution.py:18
  318.0 61.3 %collective-permute-start.29 = (f32[1,32,1,512]{3,2,1,0:T(1,128)}, f32[1,32,1,512]{3,2,1,0:T(1,128)S(1)}, u32[]{:S(2)}, u32[]{:S(2)}) collective-permute-start(f32[1,32,1,512]{3,2,1,0:T(1,128)} %get-tuple-element.30), channel_id=1, source_target_pairs={{8,0},{16,8},{24,16},{32,24},{40,32},{48,40},{56,48},{64,56},{72,6... | collective-permute-start | bytes 196616 | tf_op jit(solution)/shard_map/ppermute | solution.py:21
  319.3 60.0 %collective-permute-start.28 = (f32[1,32,1,512]{3,2,1,0:T(1,128)}, f32[1,32,1,512]{3,2,1,0:T(1,128)}, u32[]{:S(2)}, u32[]{:S(2)}) collective-permute-start(f32[1,32,1,512]{3,2,1,0:T(1,128)} %get-tuple-element.31), channel_id=1, source_target_pairs={{0,8},{8,16},{16,24},{24,32},{32,40},{40,48},{48,56},{56,64},{64,7... | collective-permute-start | bytes 196616 | tf_op jit(solution)/shard_map/ppermute | solution.py:18
  323.9 48.5 %collective-permute-start.5 = (f32[1,32,1,512]{3,2,1,0:T(1,128)}, f32[1,32,1,512]{3,2,1,0:T(1,128)}, u32[]{:S(2)}, u32[]{:S(2)}) collective-permute-start(f32[1,32,1,512]{3,2,1,0:T(1,128)} %get-tuple-element.42), channel_id=1, source_target_pairs={{8,0},{16,8},{24,16},{32,24},{40,32},{48,40},{56,48},{64,56},{72,6... | collective-permute-start | bytes 196616 | tf_op jit(solution)/shard_map/ppermute | solution.py:21
  325.2 47.2 %collective-permute-start.4 = (f32[1,32,1,512]{3,2,1,0:T(1,128)}, f32[1,32,1,512]{3,2,1,0:T(1,128)}, u32[]{:S(2)}, u32[]{:S(2)}) collective-permute-start(f32[1,32,1,512]{3,2,1,0:T(1,128)} %get-tuple-element.43), channel_id=1, source_target_pairs={{0,8},{8,16},{16,24},{24,32},{32,40},{40,48},{48,56},{56,64},{64,7... | collective-permute-start | bytes 196616 | tf_op jit(solution)/shard_map/ppermute | solution.py:18
  330.5 29.9 %all-to-all-start.14 = ((f32[1,128,1,128]{3,2,0,1:T(1,128)}), f32[1,128,1,128]{3,2,0,1:T(1,128)}, u32[]{:S(2)}, u32[]{:S(2)}) async-start(f32[1,128,1,128]{3,2,0,1:T(1,128)} %bitcast.84), calls=%async_computation.14 | async-start | bytes 131072 | tf_op jit(solution)/shard_map/all_to_all | solution.py:105
  360.4 26.0 %all-to-all-start.3 = ((f32[1,128,1,128]{3,2,0,1:T(1,128)}), f32[1,128,1,128]{3,2,0,1:T(1,128)}, u32[]{:S(2)}, u32[]{:S(2)}) async-start(f32[1,128,1,128]{3,2,0,1:T(1,128)} %slice_bitcast_fusion.6), calls=%async_computation.3 | async-start | bytes 131072 | tf_op jit(solution)/shard_map/all_to_all | solution.py:108
  380.8 174.3 %collective-permute-start.30 = (f32[1,1,18,512]{3,2,1,0:T(8,128)}, f32[1,1,18,512]{3,2,1,0:T(8,128)}, u32[]{:S(2)}, u32[]{:S(2)}) collective-permute-start(f32[1,1,18,512]{3,2,1,0:T(8,128)} %get-tuple-element.14), channel_id=1, source_target_pairs={{1,0},{2,1},{3,2},{4,3},{5,4},{6,5},{7,6},{9,8},{10,9},{11,10},{12... | collective-permute-start | bytes 110600 | tf_op jit(solution)/shard_map/ppermute | solution.py:21
  383.1 171.9 %collective-permute-start.31 = (f32[1,1,18,512]{3,2,1,0:T(8,128)}, f32[1,1,18,512]{3,2,1,0:T(8,128)}, u32[]{:S(2)}, u32[]{:S(2)}) collective-permute-start(f32[1,1,18,512]{3,2,1,0:T(8,128)} %get-tuple-element.15), channel_id=1, source_target_pairs={{0,1},{1,2},{2,3},{3,4},{4,5},{5,6},{6,7},{8,9},{9,10},{10,11},{11... | collective-permute-start | bytes 110600 | tf_op jit(solution)/shard_map/ppermute | solution.py:18
  408.9 25.8 %collective-permute-start.9 = (f32[1,32,1,512]{3,2,1,0:T(1,128)}, f32[1,32,1,512]{3,2,1,0:T(1,128)}, u32[]{:S(2)}, u32[]{:S(2)}) collective-permute-start(f32[1,32,1,512]{3,2,1,0:T(1,128)} %get-tuple-element.40), channel_id=1, source_target_pairs={{8,0},{16,8},{24,16},{32,24},{40,32},{48,40},{56,48},{64,56},{72,6... | collective-permute-start | bytes 196616 | tf_op jit(solution)/shard_map/ppermute | solution.py:21
  424.1 27.8 %all-to-all-start.5 = ((f32[1,128,1,128]{3,2,0,1:T(1,128)}), f32[1,128,1,128]{3,2,0,1:T(1,128)}, u32[]{:S(2)}, u32[]{:S(2)}) async-start(f32[1,128,1,128]{3,2,0,1:T(1,128)} %slice_bitcast_fusion.5), calls=%async_computation.5 | async-start | bytes 131072 | tf_op jit(solution)/shard_map/all_to_all | solution.py:108
  475.5 49.7 %collective-permute-start.13 = (f32[1,32,1,512]{3,2,1,0:T(1,128)}, f32[1,32,1,512]{3,2,1,0:T(1,128)}, u32[]{:S(2)}, u32[]{:S(2)}) collective-permute-start(f32[1,32,1,512]{3,2,1,0:T(1,128)} %get-tuple-element.38), channel_id=1, source_target_pairs={{8,0},{16,8},{24,16},{32,24},{40,32},{48,40},{56,48},{64,56},{72,6... | collective-permute-start | bytes 196616 | tf_op jit(solution)/shard_map/ppermute | solution.py:21
  477.0 48.2 %collective-permute-start.12 = (f32[1,32,1,512]{3,2,1,0:T(1,128)}, f32[1,32,1,512]{3,2,1,0:T(1,128)}, u32[]{:S(2)}, u32[]{:S(2)}) collective-permute-start(f32[1,32,1,512]{3,2,1,0:T(1,128)} %get-tuple-element.39), channel_id=1, source_target_pairs={{0,8},{8,16},{16,24},{24,32},{32,40},{40,48},{48,56},{56,64},{64,7... | collective-permute-start | bytes 196616 | tf_op jit(solution)/shard_map/ppermute | solution.py:18
  518.3 161.9 %all-reduce.11.cloned.1.call-start = ((), (), s32[]{:S(2)}) async-start(), calls=%async_computation.16 | async-start | bytes 1048576
  (56 other events, 1047.6 us)
Sparse Core Ops, SparseCore 0:
  533.4 146.7 all-reduce.10
where the time goes:
time: 699 us; the launch traced here: 688 us
  starting transfers between devices  261 us (37%)
  waiting for transfers between devices  125 us (18%)
  other arithmetic  105 us (15%)
  matrix products  105 us (15%)
  local copies, waits for them, and re-layouts  77.5 us (11%)
  between operations  15.2 us (2%)
    unnamed x2, waiting for transfers between devices  119 us
    dot_general x8, matrix products, layer_update(): jnp.einsum('bsij,bsjw->bsiw', maps, layer, precision=lax.Precision.HIGHEST)  98.2 us
    all_to_all x8, starting transfers between devices, out_single(): lax.all_to_all(picked, ('gx', 'gz'), split_axis=1, concat_axis=1, tiled=T...  87.2 us
    all_to_all x8, starting transfers between devices, back_single(): lax.all_to_all(rims, ('gx', 'gz'), split_axis=1, concat_axis=1, tiled=True)  80.7 us
    ppermute x16, starting transfers between devices, with_halo(): lax.ppermute(lax.slice_in_dim(block, block.shape[dim] - width, None, axis...  59.8 us
    ppermute x16, starting transfers between devices, with_halo(): lax.ppermute(lax.slice_in_dim(block, 0, width, axis=dim), axis, backward)  33.2 us
    add x6, other arithmetic, step_pair(): advance(fields, previous, speed2, padded)  24.9 us
    add x6, other arithmetic, layer_update(): return fresh + maps[:, :, :, 0][:, :, :, None] * push[:, :, None, :]  17.6 us
  transfers between devices with their start and end apart: 49, of which 6 were waited for; matrix products, arithmetic and copies ran while one was open for 39% of the time, Pallas kernels for 0%

commit v1 on v0

v1 whole, which is shorter than its diff:
```python
import functools

import jax
import jax.numpy as jnp
from jax import lax
from jax.experimental import pallas as pl
from jax.experimental.pallas import tpu as pltpu
from jax.sharding import PartitionSpec as P

STEPS = 4
KAPPA = 0.5
BETA = 0.3
TERMS = STEPS + 1
LINES = 8
META = TERMS
MIB = 1 << 20
VMEM = pltpu.VMEM
SMEM = pltpu.SMEM


def params(mib):
    return pltpu.CompilerParams(vmem_limit_bytes=mib * MIB)


def surface_kernel(block, maps, patch_ref, material_ref, layer, out, vectors, scalars):
    depth = maps.shape[1]
    width = layer.shape[2]
    mats = maps.shape[0]

    @pl.when(pl.program_id(0) == 0)
    def _():
        lane = lax.broadcasted_iota(jnp.int32, (1, width), 1)
        first = lax.broadcasted_iota(jnp.int32, (depth, 1), 0) == 0
        for mat in range(mats):
            matrix = maps[mat]
            turned = matrix.T
            row, col = matrix[0:1, :], turned[:, 0:1]
            kept = jnp.zeros((1, width), jnp.float32)
            for n in range(TERMS):
                if n > 0:
                    row, col = (
                        jnp.sum(matrix * col, axis=0, keepdims=True),
                        jnp.sum(turned * row, axis=1, keepdims=True),
                    )
                scaled = jnp.where(first, (1.0 - KAPPA) * col, col)
                vectors[mat, n] = jnp.broadcast_to(scaled, (depth, width))
                kept = jnp.where(lane == n + 1, col[0:1, 0:1], kept)
            scalars[mat] = jnp.broadcast_to(kept, (8, width))

    lane = lax.broadcasted_iota(jnp.int32, (1, width), 1)

    def one(j, carry):
        patch = patch_ref[pl.program_id(0) * block + j]
        mat = material_ref[patch]
        sums = [jnp.zeros((8, width), jnp.float32)] * TERMS
        for c in range(depth // 8):
            part = layer[j, pl.ds(8 * c, 8), :]
            sums = [
                s + vectors[mat, n, pl.ds(8 * c, 8), :] * part for n, s in enumerate(sums)
            ]
        rows = [jnp.sum(s, axis=0, keepdims=True) for s in sums]
        scalar_row = jnp.where(lane == 0, patch.astype(jnp.float32), scalars[mat][0:1, :])
        rows.append(scalar_row)
        rows.extend([jnp.zeros((1, width), jnp.float32)] * (LINES - len(rows)))
        out[j] = jnp.concatenate(rows, axis=0)
        return carry

    lax.fori_loop(0, block, one, 0, unroll=2)


def surface_rows(layer_maps, slot_patch, patch_material, layer_state):
    slots, depth, width = layer_state.shape
    mats = layer_maps.shape[0]
    block = 16
    return pl.pallas_call(
        functools.partial(surface_kernel, block),
        grid=(slots // block,),
        in_specs=[
            pl.BlockSpec((mats, depth, depth), lambda i: (0, 0, 0)),
            pl.BlockSpec(memory_space=SMEM),
            pl.BlockSpec(memory_space=SMEM),
            pl.BlockSpec((block, depth, width), lambda i: (i, 0, 0)),
        ],
        out_specs=pl.BlockSpec((block, LINES, width), lambda i: (i, 0, 0)),
        out_shape=jax.ShapeDtypeStruct((slots, LINES, width), jnp.float32),
        scratch_shapes=[
            pltpu.VMEM((mats, TERMS, depth, width), jnp.float32),
            pltpu.VMEM((mats, 8, width), jnp.float32),
        ],
        compiler_params=params(16),
        name="surface_rows",
    )(layer_maps, slot_patch, patch_material, layer_state)


def place(index, cells_x, parts):
    return index // (cells_x * parts), index // parts % cells_x, index % parts


def pick(rows_ref, fields, picked, tiles):
    cells_x = fields[0].shape[1]
    slots, width = picked.shape[1:]
    parts = fields[0].shape[2] // width

    def fetch(k, carry):
        z, x, part = place(jnp.maximum(rows_ref[k], 0), cells_x, parts)
        lines = pl.ds(pl.multiple_of(x // 8 * 8, 8), 8)
        lanes = pl.ds(pl.multiple_of(part * width, width), width)
        for side, field in enumerate(fields):
            tiles[side, pl.ds(pl.multiple_of(8 * k, 8), 8), :] = field[z, lines, lanes]
        return carry

    lax.fori_loop(0, slots, fetch, 0, unroll=8)

    def choose(k, carry):
        index = rows_ref[k]
        line = 8 * k + place(jnp.maximum(index, 0), cells_x, parts)[1] % 8
        for side in range(len(fields)):
            row = tiles[side, pl.ds(line, 1), :]
            picked[side, pl.ds(k, 1), :] = jnp.where(index >= 0, row, 0.0)
        return carry

    lax.fori_loop(0, slots, choose, 0, unroll=8)


def keep_sides(cells, side, z, x_low, x_high):
    last_x, width = cells.shape[0] - 1, x_low.shape[3]
    for part in range(x_low.shape[1]):
        lanes = slice(part * width, (part + 1) * width)
        x_low[side, part, pl.ds(z, 1), :] = cells[0:1, lanes]
        x_high[side, part, pl.ds(z, 1), :] = cells[last_x : last_x + 1, lanes]


def side_row(plane, side, z):
    parts = plane.shape[1]
    return jnp.concatenate([plane[side, part, pl.ds(z, 1), :] for part in range(parts)], axis=1)


def edges_kernel(rows_ref, field, adjoint, x_low, x_high, z_low, z_high, push, picked, tiles):
    last_z = field.shape[0] - 1

    def one(z, carry):
        for side, array in enumerate((field, adjoint)):
            keep_sides(array[z], side, z, x_low, x_high)
        return carry

    lax.fori_loop(0, field.shape[0], one, 0, unroll=4)
    for side, array in enumerate((field, adjoint)):
        z_low[side] = array[0]
        z_high[side] = array[last_z]
    pick(rows_ref, (field, adjoint), picked, tiles)
    push[...] = KAPPA * picked[...]


def edge_shapes(field, slots, width):
    cells_z, cells_x, along = field.shape
    f32 = jnp.float32
    return [
        jax.ShapeDtypeStruct((2, along // width, cells_z, width), f32),
        jax.ShapeDtypeStruct((2, along // width, cells_z, width), f32),
        jax.ShapeDtypeStruct((2, cells_x, along), f32),
        jax.ShapeDtypeStruct((2, cells_x, along), f32),
        jax.ShapeDtypeStruct((2, slots, width), f32),
    ]


def first_edges(rows, field, adjoint, slots, width):
    return pl.pallas_call(
        edges_kernel,
        in_specs=[pl.BlockSpec(memory_space=SMEM)] + [pl.BlockSpec(memory_space=VMEM)] * 2,
        out_specs=[pl.BlockSpec(memory_space=VMEM)] * 5,
        out_shape=edge_shapes(field, slots, width),
        scratch_shapes=[
            pltpu.VMEM((2, slots, width), jnp.float32),
            pltpu.VMEM((2, 8 * slots, width), jnp.float32),
        ],
        compiler_params=params(16),
        name="edges",
    )(rows, field, adjoint)


def column(meta, n):
    return meta[:, n : n + 1]


def step_kernel(step, *refs):
    last = step == STEPS - 1
    rows_ref, field, field_prev, adjoint, adjoint_prev, speed2 = refs[:6]
    x_before, x_after, z_before, z_after, lines = refs[6:11]
    pushes = refs[11 : 12 + step]
    refs = refs[12 + step :]
    field_out, adjoint_out = refs[:2]
    refs = refs[2:]
    if not last:
        x_low, x_high, z_low, z_high, push_out = refs[:5]
        refs = refs[5:]
        if step == STEPS - 2:
            gradient_out = refs[0]
            refs = refs[1:]
    coupling, change, picked, tiles = refs

    cells_z, cells_x, along = field.shape
    slots, width = change.shape[1:]
    parts = along // width
    meta = lines[pl.ds(META, slots, stride=LINES), :]

    def line(n):
        return lines[pl.ds(n - 1, slots, stride=LINES), :]

    scalars = [None] + [column(meta, n) for n in range(1, TERMS + 1)]
    surface = []
    pick(rows_ref, (field, adjoint), picked, tiles)
    for side in range(2):
        new = line(step + 1) if side == 0 else None
        for t in range(step + 1):
            term = scalars[step + 1 - t] * pushes[t][side]
            new = term if new is None else new + term
        surface.append(new)
        change[side] = BETA * (new - picked[side])

    coupling[...] = jnp.zeros_like(coupling)

    def put(k, carry):
        index = rows_ref[k]
        z, x, part = place(jnp.maximum(index, 0), cells_x, parts)
        z = jnp.where(index >= 0, z, cells_z)
        for side in range(2):
            coupling[side * parts + part, z, pl.ds(x, 1), :] = change[side, pl.ds(k, 1), :]
        return carry

    lax.fori_loop(0, slots, put, 0, unroll=8)

    gx, gz = lax.axis_index("gx"), lax.axis_index("gz")
    at_x_low, at_x_high = gx == 0, gx == lax.axis_size("gx") - 1
    at_z_low, at_z_high = gz == 0, gz == lax.axis_size("gz") - 1
    row_id = lax.broadcasted_iota(jnp.int32, (cells_x, along), 0)
    lane_id = lax.broadcasted_iota(jnp.int32, (cells_x, along), 1)

    def plane(z, below, above):
        speed = speed2[z]
        for side, (now, before, out) in enumerate(
            ((field, field_prev, field_out), (adjoint, adjoint_prev, adjoint_out))
        ):
            cells = now[z]
            low = jnp.where(at_x_low, 0.0, side_row(x_before, side, z))
            high = jnp.where(at_x_high, 0.0, side_row(x_after, side, z))
            beside = below(side, now) + above(side, now)
            beside = beside + jnp.where(row_id == 0, low, pltpu.roll(cells, 1, axis=0))
            beside = beside + jnp.where(
                row_id == cells_x - 1, high, pltpu.roll(cells, cells_x - 1, axis=0)
            )
            beside = beside + jnp.where(lane_id == 0, 0.0, pltpu.roll(cells, 1, axis=1))
            beside = beside + jnp.where(
                lane_id == along - 1, 0.0, pltpu.roll(cells, along - 1, axis=1)
            )
            extra = jnp.concatenate(
                [coupling[side * parts + part, z] for part in range(parts)], axis=1
            )
            new = 2.0 * cells - before[z] + speed * (beside - 6.0 * cells) + extra
            out[z] = new
            if not last:
                keep_sides(new, side, z, x_low, x_high)

    def inner(z, carry):
        plane(z, lambda side, now: now[z - 1], lambda side, now: now[z + 1])
        return carry

    plane(
        0,
        lambda side, now: jnp.where(at_z_low, 0.0, z_before[side]),
        lambda side, now: now[1],
    )
    lax.fori_loop(1, cells_z - 1, inner, 0, unroll=2)
    plane(
        cells_z - 1,
        lambda side, now: now[cells_z - 2],
        lambda side, now: jnp.where(at_z_high, 0.0, z_after[side]),
    )
    if last:
        return

    for side, out in enumerate((field_out, adjoint_out)):
        z_low[side] = out[0]
        z_high[side] = out[cells_z - 1]
    pick(rows_ref, (field_out, adjoint_out), picked, tiles)
    for side in range(2):
        push_out[side] = KAPPA * (picked[side] - surface[side])

    if step == STEPS - 2:
        forward = [pushes[t][0] for t in range(step + 1)] + [push_out[0]]
        backward = [pushes[t][1] for t in range(step + 1)] + [push_out[1]]
        total = jnp.zeros((slots, width), jnp.float32)
        for late in range(STEPS):
            inside = (STEPS - late) * line(TERMS - late)
            for t in range(STEPS - late):
                inside = inside + ((STEPS - late - t) * scalars[TERMS - late - t]) * forward[t]
            total = total + backward[late] * inside
        patches = gradient_out.shape[0]
        ids = column(meta, 0).astype(jnp.int32)
        owners = lax.broadcasted_iota(jnp.int32, (slots, patches), 1) == ids
        gradient_out[...] = lax.dot_general(
            owners.astype(jnp.float32),
            total,
            (((0,), (0,)), ((), ())),
            precision=lax.Precision.HIGHEST,
            preferred_element_type=jnp.float32,
        )


def step_call(step, rows, field, field_prev, adjoint, adjoint_prev, speed2, halos, lines, pushes, patches):
    slots, width = pushes[0].shape[1:]
    last = step == STEPS - 1
    cells_z, cells_x, along = field.shape
    parts = along // width
    shapes = [jax.ShapeDtypeStruct(field.shape, jnp.float32)] * 2
    if not last:
        shapes = shapes + edge_shapes(field, slots, width)
    if step == STEPS - 2:
        shapes = shapes + [jax.ShapeDtypeStruct((patches, width), jnp.float32)]
    operands = [field, field_prev, adjoint, adjoint_prev, speed2, *halos, lines, *pushes]
    return pl.pallas_call(
        functools.partial(step_kernel, step),
        in_specs=[pl.BlockSpec(memory_space=SMEM)]
        + [pl.BlockSpec(memory_space=VMEM)] * len(operands),
        out_specs=[pl.BlockSpec(memory_space=VMEM)] * len(shapes),
        out_shape=shapes,
        scratch_shapes=[
            pltpu.VMEM((2 * parts, cells_z + 1, cells_x, width), jnp.float32),
            pltpu.VMEM((2, slots, width), jnp.float32),
            pltpu.VMEM((2, slots, width), jnp.float32),
            pltpu.VMEM((2, 8 * slots, width), jnp.float32),
        ],
        compiler_params=params(24),
        name=f"step{step}",
    )(rows, *operands)


def ring(axis, shift):
    count = lax.axis_size(axis)
    return [(i, (i + shift) % count) for i in range(count)]


def exchange(edges):
    x_low, x_high, z_low, z_high = edges
    x_before = lax.ppermute(x_high, "gx", ring("gx", 1))
    x_after = lax.ppermute(x_low, "gx", ring("gx", -1))
    z_before = lax.ppermute(z_high, "gz", ring("gz", 1))
    z_after = lax.ppermute(z_low, "gz", ring("gz", -1))
    return x_before, x_after, z_before, z_after


def body(
    pressure_now,
    pressure_prev,
    adjoint_now,
    adjoint_prev,
    speed2,
    layer_state,
    layer_maps,
    send_rows,
    slot_patch,
    patch_material,
):
    slots, _, width = layer_state.shape
    patches = patch_material.shape[0]
    devices = lax.axis_size(("gx", "gz"))
    rows = send_rows.reshape(-1)

    *edges, push = first_edges(rows, pressure_now, adjoint_now, slots, width)
    halos = exchange(edges)
    lines = surface_rows(layer_maps, slot_patch, patch_material, layer_state)
    lines = lax.all_to_all(lines, ("gx", "gz"), split_axis=0, concat_axis=0, tiled=True)
    lines = lines.reshape(slots * LINES, width)

    fields = (pressure_now, pressure_prev, adjoint_now, adjoint_prev)
    pushes = [push]
    for step in range(STEPS):
        results = step_call(step, rows, *fields, speed2, halos, lines, pushes, patches)
        fields = (results[0], fields[0], results[1], fields[2])
        if step < STEPS - 1:
            halos = exchange(results[2:6])
            pushes.append(results[6])
        if step == STEPS - 2:
            parts = results[7].reshape(devices, patches // devices, width)
            parts = lax.all_to_all(parts, ("gx", "gz"), split_axis=0, concat_axis=0, tiled=True)
            gradient = jnp.sum(parts, axis=0)
    return fields[0], fields[2], gradient


def solution(mesh):
    grid = P("gz", "gx", None)
    split = P(("gx", "gz"), None, None)
    in_specs = (grid, grid, grid, grid, grid, split, P(), split, P(("gx", "gz")), P())
    out_specs = (grid, grid, P(("gx", "gz"), None))
    return jax.shard_map(body, mesh=mesh, in_specs=in_specs, out_specs=out_specs, check_vma=False)
```

time: 699 us -> 135 us (0.19); the launches traced: 688 us -> 135 us
  starting transfers between devices: 261 us -> 47.6 us
  waiting for transfers between devices: 125 us -> 15.4 us
  matrix products: 105 us -> 0 us
  other arithmetic: 105 us -> 1.77 us
  local copies, waits for them, and re-layouts: 77.5 us -> 14.2 us
  Pallas kernels: 0 us -> 55 us
  between operations: 15.2 us -> 0.8 us
    all_to_all x16 -> x2, starting transfers between devices: 168 us -> 20.2 us  [the longest x1 11.5 us: body(): lax.all_to_all(lines, ('gx', 'gz'), split_axis=0, concat_axis=0, tiled=True)]
    unnamed x2 -> x0, waiting for transfers between devices: 119 us -> none
    dot_general x12 -> x0, matrix products: 105 us -> none  [the longest x8 98.2 us: layer_update(): jnp.einsum('bsij,bsjw->bsiw', maps, layer, precision=lax.Precision.HIGHEST)]
    ppermute x32 -> x16, starting transfers between devices: 93 us -> 27.3 us  [the longest x4 16.6 us: exchange(): x_after = lax.ppermute(x_low, 'gx', ring('gx', -1))]
    pallas_call x0 -> x6, Pallas kernels: none -> 55 us  [the longest x4 44.4 us: step_call(): pl.pallas_call(functools.partial(step_kernel, step), in_specs=[pl.BlockSp...]
    add x12 -> x0, other arithmetic: 42.6 us -> none  [the longest x6 24.9 us: step_pair(): advance(fields, previous, speed2, padded)]
    slice x17 -> x0, local copies, waits for them, and re-layouts: 22 us -> none  [the longest x8 13.3 us: with_halo(): lax.slice_in_dim(block, 0, width, axis=dim)]
    scatter-add x8 -> x0, other arithmetic: 17.3 us -> none  [couple(): jnp.zeros((batch, total, width), jnp.float32).at[:, target]]
  transfers between devices with their start and end apart: 49 -> 18, of which waited for: 6 -> 9; matrix products, arithmetic and copies ran while one was open for 39% -> 0% of each run, Pallas kernels for 0% -> 10%
where the time goes in v1:
time: 135 us
  Pallas kernels  55 us (41%)
  starting transfers between devices  47.6 us (35%)
  waiting for transfers between devices  15.4 us (11%)
  local copies, waits for them, and re-layouts  14.2 us (11%)
  other arithmetic  1.77 us (1%)
    pallas_call x4, Pallas kernels, step_call(): pl.pallas_call(functools.partial(step_kernel, step), in_specs=[pl.BlockSp...  44.4 us
    ppermute x4, starting transfers between devices, exchange(): x_after = lax.ppermute(x_low, 'gx', ring('gx', -1))  16.6 us
    unnamed x36, local copies, waits for them, and re-layouts  14.2 us
    all_to_all x1, starting transfers between devices, body(): lax.all_to_all(lines, ('gx', 'gz'), split_axis=0, concat_axis=0, tiled=True)  11.5 us
    ppermute x4, waiting for transfers between devices, exchange(): z_after = lax.ppermute(z_low, 'gz', ring('gz', -1))  9.48 us
    all_to_all x1, starting transfers between devices, body(): lax.all_to_all(parts, ('gx', 'gz'), split_axis=0, concat_axis=0, tiled=True)  8.75 us
    pallas_call x1, Pallas kernels, surface_rows(): pl.pallas_call(functools.partial(surface_kernel, block), grid=(slots // b...  6.66 us
    ppermute x4, starting transfers between devices, exchange(): z_before = lax.ppermute(z_high, 'gz', ring('gz', 1))  5.59 us
  transfers between devices with their start and end apart: 18, of which 9 were waited for; matrix products, arithmetic and copies ran while one was open for 0% of the time, Pallas kernels for 10%

profile of v1, /device:TPU:1, one launch (start us, length us, event | category | flops | bytes accessed | tf_op | source)
XLA Modules:
  0.0 134.7 jit_solution(4746001935611654711)
XLA Ops:
  0.7 2.3 %copy-done.5 = f32[128,64,128]{2,1,0:T(8,128)S(1)} copy-done((f32[128,64,128]{2,1,0:T(8,128)S(1)}, f32[128,64,128]{2,1,0:T(8,128)}, u32[]{:S(2)}) %copy-start.5) | copy-done | bytes 4194328
  5.3 6.7 %surface_rows.1 = f32[128,8,128]{2,1,0:T(8,128)} custom-call(f32[8,64,64]{2,1,0:T(8,128)S(1)} %copy-done.14, s32[128]{0:T(128)S(1)} %copy-done.17, s32[1024]{0:T(1024)S(1)} %copy-done.16, f32[128,64,128]{2,1,0:T(8,128)S(1)} %copy-done.5), custom_call_target="tpu_custom_call" | custom-call | tf_op jit(solution)/shard_map/surface_rows/pallas_call | solution.py:75
  11.9 11.5 %all-to-all-start = ((f32[128,8,128]{2,1,0:T(8,128)}), f32[128,8,128]{2,1,0:T(8,128)S(1)}, u32[]{:S(2)}, u32[]{:S(2)}) async-start(f32[128,8,128]{2,1,0:T(8,128)} %surface_rows.1), calls=%async_computation | async-start | bytes 1048576 | tf_op jit(solution)/shard_map/all_to_all | solution.py:371
  24.7 4.0 %edges.1 = (f32[2,4,32,128]{3,2,1,0:T(8,128)S(1)}, f32[2,4,32,128]{3,2,1,0:T(8,128)S(1)}, f32[2,16,512]{2,1,0:T(8,128)S(1)}, f32[2,16,512]{2,1,0:T(8,128)S(1)}, f32[2,128,128]{2,1,0:T(8,128)S(1)}) custom-call(s32[128]{0:T(128)S(1)} %bitcast.7, f32[32,16,512]{2,1,0:T(8,128)S(1)} %copy-done.1, f32[32,16,512]{2,1,0:T(8,128)S(1)} %copy-done.2), custom_call_target="tpu_custom_call" | custom-call | tf_op jit(solution)/shard_map/edges/pallas_call | solution.py:167
  28.7 1.5 %collective-permute-start = (f32[2,4,32,128]{3,2,1,0:T(8,128)S(1)}, f32[2,4,32,128]{3,2,1,0:T(8,128)S(1)}, u32[]{:S(2)}, u32[]{:S(2)}) collective-permute-start(f32[2,4,32,128]{3,2,1,0:T(8,128)S(1)} %get-tuple-element.32), channel_id=1, source_target_pairs={{0,8},{8,16},{16,24},{24,32},{32,40},{40,48},{48,56},{56,64},{64,7... | collective-permute-start | bytes 393224 | tf_op jit(solution)/shard_map/ppermute | solution.py:344
  30.1 3.5 %collective-permute-start.1 = (f32[2,4,32,128]{3,2,1,0:T(8,128)S(1)}, f32[2,4,32,128]{3,2,1,0:T(8,128)S(1)}, u32[]{:S(2)}, u32[]{:S(2)}) collective-permute-start(f32[2,4,32,128]{3,2,1,0:T(8,128)S(1)} %get-tuple-element.33), channel_id=1, source_target_pairs={{0,120},{8,0},{16,8},{24,16},{32,24},{40,32},{48,40},{56,48},{64,5... | collective-permute-start | bytes 393224 | tf_op jit(solution)/shard_map/ppermute | solution.py:345
  33.6 2.2 %collective-permute-start.2 = (f32[2,16,512]{2,1,0:T(8,128)S(1)}, f32[2,16,512]{2,1,0:T(8,128)S(1)}, u32[]{:S(2)}, u32[]{:S(2)}) collective-permute-start(f32[2,16,512]{2,1,0:T(8,128)S(1)} %get-tuple-element.34), channel_id=1, source_target_pairs={{0,1},{1,2},{2,3},{3,4},{4,5},{5,6},{6,7},{7,0},{8,9},{9,10},{10,1... | collective-permute-start | bytes 196616 | tf_op jit(solution)/shard_map/ppermute | solution.py:346
  37.2 2.5 %collective-permute-done.3.refs_9_ = f32[2,16,512]{2,1,0:T(8,128)S(1)} collective-permute-done((f32[2,16,512]{2,1,0:T(8,128)S(1)}, f32[2,16,512]{2,1,0:T(8,128)S(1)}, u32[]{:S(2)}, u32[]{:S(2)}) %collective-permute-start.3) | collective-permute-done | bytes 65568 | tf_op jit(solution)/shard_map/ppermute | solution.py:347
  43.4 11.2 %step0.1 = (f32[32,16,512]{2,1,0:T(8,128)S(1)}, f32[32,16,512]{2,1,0:T(8,128)S(1)}, f32[2,4,32,128]{3,2,1,0:T(8,128)S(1)}, f32[2,4,32,128]{3,2,1,0:T(8,128)S(1)}...) custom-call(s32[128]{0:T(128)S(1)} %bitcast.8, f32[32,16,512]{2,1,0:T(8,128)S(1)} %copy-done.1, ...), custom_call_target="tpu_custom_call" | custom-call | tf_op jit(solution)/shard_map/step0/pallas_call | solution.py:320
  54.6 4.8 %collective-permute-start.5 = (f32[2,4,32,128]{3,2,1,0:T(8,128)S(1)}, f32[2,4,32,128]{3,2,1,0:T(8,128)S(1)}, u32[]{:S(2)}, u32[]{:S(2)}) collective-permute-start(f32[2,4,32,128]{3,2,1,0:T(8,128)S(1)} %get-tuple-element.40), channel_id=1, source_target_pairs={{0,120},{8,0},{16,8},{24,16},{32,24},{40,32},{48,40},{56,48},{64,5... | collective-permute-start | bytes 393224 | tf_op jit(solution)/shard_map/ppermute | solution.py:345
  61.2 2.4 %collective-permute-done.7.refs_9_ = f32[2,16,512]{2,1,0:T(8,128)S(1)} collective-permute-done((f32[2,16,512]{2,1,0:T(8,128)S(1)}, f32[2,16,512]{2,1,0:T(8,128)S(1)}, u32[]{:S(2)}, u32[]{:S(2)}) %collective-permute-start.7) | collective-permute-done | bytes 65568 | tf_op jit(solution)/shard_map/ppermute | solution.py:347
  63.6 11.2 %step1.1 = (f32[32,16,512]{2,1,0:T(8,128)S(1)}, f32[32,16,512]{2,1,0:T(8,128)S(1)}, f32[2,4,32,128]{3,2,1,0:T(8,128)S(1)}, f32[2,4,32,128]{3,2,1,0:T(8,128)S(1)}...) custom-call(s32[128]{0:T(128)S(1)} %bitcast.9, ...), custom_call_target="tpu_custom_call" | custom-call | tf_op jit(solution)/shard_map/step1/pallas_call | solution.py:320
  74.9 4.8 %collective-permute-start.9 = (f32[2,4,32,128]{3,2,1,0:T(8,128)S(1)}, f32[2,4,32,128]{3,2,1,0:T(8,128)S(1)}, u32[]{:S(2)}, u32[]{:S(2)}) collective-permute-start(f32[2,4,32,128]{3,2,1,0:T(8,128)S(1)} %get-tuple-element.47), channel_id=1, source_target_pairs={{0,120},{8,0},{16,8},{24,16},{32,24},{40,32},{48,40},{56,48},{64,5... | collective-permute-start | bytes 393224 | tf_op jit(solution)/shard_map/ppermute | solution.py:345
  80.4 1.6 %collective-permute-start.11 = (f32[2,16,512]{2,1,0:T(8,128)S(1)}, f32[2,16,512]{2,1,0:T(8,128)S(1)}, u32[]{:S(2)}, u32[]{:S(2)}) collective-permute-start(f32[2,16,512]{2,1,0:T(8,128)S(1)} %get-tuple-element.49), channel_id=1, source_target_pairs={{0,7},{1,0},{2,1},{3,2},{4,3},{5,4},{6,5},{7,6},{8,15},{9,8},{10,9... | collective-permute-start | bytes 196616 | tf_op jit(solution)/shard_map/ppermute | solution.py:347
  82.7 1.7 %collective-permute-done.11.refs_9_ = f32[2,16,512]{2,1,0:T(8,128)S(1)} collective-permute-done((f32[2,16,512]{2,1,0:T(8,128)S(1)}, f32[2,16,512]{2,1,0:T(8,128)S(1)}, u32[]{:S(2)}, u32[]{:S(2)}) %collective-permute-start.11) | collective-permute-done | bytes 65568 | tf_op jit(solution)/shard_map/ppermute | solution.py:347
  84.4 12.7 %step2.1 = (f32[32,16,512]{2,1,0:T(8,128)S(1)}, f32[32,16,512]{2,1,0:T(8,128)S(1)}, f32[2,4,32,128]{3,2,1,0:T(8,128)S(1)}, f32[2,4,32,128]{3,2,1,0:T(8,128)S(1)}...) custom-call(s32[128]{0:T(128)S(1)} %bitcast.10, ...), custom_call_target="tpu_custom_call" | custom-call | tf_op jit(solution)/shard_map/step2/pallas_call | solution.py:320
  98.1 8.8 %all-to-all-start.1 = ((f32[128,8,128]{2,1,0:T(8,128)}), f32[128,8,128]{2,1,0:T(8,128)}, u32[]{:S(2)}, u32[]{:S(2)}) async-start(f32[128,8,128]{2,1,0:T(8,128)} %bitcast.2), calls=%async_computation.1 | async-start | bytes 1048576 | tf_op jit(solution)/shard_map/all_to_all | solution.py:384
  108.3 3.5 %collective-permute-start.13 = (f32[2,4,32,128]{3,2,1,0:T(8,128)S(1)}, f32[2,4,32,128]{3,2,1,0:T(8,128)S(1)}, u32[]{:S(2)}, u32[]{:S(2)}) collective-permute-start(f32[2,4,32,128]{3,2,1,0:T(8,128)S(1)} %get-tuple-element.54), channel_id=1, source_target_pairs={{0,120},{8,0},{16,8},{24,16},{32,24},{40,32},{48,40},{56,48},{64,5... | collective-permute-start | bytes 393224 | tf_op jit(solution)/shard_map/ppermute | solution.py:345
  111.8 2.2 %collective-permute-start.14 = (f32[2,16,512]{2,1,0:T(8,128)S(1)}, f32[2,16,512]{2,1,0:T(8,128)S(1)}, u32[]{:S(2)}, u32[]{:S(2)}) collective-permute-start(f32[2,16,512]{2,1,0:T(8,128)S(1)} %get-tuple-element.55), channel_id=1, source_target_pairs={{0,1},{1,2},{2,3},{3,4},{4,5},{5,6},{6,7},{7,0},{8,9},{9,10},{10,1... | collective-permute-start | bytes 196616 | tf_op jit(solution)/shard_map/ppermute | solution.py:346
  114.0 1.5 %collective-permute-done.14.refs_8_ = f32[2,16,512]{2,1,0:T(8,128)S(1)} collective-permute-done((f32[2,16,512]{2,1,0:T(8,128)S(1)}, f32[2,16,512]{2,1,0:T(8,128)S(1)}, u32[]{:S(2)}, u32[]{:S(2)}) %collective-permute-start.14) | collective-permute-done | bytes 65568 | tf_op jit(solution)/shard_map/ppermute | solution.py:346
  115.5 3.0 %collective-permute-done.15.refs_9_ = f32[2,16,512]{2,1,0:T(8,128)S(1)} collective-permute-done((f32[2,16,512]{2,1,0:T(8,128)S(1)}, f32[2,16,512]{2,1,0:T(8,128)S(1)}, u32[]{:S(2)}, u32[]{:S(2)}) %collective-permute-start.15) | collective-permute-done | bytes 65568 | tf_op jit(solution)/shard_map/ppermute | solution.py:347
  118.5 1.5 %collective-permute-done.12.refs_6_ = f32[2,4,32,128]{3,2,1,0:T(8,128)S(1)} collective-permute-done((f32[2,4,32,128]{3,2,1,0:T(8,128)S(1)}, f32[2,4,32,128]{3,2,1,0:T(8,128)S(1)}, u32[]{:S(2)}, u32[]{:S(2)}) %collective-permute-start.12) | collective-permute-done | bytes 131104 | tf_op jit(solution)/shard_map/ppermute | solution.py:344
  123.7 9.3 %step3.1 = (f32[32,16,512]{2,1,0:T(8,128)}, f32[32,16,512]{2,1,0:T(8,128)}) custom-call(s32[128]{0:T(128)S(1)} %bitcast.11, f32[32,16,512]{2,1,0:T(8,128)S(1)} %get-tuple-element.51.refs_1_, f32[32,16,512]{2,1,0:T(8,128)S(1)} %copy-done.7, f32[32,16,512]{2,1,0:T(8,128)S(1)} %copy-done.13, f32[32,16,512]{2,1,0:T(8,128)S(1)} %copy-done.9, ...), custom_call_target="tpu_custom_call" | custom-call | tf_op jit(solution)/shard_map/step3/pallas_call | solution.py:320
  132.9 1.8 %reduce_sum.9 = f32[8,128]{1,0:T(8,128)} reduce(f32[128,8,128]{2,1,0:T(8,128)} %all-to-all-done.1, f32[]{:T(128)} %constant.0.clone.1), dimensions={0}, to_apply=%region_0.0 | reduce | flops 130048 | bytes 528388 | tf_op jit(solution)/shard_map/reduce_sum | solution.py:385
  (55 shorter events, 18.1 us)
Async XLA Ops:
  0.6 22.8 %copy-start.1 = (f32[32,16,512]{2,1,0:T(8,128)S(1)}, f32[32,16,512]{2,1,0:T(8,128)}, u32[]{:S(2)}) copy-start(f32[32,16,512]{2,1,0:T(8,128)} %refs_2_.3) | copy-start | bytes 3145732
  0.6 39.0 %copy-start = (f32[32,16,512]{2,1,0:T(8,128)S(1)}, f32[32,16,512]{2,1,0:T(8,128)}, u32[]{:S(2)}) copy-start(f32[32,16,512]{2,1,0:T(8,128)} %refs_5_.7) | copy-start | bytes 3145732
  5.3 18.2 %copy-start.15 = (s32[1,128,1]{1,2,0:T(1,128)S(1)}, s32[1,128,1]{1,2,0:T(1,128)}, u32[]{:S(2)}) copy-start(s32[1,128,1]{1,2,0:T(1,128)} %param.17) | copy-start | bytes 1540
  11.9 27.7 %all-to-all-start = ((f32[128,8,128]{2,1,0:T(8,128)}), f32[128,8,128]{2,1,0:T(8,128)S(1)}, u32[]{:S(2)}, u32[]{:S(2)}) async-start(f32[128,8,128]{2,1,0:T(8,128)} %surface_rows.1), calls=%async_computation | async-start | bytes 1048576 | tf_op jit(solution)/shard_map/all_to_all | solution.py:371
  28.7 11.0 %collective-permute-start = (f32[2,4,32,128]{3,2,1,0:T(8,128)S(1)}, f32[2,4,32,128]{3,2,1,0:T(8,128)S(1)}, u32[]{:S(2)}, u32[]{:S(2)}) collective-permute-start(f32[2,4,32,128]{3,2,1,0:T(8,128)S(1)} %get-tuple-element.32), channel_id=1, source_target_pairs={{0,8},{8,16},{16,24},{24,32},{32,40},{40,48},{48,56},{56,64},{64,7... | collective-permute-start | bytes 393224 | tf_op jit(solution)/shard_map/ppermute | solution.py:344
  30.1 9.5 %collective-permute-start.1 = (f32[2,4,32,128]{3,2,1,0:T(8,128)S(1)}, f32[2,4,32,128]{3,2,1,0:T(8,128)S(1)}, u32[]{:S(2)}, u32[]{:S(2)}) collective-permute-start(f32[2,4,32,128]{3,2,1,0:T(8,128)S(1)} %get-tuple-element.33), channel_id=1, source_target_pairs={{0,120},{8,0},{16,8},{24,16},{32,24},{40,32},{48,40},{56,48},{64,5... | collective-permute-start | bytes 393224 | tf_op jit(solution)/shard_map/ppermute | solution.py:345
  33.6 3.5 %collective-permute-start.2 = (f32[2,16,512]{2,1,0:T(8,128)S(1)}, f32[2,16,512]{2,1,0:T(8,128)S(1)}, u32[]{:S(2)}, u32[]{:S(2)}) collective-permute-start(f32[2,16,512]{2,1,0:T(8,128)S(1)} %get-tuple-element.34), channel_id=1, source_target_pairs={{0,1},{1,2},{2,3},{3,4},{4,5},{5,6},{6,7},{7,0},{8,9},{9,10},{10,1... | collective-permute-start | bytes 196616 | tf_op jit(solution)/shard_map/ppermute | solution.py:346
  35.8 3.8 %collective-permute-start.3 = (f32[2,16,512]{2,1,0:T(8,128)S(1)}, f32[2,16,512]{2,1,0:T(8,128)S(1)}, u32[]{:S(2)}, u32[]{:S(2)}) collective-permute-start(f32[2,16,512]{2,1,0:T(8,128)S(1)} %get-tuple-element.35), channel_id=1, source_target_pairs={{0,7},{1,0},{2,1},{3,2},{4,3},{5,4},{6,5},{7,6},{8,15},{9,8},{10,9... | collective-permute-start | bytes 196616 | tf_op jit(solution)/shard_map/ppermute | solution.py:347
  43.4 20.2 %copy-start.4 = (f32[32,16,512]{2,1,0:T(8,128)S(1)}, f32[32,16,512]{2,1,0:T(8,128)}, u32[]{:S(2)}) copy-start(f32[32,16,512]{2,1,0:T(8,128)} %refs_4_.3) | copy-start | bytes 3145732
  54.6 9.0 %collective-permute-start.4 = (f32[2,4,32,128]{3,2,1,0:T(8,128)S(1)}, f32[2,4,32,128]{3,2,1,0:T(8,128)S(1)}, u32[]{:S(2)}, u32[]{:S(2)}) collective-permute-start(f32[2,4,32,128]{3,2,1,0:T(8,128)S(1)} %get-tuple-element.39), channel_id=1, source_target_pairs={{0,8},{8,16},{16,24},{24,32},{32,40},{40,48},{48,56},{56,64},{64,7... | collective-permute-start | bytes 393224 | tf_op jit(solution)/shard_map/ppermute | solution.py:344
  54.6 8.9 %collective-permute-start.5 = (f32[2,4,32,128]{3,2,1,0:T(8,128)S(1)}, f32[2,4,32,128]{3,2,1,0:T(8,128)S(1)}, u32[]{:S(2)}, u32[]{:S(2)}) collective-permute-start(f32[2,4,32,128]{3,2,1,0:T(8,128)S(1)} %get-tuple-element.40), channel_id=1, source_target_pairs={{0,120},{8,0},{16,8},{24,16},{32,24},{40,32},{48,40},{56,48},{64,5... | collective-permute-start | bytes 393224 | tf_op jit(solution)/shard_map/ppermute | solution.py:345
  59.4 1.8 %collective-permute-start.6 = (f32[2,16,512]{2,1,0:T(8,128)S(1)}, f32[2,16,512]{2,1,0:T(8,128)S(1)}, u32[]{:S(2)}, u32[]{:S(2)}) collective-permute-start(f32[2,16,512]{2,1,0:T(8,128)S(1)} %get-tuple-element.41), channel_id=1, source_target_pairs={{0,1},{1,2},{2,3},{3,4},{4,5},{5,6},{6,7},{7,0},{8,9},{9,10},{10,1... | collective-permute-start | bytes 196616 | tf_op jit(solution)/shard_map/ppermute | solution.py:346
  59.9 3.7 %collective-permute-start.7 = (f32[2,16,512]{2,1,0:T(8,128)S(1)}, f32[2,16,512]{2,1,0:T(8,128)S(1)}, u32[]{:S(2)}, u32[]{:S(2)}) collective-permute-start(f32[2,16,512]{2,1,0:T(8,128)S(1)} %get-tuple-element.42), channel_id=1, source_target_pairs={{0,7},{1,0},{2,1},{3,2},{4,3},{5,4},{6,5},{7,6},{8,15},{9,8},{10,9... | collective-permute-start | bytes 196616 | tf_op jit(solution)/shard_map/ppermute | solution.py:347
  74.8 22.3 %copy-start.6 = (f32[32,16,512]{2,1,0:T(8,128)}, f32[32,16,512]{2,1,0:T(8,128)S(1)}, u32[]{:S(2)}) copy-start(f32[32,16,512]{2,1,0:T(8,128)S(1)} %get-tuple-element.44.refs_1_.refs_2_) | copy-start | bytes 3145732
  74.8 23.3 %copy-start.8 = (f32[32,16,512]{2,1,0:T(8,128)}, f32[32,16,512]{2,1,0:T(8,128)S(1)}, u32[]{:S(2)}) copy-start(f32[32,16,512]{2,1,0:T(8,128)S(1)} %get-tuple-element.45.refs_3_.refs_4_) | copy-start | bytes 3145732
  74.8 9.6 %collective-permute-start.8 = (f32[2,4,32,128]{3,2,1,0:T(8,128)S(1)}, f32[2,4,32,128]{3,2,1,0:T(8,128)S(1)}, u32[]{:S(2)}, u32[]{:S(2)}) collective-permute-start(f32[2,4,32,128]{3,2,1,0:T(8,128)S(1)} %get-tuple-element.46), channel_id=1, source_target_pairs={{0,8},{8,16},{16,24},{24,32},{32,40},{40,48},{48,56},{56,64},{64,7... | collective-permute-start | bytes 393224 | tf_op jit(solution)/shard_map/ppermute | solution.py:344
  74.9 9.5 %collective-permute-start.9 = (f32[2,4,32,128]{3,2,1,0:T(8,128)S(1)}, f32[2,4,32,128]{3,2,1,0:T(8,128)S(1)}, u32[]{:S(2)}, u32[]{:S(2)}) collective-permute-start(f32[2,4,32,128]{3,2,1,0:T(8,128)S(1)} %get-tuple-element.47), channel_id=1, source_target_pairs={{0,120},{8,0},{16,8},{24,16},{32,24},{40,32},{48,40},{56,48},{64,5... | collective-permute-start | bytes 393224 | tf_op jit(solution)/shard_map/ppermute | solution.py:345
  79.6 3.1 %collective-permute-start.10 = (f32[2,16,512]{2,1,0:T(8,128)S(1)}, f32[2,16,512]{2,1,0:T(8,128)S(1)}, u32[]{:S(2)}, u32[]{:S(2)}) collective-permute-start(f32[2,16,512]{2,1,0:T(8,128)S(1)} %get-tuple-element.48), channel_id=1, source_target_pairs={{0,1},{1,2},{2,3},{3,4},{4,5},{5,6},{6,7},{7,0},{8,9},{9,10},{10,1... | collective-permute-start | bytes 196616 | tf_op jit(solution)/shard_map/ppermute | solution.py:346
  80.4 4.0 %collective-permute-start.11 = (f32[2,16,512]{2,1,0:T(8,128)S(1)}, f32[2,16,512]{2,1,0:T(8,128)S(1)}, u32[]{:S(2)}, u32[]{:S(2)}) collective-permute-start(f32[2,16,512]{2,1,0:T(8,128)S(1)} %get-tuple-element.49), channel_id=1, source_target_pairs={{0,7},{1,0},{2,1},{3,2},{4,3},{5,4},{6,5},{7,6},{8,15},{9,8},{10,9... | collective-permute-start | bytes 196616 | tf_op jit(solution)/shard_map/ppermute | solution.py:347
  98.1 34.8 %all-to-all-start.1 = ((f32[128,8,128]{2,1,0:T(8,128)}), f32[128,8,128]{2,1,0:T(8,128)}, u32[]{:S(2)}, u32[]{:S(2)}) async-start(f32[128,8,128]{2,1,0:T(8,128)} %bitcast.2), calls=%async_computation.1 | async-start | bytes 1048576 | tf_op jit(solution)/shard_map/all_to_all | solution.py:384
  106.8 13.2 %collective-permute-start.12 = (f32[2,4,32,128]{3,2,1,0:T(8,128)S(1)}, f32[2,4,32,128]{3,2,1,0:T(8,128)S(1)}, u32[]{:S(2)}, u32[]{:S(2)}) collective-permute-start(f32[2,4,32,128]{3,2,1,0:T(8,128)S(1)} %get-tuple-element.53), channel_id=1, source_target_pairs={{0,8},{8,16},{16,24},{24,32},{32,40},{40,48},{48,56},{56,64},{64,7... | collective-permute-start | bytes 393224 | tf_op jit(solution)/shard_map/ppermute | solution.py:344
  108.3 11.7 %collective-permute-start.13 = (f32[2,4,32,128]{3,2,1,0:T(8,128)S(1)}, f32[2,4,32,128]{3,2,1,0:T(8,128)S(1)}, u32[]{:S(2)}, u32[]{:S(2)}) collective-permute-start(f32[2,4,32,128]{3,2,1,0:T(8,128)S(1)} %get-tuple-element.54), channel_id=1, source_target_pairs={{0,120},{8,0},{16,8},{24,16},{32,24},{40,32},{48,40},{56,48},{64,5... | collective-permute-start | bytes 393224 | tf_op jit(solution)/shard_map/ppermute | solution.py:345
  111.8 3.7 %collective-permute-start.14 = (f32[2,16,512]{2,1,0:T(8,128)S(1)}, f32[2,16,512]{2,1,0:T(8,128)S(1)}, u32[]{:S(2)}, u32[]{:S(2)}) collective-permute-start(f32[2,16,512]{2,1,0:T(8,128)S(1)} %get-tuple-element.55), channel_id=1, source_target_pairs={{0,1},{1,2},{2,3},{3,4},{4,5},{5,6},{6,7},{7,0},{8,9},{9,10},{10,1... | collective-permute-start | bytes 196616 | tf_op jit(solution)/shard_map/ppermute | solution.py:346
  114.0 4.5 %collective-permute-start.15 = (f32[2,16,512]{2,1,0:T(8,128)S(1)}, f32[2,16,512]{2,1,0:T(8,128)S(1)}, u32[]{:S(2)}, u32[]{:S(2)}) collective-permute-start(f32[2,16,512]{2,1,0:T(8,128)S(1)} %get-tuple-element.56), channel_id=1, source_target_pairs={{0,7},{1,0},{2,1},{3,2},{4,3},{5,4},{6,5},{7,6},{8,15},{9,8},{10,9... | collective-permute-start | bytes 196616 | tf_op jit(solution)/shard_map/ppermute | solution.py:347
  (12 other events, 14.2 us)

commit v2 on v1

v2 whole, which is shorter than its diff:
```python
import functools

import jax
import jax.numpy as jnp
from jax import lax
from jax.experimental import pallas as pl
from jax.experimental.pallas import tpu as pltpu
from jax.sharding import PartitionSpec as P

STEPS = 4
KAPPA = 0.5
BETA = 0.3
TERMS = STEPS + 1
LINES = 8
META = TERMS
MIB = 1 << 20
VMEM = pltpu.VMEM
SMEM = pltpu.SMEM
HBM = pltpu.HBM
UNROLL = 10


def in_hbm(*arrays):
    return [pltpu.with_memory_space_constraint(array, HBM) for array in arrays]


def params(mib):
    return pltpu.CompilerParams(vmem_limit_bytes=mib * MIB)


def surface_kernel(maps_hbm, patch_hbm, material_hbm, layer_hbm, out, maps, patch_ref, material_ref, layer, vectors, scalars, sems):
    mats, _, depth = maps.shape
    slots, _, width = layer.shape
    chunks = sems.shape[0] - 3
    block = slots // chunks
    small = [
        pltpu.make_async_copy(maps_hbm, maps, sems.at[chunks]),
        pltpu.make_async_copy(patch_hbm, patch_ref, sems.at[chunks + 1]),
        pltpu.make_async_copy(material_hbm, material_ref, sems.at[chunks + 2]),
    ]
    large = [
        pltpu.make_async_copy(
            layer_hbm.at[pl.ds(i * block, block)], layer.at[pl.ds(i * block, block)], sems.at[i]
        )
        for i in range(chunks)
    ]
    for copy in small + large:
        copy.start()

    lane = lax.broadcasted_iota(jnp.int32, (1, width), 1)
    first = lax.broadcasted_iota(jnp.int32, (depth, 1), 0) == 0
    small[0].wait()
    matrices = [maps[mat] for mat in range(mats)]
    turned = [matrix.T for matrix in matrices]
    rows = [matrix[0:1, :] for matrix in matrices]
    cols = [matrix[:, 0:1] for matrix in turned]
    kept = [jnp.zeros((1, width), jnp.float32)] * mats
    for n in range(TERMS):
        for mat in range(mats):
            if n > 0:
                rows[mat], cols[mat] = (
                    jnp.sum(matrices[mat] * cols[mat], axis=0, keepdims=True),
                    jnp.sum(turned[mat] * rows[mat], axis=1, keepdims=True),
                )
            scaled = jnp.where(first, (1.0 - KAPPA) * cols[mat], cols[mat])
            vectors[mat, n] = jnp.broadcast_to(scaled, (depth, width))
            kept[mat] = jnp.where(lane == n + 1, cols[mat][0:1, 0:1], kept[mat])
    for mat in range(mats):
        scalars[mat] = jnp.broadcast_to(kept[mat], (8, width))
    small[1].wait()
    small[2].wait()

    def one(j, carry):
        patch = patch_ref[j]
        mat = material_ref[patch]
        sums = [jnp.zeros((8, width), jnp.float32)] * TERMS
        for c in range(depth // 8):
            part = layer[j, pl.ds(8 * c, 8), :]
            sums = [
                s + vectors[mat, n, pl.ds(8 * c, 8), :] * part for n, s in enumerate(sums)
            ]
        rows = [jnp.sum(s, axis=0, keepdims=True) for s in sums]
        scalar_row = jnp.where(lane == 0, patch.astype(jnp.float32), scalars[mat][0:1, :])
        rows.append(scalar_row)
        rows.extend([jnp.zeros((1, width), jnp.float32)] * (LINES - len(rows)))
        out[j] = jnp.concatenate(rows, axis=0)
        return carry

    for i in range(chunks):
        large[i].wait()
        lax.fori_loop(i * block, (i + 1) * block, one, 0, unroll=4)


def surface_rows(layer_maps, slot_patch, patch_material, layer_state):
    slots, depth, width = layer_state.shape
    mats = layer_maps.shape[0]
    chunks = 4
    return pl.pallas_call(
        surface_kernel,
        in_specs=[pl.BlockSpec(memory_space=HBM)] * 4,
        out_specs=pl.BlockSpec(memory_space=VMEM),
        out_shape=jax.ShapeDtypeStruct((slots, LINES, width), jnp.float32),
        scratch_shapes=[
            pltpu.VMEM((mats, depth, depth), jnp.float32),
            pltpu.SMEM(slot_patch.shape, jnp.int32),
            pltpu.SMEM(patch_material.shape, jnp.int32),
            pltpu.VMEM((slots, depth, width), jnp.float32),
            pltpu.VMEM((mats, TERMS, depth, width), jnp.float32),
            pltpu.VMEM((mats, 8, width), jnp.float32),
            pltpu.SemaphoreType.DMA((chunks + 3,)),
        ],
        compiler_params=params(24),
        name="surface_rows",
    )(*in_hbm(layer_maps, slot_patch, patch_material, layer_state))


def place(index, cells_x, parts):
    low, middle = parts.bit_length() - 1, cells_x.bit_length() - 1
    return (
        jnp.right_shift(index, low + middle),
        jnp.bitwise_and(jnp.right_shift(index, low), cells_x - 1),
        jnp.bitwise_and(index, parts - 1),
    )


def pick(rows_ref, fields, picked, tiles):
    cells_x = fields[0].shape[1]
    slots, width = picked.shape[1:]
    parts = fields[0].shape[2] // width

    def fetch(k, carry):
        z, x, part = place(jnp.maximum(rows_ref[k], 0), cells_x, parts)
        lines = pl.ds(pl.multiple_of(jnp.bitwise_and(x, -8), 8), 8)
        lanes = pl.ds(pl.multiple_of(part * width, width), width)
        for side, field in enumerate(fields):
            tiles[side, pl.ds(pl.multiple_of(8 * k, 8), 8), :] = field[z, lines, lanes]
        return carry

    lax.fori_loop(0, slots, fetch, 0, unroll=8)

    def choose(k, carry):
        index = rows_ref[k]
        line = 8 * k + jnp.bitwise_and(place(jnp.maximum(index, 0), cells_x, parts)[1], 7)
        for side in range(len(fields)):
            row = tiles[side, pl.ds(line, 1), :]
            picked[side, pl.ds(k, 1), :] = jnp.where(index >= 0, row, 0.0)
        return carry

    lax.fori_loop(0, slots, choose, 0, unroll=8)


def even(axis):
    return lax.axis_index(axis) % 2 == 0


def at_start(axis):
    return lax.axis_index(axis) == 0


def at_end(axis):
    return lax.axis_index(axis) == lax.axis_size(axis) - 1


def outgoing(axis, low, high):
    choice = even(axis)
    return jnp.where(choice, low, high), jnp.where(choice, high, low)


def incoming(axis, outer, inner):
    choice = even(axis)
    before = jnp.where(at_start(axis), 0.0, jnp.where(choice, outer, inner))
    after = jnp.where(at_end(axis), 0.0, jnp.where(choice, inner, outer))
    return before, after


def keep_sides(cells, side, z, x_outer, x_inner):
    last_x, width = cells.shape[0] - 1, x_outer.shape[3]
    for part in range(x_outer.shape[1]):
        lanes = slice(part * width, (part + 1) * width)
        x_outer[side, part, pl.ds(z, 1), :], x_inner[side, part, pl.ds(z, 1), :] = outgoing(
            "gx", cells[0:1, lanes], cells[last_x : last_x + 1, lanes]
        )


def side_row(plane, side, z):
    parts = plane.shape[1]
    return jnp.concatenate([plane[side, part, pl.ds(z, 1), :] for part in range(parts)], axis=1)


def edges_kernel(rows_hbm, field_hbm, adjoint_hbm, x_outer, x_inner, z_outer, z_inner, push, picked, rows_ref, field, adjoint, tiles, sems):
    fields = (field, adjoint)
    copies = [
        pltpu.make_async_copy(rows_hbm, rows_ref, sems.at[2]),
        pltpu.make_async_copy(field_hbm, field, sems.at[0]),
        pltpu.make_async_copy(adjoint_hbm, adjoint, sems.at[1]),
    ]
    for copy in copies:
        copy.start()
    for side, array in enumerate(fields):
        copies[side + 1].wait()

        def one(z, carry):
            keep_sides(array[z], side, z, x_outer, x_inner)
            return carry

        lax.fori_loop(0, array.shape[0], one, 0, unroll=8)
        z_outer[side], z_inner[side] = outgoing("gz", array[0], array[array.shape[0] - 1])
    copies[0].wait()
    pick(rows_ref, fields, picked, tiles)
    push[...] = KAPPA * picked[...]


def edge_shapes(field, slots, width):
    cells_z, cells_x, along = field.shape
    f32 = jnp.float32
    return [
        jax.ShapeDtypeStruct((2, along // width, cells_z, width), f32),
        jax.ShapeDtypeStruct((2, along // width, cells_z, width), f32),
        jax.ShapeDtypeStruct((2, cells_x, along), f32),
        jax.ShapeDtypeStruct((2, cells_x, along), f32),
        jax.ShapeDtypeStruct((2, slots, width), f32),
        jax.ShapeDtypeStruct((2, slots, width), f32),
    ]


def first_edges(rows, field, adjoint, slots, width):
    return pl.pallas_call(
        edges_kernel,
        in_specs=[pl.BlockSpec(memory_space=HBM)] * 3,
        out_specs=[pl.BlockSpec(memory_space=VMEM)] * 6,
        out_shape=edge_shapes(field, slots, width),
        scratch_shapes=[
            pltpu.SMEM((slots,), jnp.int32),
            pltpu.VMEM(field.shape, jnp.float32),
            pltpu.VMEM(field.shape, jnp.float32),
            pltpu.VMEM((2, 8 * slots, width), jnp.float32),
            pltpu.SemaphoreType.DMA((3,)),
        ],
        compiler_params=params(8),
        name="edges",
    )(*in_hbm(rows, field, adjoint))


def column(meta, n):
    return meta[:, n : n + 1]


def couple(rows_ref, change, coupling):
    parts, cells_z, cells_x = coupling.shape[0] // 2, coupling.shape[1] - 1, coupling.shape[2]

    def put(k, carry):
        index = rows_ref[k]
        z, x, part = place(jnp.maximum(index, 0), cells_x, parts)
        z = jnp.where(index >= 0, z, cells_z)
        for side in range(2):
            coupling[side * parts + part, z, pl.ds(x, 1), :] = change[side, pl.ds(k, 1), :]
        return carry

    lax.fori_loop(0, change.shape[1], put, 0, unroll=8)


def inner_planes(cells_z, plane):
    def inner(z, carry):
        plane(z, lambda side, now: now[z - 1], lambda side, now: now[z + 1])
        return carry

    lax.fori_loop(1, cells_z - 1, inner, 0, unroll=UNROLL)


def stencil(cells, before, speed, beside, low, high, extra):
    cells_x, along = cells.shape
    row_id = lax.broadcasted_iota(jnp.int32, cells.shape, 0)
    lane_id = lax.broadcasted_iota(jnp.int32, cells.shape, 1)
    low = 0.0 if low is None else low
    high = 0.0 if high is None else high
    beside = beside + jnp.where(row_id == 0, low, pltpu.roll(cells, 1, axis=0))
    beside = beside + jnp.where(row_id == cells_x - 1, high, pltpu.roll(cells, cells_x - 1, axis=0))
    beside = beside + jnp.where(lane_id == 0, 0.0, pltpu.roll(cells, 1, axis=1))
    beside = beside + jnp.where(lane_id == along - 1, 0.0, pltpu.roll(cells, along - 1, axis=1))
    return 2.0 * cells - before + speed * (beside - 6.0 * cells) + extra


def step_kernel(step, *refs):
    ahead = step == STEPS - 2
    loads = []
    rows_ref, field, field_prev, adjoint, adjoint_prev, speed2 = refs[:6]
    x_from_outer, x_from_inner, z_from_outer, z_from_inner, lines, picked = refs[6:12]
    pushes = refs[12 : 13 + step]
    refs = refs[13 + step :]
    if ahead:
        x_outer, x_inner, z_outer, z_inner, speed_low, speed_high, gradient_out = refs[:7]
        partial_hbm = refs[7:9]
        coupling, change, tiles, field_out, adjoint_out, push_out, picked_out = refs[9:16]
        partial, sems = refs[16:18], refs[18]
    else:
        field_out, adjoint_out, x_outer, x_inner, z_outer, z_inner, push_out, picked_out = refs[:8]
        refs = refs[8:]
        if step == 0:
            sources = (field, adjoint, speed2, field_prev, adjoint_prev)
            field, adjoint, speed2 = refs[:3]
            refs = refs[3:]
            field_prev, adjoint_prev, load_sems = refs[3:]
            targets = (field, adjoint, speed2, field_prev, adjoint_prev)
            loads = [
                pltpu.make_async_copy(source, target, load_sems.at[i])
                for i, (source, target) in enumerate(zip(sources, targets))
            ]
        coupling, change, tiles = refs[:3]
    for copy in loads:
        copy.start()

    cells_z, cells_x, along = field.shape
    slots, width = change.shape[1:]
    parts = along // width
    meta = lines[pl.ds(META, slots, stride=LINES), :]

    def line(n):
        return lines[pl.ds(n - 1, slots, stride=LINES), :]

    scalars = [None] + [column(meta, n) for n in range(1, TERMS + 1)]

    def surfaces(at, known):
        found = []
        for side in range(2):
            new = line(at + 1) if side == 0 else None
            for t in range(at + 1):
                term = scalars[at + 1 - t] * known[t][side]
                new = term if new is None else new + term
            found.append(new)
        return found

    def extra(side, z):
        return jnp.concatenate([coupling[side * parts + part, z] for part in range(parts)], axis=1)

    surface = surfaces(step, pushes)
    for side in range(2):
        change[side] = BETA * (surface[side] - picked[side])
    coupling[...] = jnp.zeros_like(coupling)
    couple(rows_ref, change, coupling)
    for copy in loads:
        copy.wait()

    z_halo = [incoming("gz", z_from_outer[side], z_from_inner[side]) for side in range(2)]

    def plane(z, below, above):
        speed = speed2[z]
        for side, (now, before, out) in enumerate(
            ((field, field_prev, field_out), (adjoint, adjoint_prev, adjoint_out))
        ):
            low, high = incoming(
                "gx", side_row(x_from_outer, side, z), side_row(x_from_inner, side, z)
            )
            beside = below(side, now) + above(side, now)
            new = stencil(now[z], before[z], speed, beside, low, high, extra(side, z))
            out[z] = new
            keep_sides(new, side, z, x_outer, x_inner)

    plane(
        0,
        lambda side, now: z_halo[side][0],
        lambda side, now: now[1],
    )
    inner_planes(cells_z, plane)
    plane(
        cells_z - 1,
        lambda side, now: now[cells_z - 2],
        lambda side, now: z_halo[side][1],
    )
    for side, out in enumerate((field_out, adjoint_out)):
        z_outer[side], z_inner[side] = outgoing("gz", out[0], out[cells_z - 1])
    pick(rows_ref, (field_out, adjoint_out), picked_out, tiles)
    for side in range(2):
        push_out[side] = KAPPA * (picked_out[side] - surface[side])
    if not ahead:
        return

    known = [*pushes, push_out]
    total = jnp.zeros((slots, width), jnp.float32)
    for late in range(STEPS):
        inside = (STEPS - late) * line(TERMS - late)
        for t in range(STEPS - late):
            inside = inside + ((STEPS - late - t) * scalars[TERMS - late - t]) * known[t][0]
        total = total + known[late][1] * inside
    patches = gradient_out.shape[0]
    ids = column(meta, 0).astype(jnp.int32)
    owners = lax.broadcasted_iota(jnp.int32, (slots, patches), 1) == ids
    gradient_out[...] = lax.dot_general(
        owners.astype(jnp.float32),
        total,
        (((0,), (0,)), ((), ())),
        precision=lax.Precision.HIGHEST,
        preferred_element_type=jnp.float32,
    )

    surface = surfaces(step + 1, known)
    for side in range(2):
        change[side] = BETA * (surface[side] - picked_out[side])
    couple(rows_ref, change, coupling)

    def next_plane(z, below, above):
        speed = speed2[z]
        keep_side(speed, z, speed_low, speed_high)
        for side, (now, before, out) in enumerate(
            ((field_out, field, partial[0]), (adjoint_out, adjoint, partial[1]))
        ):
            beside = below(side, now) + above(side, now)
            out[z] = stencil(now[z], before[z], speed, beside, None, None, extra(side, z))

    next_plane(0, lambda side, now: 0.0, lambda side, now: now[1])
    inner_planes(cells_z, next_plane)
    next_plane(cells_z - 1, lambda side, now: now[cells_z - 2], lambda side, now: 0.0)
    copies = [pltpu.make_async_copy(partial[i], partial_hbm[i], sems.at[i]) for i in range(2)]
    for copy in copies:
        copy.start()
    for copy in copies:
        copy.wait()


def step_call(step, rows, field, field_prev, adjoint, adjoint_prev, speed2, halos, lines, picked, pushes, patches):
    slots, width = pushes[0].shape[1:]
    ahead = step == STEPS - 2
    cells_z, cells_x, along = field.shape
    parts = along // width
    whole = jax.ShapeDtypeStruct(field.shape, jnp.float32)
    edges = edge_shapes(field, slots, width)
    in_vmem = pl.BlockSpec(memory_space=VMEM)
    scratch = [
        pltpu.VMEM((2 * parts, cells_z + 1, cells_x, width), jnp.float32),
        pltpu.VMEM((2, slots, width), jnp.float32),
        pltpu.VMEM((2, 8 * slots, width), jnp.float32),
    ]
    if ahead:
        sides = jax.ShapeDtypeStruct((parts, cells_z, width), jnp.float32)
        shapes = edges[:4] + [sides, sides, jax.ShapeDtypeStruct((patches, width), jnp.float32)]
        out_specs = [in_vmem] * 7 + [pl.BlockSpec(memory_space=HBM)] * 2
        shapes = shapes + [HBM(field.shape, jnp.float32)] * 2
        scratch = scratch + [pltpu.VMEM(field.shape, jnp.float32)] * 2
        scratch = scratch + [pltpu.VMEM((2, slots, width), jnp.float32)] * 2
        scratch = scratch + [pltpu.VMEM(field.shape, jnp.float32)] * 2
        scratch = scratch + [pltpu.SemaphoreType.DMA((2,))]
    else:
        shapes = [whole] * 2 + edges
        if step == 0:
            shapes = shapes + [whole] * 3
            scratch = scratch + [pltpu.VMEM(field.shape, jnp.float32)] * 2
            scratch = scratch + [pltpu.SemaphoreType.DMA((5,))]
        out_specs = [in_vmem] * len(shapes)
    arrays = [field, field_prev, adjoint, adjoint_prev, speed2]
    if step == 0:
        arrays = in_hbm(*arrays)
    operands = [*arrays, *halos, lines, picked, *pushes]
    return pl.pallas_call(
        functools.partial(step_kernel, step),
        in_specs=[pl.BlockSpec(memory_space=SMEM)]
        + [pl.BlockSpec(memory_space=HBM) if step == 0 else in_vmem] * 5
        + [in_vmem] * (len(operands) - 5),
        out_specs=out_specs,
        out_shape=shapes,
        scratch_shapes=scratch,
        compiler_params=params(16),
        name=f"step{step}",
    )(rows, *operands)


def keep_side(cells, z, x_low, x_high):
    last_x, width = cells.shape[0] - 1, x_low.shape[2]
    for part in range(x_low.shape[0]):
        lanes = slice(part * width, (part + 1) * width)
        x_low[part, pl.ds(z, 1), :] = cells[0:1, lanes]
        x_high[part, pl.ds(z, 1), :] = cells[last_x : last_x + 1, lanes]


def finish_kernel(field, adjoint, speed_z_low, speed_z_high, speed_low, speed_high, x_from_outer, x_from_inner, z_from_outer, z_from_inner, field_out, adjoint_out):
    block, cells_x, along = field.shape
    row_id = lax.broadcasted_iota(jnp.int32, (cells_x, along), 0)
    step, steps = pl.program_id(0), pl.num_programs(0)

    def speeds(side_plane, z):
        parts = side_plane.shape[0]
        return jnp.concatenate([side_plane[p, pl.ds(z, 1), :] for p in range(parts)], axis=1)

    for side, (partial, out) in enumerate(((field, field_out), (adjoint, adjoint_out))):
        for z in range(block):
            low, high = incoming(
                "gx", side_row(x_from_outer, side, z), side_row(x_from_inner, side, z)
            )
            low, high = low * speeds(speed_low, z), high * speeds(speed_high, z)
            added = jnp.where(row_id == 0, low, jnp.where(row_id == cells_x - 1, high, 0.0))
            out[z] = partial[z] + added

        before, after = incoming("gz", z_from_outer[side], z_from_inner[side])

        @pl.when(step == 0)
        def _():
            out[0] = out[0] + speed_z_low[0] * before

        @pl.when(step == steps - 1)
        def _():
            out[block - 1] = out[block - 1] + speed_z_high[0] * after


def finish_call(field, adjoint, speed2, speed_low, speed_high, halos):
    cells_z, cells_x, along = field.shape
    parts, _, width = speed_low.shape
    block = 8
    planes = pl.BlockSpec((block, cells_x, along), lambda i: (i, 0, 0))
    sides = pl.BlockSpec((parts, block, width), lambda i: (0, i, 0))
    both = pl.BlockSpec((2, parts, block, width), lambda i: (0, 0, i, 0))
    edge = pl.BlockSpec((2, cells_x, along), lambda i: (0, 0, 0))
    return pl.pallas_call(
        finish_kernel,
        grid=(cells_z // block,),
        in_specs=[
            planes,
            planes,
            pl.BlockSpec((1, cells_x, along), lambda i: (0, 0, 0)),
            pl.BlockSpec((1, cells_x, along), lambda i: (cells_z - 1, 0, 0)),
            sides,
            sides,
            both,
            both,
            edge,
            edge,
        ],
        out_specs=[planes, planes],
        out_shape=[jax.ShapeDtypeStruct(field.shape, jnp.float32)] * 2,
        compiler_params=params(8),
        name="finish",
    )(*in_hbm(field, adjoint), speed2, speed2, speed_low, speed_high, *halos)


def swaps(axis, first):
    count = lax.axis_size(axis)
    if first:
        return [(i, i ^ 1) for i in range(count)]
    return [(i, (i + 1 if i % 2 else i - 1) % count) for i in range(count)]


def exchange(edges):
    axes = (("gx", False), ("gx", True), ("gz", False), ("gz", True))
    return [lax.ppermute(edge, axis, swaps(axis, first)) for edge, (axis, first) in zip(edges, axes)]


def body(
    pressure_now,
    pressure_prev,
    adjoint_now,
    adjoint_prev,
    speed2,
    layer_state,
    layer_maps,
    send_rows,
    slot_patch,
    patch_material,
):
    slots, _, width = layer_state.shape
    patches = patch_material.shape[0]
    devices = lax.axis_size(("gx", "gz"))
    rows = send_rows.reshape(-1)

    lines = surface_rows(layer_maps, slot_patch, patch_material, layer_state)
    lines = lax.all_to_all(lines, ("gx", "gz"), split_axis=0, concat_axis=0, tiled=True)
    lines = lines.reshape(slots * LINES, width)

    results = first_edges(rows, pressure_now, adjoint_now, slots, width)
    fields = (pressure_now, pressure_prev, adjoint_now, adjoint_prev)
    speed = speed2
    halos = exchange(results[:4])
    pushes, picked = [results[4]], results[5]
    for step in range(STEPS - 1):
        results = step_call(step, rows, *fields, speed, halos, lines, picked, pushes, patches)
        if step < STEPS - 2:
            if step == 0:
                fields, speed = (results[8], None, results[9], None), results[10]
            fields = (results[0], fields[0], results[1], fields[2])
            halos = exchange(results[2:6])
            pushes.append(results[6])
            picked = results[7]
    speed_low, speed_high, gradient, *partial = results[4:]
    parts = gradient.reshape(devices, patches // devices, width)
    parts = lax.all_to_all(parts, ("gx", "gz"), split_axis=0, concat_axis=0, tiled=True)
    halos = exchange(results[:4])
    field, adjoint = finish_call(*partial, speed2, speed_low, speed_high, halos)
    return field, adjoint, jnp.sum(parts, axis=0)


def solution(mesh):
    grid = P("gz", "gx", None)
    split = P(("gx", "gz"), None, None)
    in_specs = (grid, grid, grid, grid, grid, split, P(), split, P(("gx", "gz")), P())
    out_specs = (grid, grid, P(("gx", "gz"), None))
    return jax.shard_map(body, mesh=mesh, in_specs=in_specs, out_specs=out_specs, check_vma=False)
```

time: 135 us -> 94 us (0.70)
  Pallas kernels: 55 us -> 32.2 us
  local copies, waits for them, and re-layouts: 14.2 us -> 0.01 us
  waiting for transfers between devices: 15.4 us -> 11.2 us
    pallas_call x4 -> x3, Pallas kernels: 44.4 us -> 20.6 us  [step_call(): pl.pallas_call(functools.partial(step_kernel, step), in_specs=[pl.BlockSp...]
    unnamed x36 -> x4, local copies, waits for them, and re-layouts: 14.2 us -> 0.01 us
    ppermute x16, waiting for transfers between devices: 15.4 us -> 10.8 us  [exchange(): lax.ppermute(edge, axis, swaps(axis, first))]
    ppermute x16, starting transfers between devices: 27.3 us -> 28.8 us  [exchange(): lax.ppermute(edge, axis, swaps(axis, first))]
    pallas_call x2 -> x3, Pallas kernels: 10.6 us -> 11.6 us  [the longest x1 4.84 us: surface_rows(): pl.pallas_call(surface_kernel, in_specs=[pl.BlockSpec(memory_space=HBM)]...]
  transfers between devices with their start and end apart: 18 -> 18, of which waited for: 9 -> 9; matrix products, arithmetic and copies ran while one was open for 0% -> 0% of each run, Pallas kernels for 10% -> 7%
where the time goes in v2:
time: 94 us; the launch traced here: 93.7 us
  starting transfers between devices  48.8 us (52%)
  Pallas kernels  32.2 us (34%)
  waiting for transfers between devices  11.2 us (12%)
    ppermute x16, starting transfers between devices, exchange(): lax.ppermute(edge, axis, swaps(axis, first))  28.8 us
    pallas_call x3, Pallas kernels, step_call(): pl.pallas_call(functools.partial(step_kernel, step), in_specs=[pl.BlockSp...  20.6 us
    all_to_all x1, starting transfers between devices, body(): lax.all_to_all(lines, ('gx', 'gz'), split_axis=0, concat_axis=0, tiled=True)  11.5 us
    ppermute x16, waiting for transfers between devices, exchange(): lax.ppermute(edge, axis, swaps(axis, first))  10.8 us
    all_to_all x1, starting transfers between devices, body(): lax.all_to_all(parts, ('gx', 'gz'), split_axis=0, concat_axis=0, tiled=True)  8.49 us
    pallas_call x1, Pallas kernels, surface_rows(): pl.pallas_call(surface_kernel, in_specs=[pl.BlockSpec(memory_space=HBM)]...  4.84 us
    pallas_call x1, Pallas kernels, finish_call(): pl.pallas_call(finish_kernel, grid=(cells_z // block,), in_specs=[planes,...  3.98 us
    pallas_call x1, Pallas kernels, first_edges(): pl.pallas_call(edges_kernel, in_specs=[pl.BlockSpec(memory_space=HBM)] *...  2.83 us
  transfers between devices with their start and end apart: 18, of which 9 were waited for; matrix products, arithmetic and copies ran while one was open for 0% of the time, Pallas kernels for 7%

profile of v2, /device:TPU:1, one launch (start us, length us, event | category | flops | bytes accessed | tf_op | source)
XLA Modules:
  0.0 93.7 jit_solution(5579397987199144334)
XLA Ops:
  0.6 4.8 %surface_rows.1 = f32[128,8,128]{2,1,0:T(8,128)} custom-call(f32[8,64,64]{2,1,0:T(8,128)} %maps_hbm.1, s32[128]{0:T(128)} %patch_hbm.1, s32[1024]{0:T(1024)} %material_hbm.1, f32[128,64,128]{2,1,0:T(8,128)} %layer_hbm.1), custom_call_target="tpu_custom_call" | custom-call | tf_op jit(solution)/shard_map/surface_rows/pallas_call | solution.py:98
  5.5 11.5 %all-to-all-start = ((f32[128,8,128]{2,1,0:T(8,128)}), f32[128,8,128]{2,1,0:T(8,128)S(1)}, u32[]{:S(2)}, u32[]{:S(2)}) async-start(f32[128,8,128]{2,1,0:T(8,128)} %surface_rows.1), calls=%async_computation | async-start | bytes 1048576 | tf_op jit(solution)/shard_map/all_to_all | solution.py:562
  17.0 2.8 %edges.1 = (f32[2,4,32,128]{3,2,1,0:T(8,128)S(1)}, f32[2,4,32,128]{3,2,1,0:T(8,128)S(1)}, f32[2,16,512]{2,1,0:T(8,128)S(1)}, f32[2,16,512]{2,1,0:T(8,128)S(1)}, ...) custom-call(s32[128]{0:T(128)} %bitcast.6, f32[32,16,512]{2,1,0:T(8,128)} %refs_1_.1, f32[32,16,512]{2,1,0:T(8,128)} %refs_3_.1), custom_call_target="tpu_custom_call" | custom-call | tf_op jit(solution)/shard_map/edges/pallas_call | solution.py:227
  19.8 4.9 %collective-permute-start = (f32[2,4,32,128]{3,2,1,0:T(8,128)S(1)}, f32[2,4,32,128]{3,2,1,0:T(8,128)S(1)}, u32[]{:S(2)}, u32[]{:S(2)}) collective-permute-start(f32[2,4,32,128]{3,2,1,0:T(8,128)S(1)} %get-tuple-element.39), channel_id=1, source_target_pairs={{0,120},{8,16},{16,8},{24,32},{32,24},{40,48},{48,40},{56,64},{64,... | collective-permute-start | bytes 393224 | tf_op jit(solution)/shard_map/ppermute | solution.py:541
  24.7 2.0 %collective-permute-start.2 = (f32[2,16,512]{2,1,0:T(8,128)S(1)}, f32[2,16,512]{2,1,0:T(8,128)S(1)}, u32[]{:S(2)}, u32[]{:S(2)}) collective-permute-start(f32[2,16,512]{2,1,0:T(8,128)S(1)} %get-tuple-element.41), channel_id=1, source_target_pairs={{0,7},{1,2},{2,1},{3,4},{4,3},{5,6},{6,5},{7,0},{8,15},{9,10},{10,... | collective-permute-start | bytes 196616 | tf_op jit(solution)/shard_map/ppermute | solution.py:541
  26.7 1.6 %collective-permute-start.3 = (f32[2,16,512]{2,1,0:T(8,128)S(1)}, f32[2,16,512]{2,1,0:T(8,128)S(1)}, u32[]{:S(2)}, u32[]{:S(2)}) collective-permute-start(f32[2,16,512]{2,1,0:T(8,128)S(1)} %get-tuple-element.42), channel_id=1, source_target_pairs={{0,1},{1,0},{2,3},{3,2},{4,5},{5,4},{6,7},{7,6},{8,9},{9,8},{10,11... | collective-permute-start | bytes 196616 | tf_op jit(solution)/shard_map/ppermute | solution.py:541
  28.3 0.8 collective-permute-done.2.refs_8_
  29.2 1.3 %collective-permute-done.refs_6_ = f32[2,4,32,128]{3,2,1,0:T(8,128)S(1)} collective-permute-done((f32[2,4,32,128]{3,2,1,0:T(8,128)S(1)}, f32[2,4,32,128]{3,2,1,0:T(8,128)S(1)}, u32[]{:S(2)}, u32[]{:S(2)}) %collective-permute-start) | collective-permute-done | bytes 131104 | tf_op jit(solution)/shard_map/ppermute | solution.py:541
  30.9 6.3 %step0.1 = (f32[32,16,512]{2,1,0:T(8,128)S(1)}, f32[32,16,512]{2,1,0:T(8,128)S(1)}, f32[2,4,32,128]{3,2,1,0:T(8,128)S(1)}, f32[2,4,32,128]{3,2,1,0:T(8,128)S(1)}...) custom-call(s32[128]{0:T(128)S(1)} %bitcast.7, ...), custom_call_target="tpu_custom_call" | custom-call | tf_op jit(solution)/shard_map/step0/pallas_call | solution.py:452
  37.1 2.0 %collective-permute-start.4 = (f32[2,4,32,128]{3,2,1,0:T(8,128)S(1)}, f32[2,4,32,128]{3,2,1,0:T(8,128)S(1)}, u32[]{:S(2)}, u32[]{:S(2)}) collective-permute-start(f32[2,4,32,128]{3,2,1,0:T(8,128)S(1)} %get-tuple-element.50), channel_id=1, source_target_pairs={{0,120},{8,16},{16,8},{24,32},{32,24},{40,48},{48,40},{56,64},{64,... | collective-permute-start | bytes 393224 | tf_op jit(solution)/shard_map/ppermute | solution.py:541
  39.2 2.8 %collective-permute-start.6 = (f32[2,16,512]{2,1,0:T(8,128)S(1)}, f32[2,16,512]{2,1,0:T(8,128)S(1)}, u32[]{:S(2)}, u32[]{:S(2)}) collective-permute-start(f32[2,16,512]{2,1,0:T(8,128)S(1)} %get-tuple-element.52), channel_id=1, source_target_pairs={{0,7},{1,2},{2,1},{3,4},{4,3},{5,6},{6,5},{7,0},{8,15},{9,10},{10,... | collective-permute-start | bytes 196616 | tf_op jit(solution)/shard_map/ppermute | solution.py:541
  42.8 1.5 %collective-permute-done.6.refs_8_ = f32[2,16,512]{2,1,0:T(8,128)S(1)} collective-permute-done((f32[2,16,512]{2,1,0:T(8,128)S(1)}, f32[2,16,512]{2,1,0:T(8,128)S(1)}, u32[]{:S(2)}, u32[]{:S(2)}) %collective-permute-start.6) | collective-permute-done | bytes 65568 | tf_op jit(solution)/shard_map/ppermute | solution.py:541
  44.4 4.5 %step1.1 = (f32[32,16,512]{2,1,0:T(8,128)S(1)}, f32[32,16,512]{2,1,0:T(8,128)S(1)}, f32[2,4,32,128]{3,2,1,0:T(8,128)S(1)}, f32[2,4,32,128]{3,2,1,0:T(8,128)S(1)}...) custom-call(s32[128]{0:T(128)S(1)} %bitcast.8, ...), custom_call_target="tpu_custom_call" | custom-call | tf_op jit(solution)/shard_map/step1/pallas_call | solution.py:452
  48.9 2.0 %collective-permute-start.8 = (f32[2,4,32,128]{3,2,1,0:T(8,128)S(1)}, f32[2,4,32,128]{3,2,1,0:T(8,128)S(1)}, u32[]{:S(2)}, u32[]{:S(2)}) collective-permute-start(f32[2,4,32,128]{3,2,1,0:T(8,128)S(1)} %get-tuple-element.58), channel_id=1, source_target_pairs={{0,120},{8,16},{16,8},{24,32},{32,24},{40,48},{48,40},{56,64},{64,... | collective-permute-start | bytes 393224 | tf_op jit(solution)/shard_map/ppermute | solution.py:541
  50.9 4.0 %collective-permute-start.10 = (f32[2,16,512]{2,1,0:T(8,128)S(1)}, f32[2,16,512]{2,1,0:T(8,128)S(1)}, u32[]{:S(2)}, u32[]{:S(2)}) collective-permute-start(f32[2,16,512]{2,1,0:T(8,128)S(1)} %get-tuple-element.60), channel_id=1, source_target_pairs={{0,7},{1,2},{2,1},{3,4},{4,3},{5,6},{6,5},{7,0},{8,15},{9,10},{10,... | collective-permute-start | bytes 196616 | tf_op jit(solution)/shard_map/ppermute | solution.py:541
  55.1 2.0 %collective-permute-done.10.refs_8_ = f32[2,16,512]{2,1,0:T(8,128)S(1)} collective-permute-done((f32[2,16,512]{2,1,0:T(8,128)S(1)}, f32[2,16,512]{2,1,0:T(8,128)S(1)}, u32[]{:S(2)}, u32[]{:S(2)}) %collective-permute-start.10) | collective-permute-done | bytes 65568 | tf_op jit(solution)/shard_map/ppermute | solution.py:541
  57.2 9.8 %step2.1 = (f32[2,4,32,128]{3,2,1,0:T(8,128)S(1)}, f32[2,4,32,128]{3,2,1,0:T(8,128)S(1)}, f32[2,16,512]{2,1,0:T(8,128)S(1)}, f32[2,16,512]{2,1,0:T(8,128)S(1)}, ...) custom-call(s32[128]{0:T(128)S(1)} %bitcast.9, ...), custom_call_target="tpu_custom_call" | custom-call | tf_op jit(solution)/shard_map/step2/pallas_call | solution.py:452
  66.9 8.5 %all-to-all-start.1 = ((f32[128,8,128]{2,1,0:T(8,128)}), f32[128,8,128]{2,1,0:T(8,128)S(1)}, u32[]{:S(2)}, u32[]{:S(2)}) async-start(f32[128,8,128]{2,1,0:T(8,128)} %bitcast.2), calls=%async_computation.1 | async-start | bytes 1048576 | tf_op jit(solution)/shard_map/all_to_all | solution.py:581
  75.4 4.9 %collective-permute-start.12 = (f32[2,4,32,128]{3,2,1,0:T(8,128)S(1)}, f32[2,4,32,128]{3,2,1,0:T(8,128)S(1)}, u32[]{:S(2)}, u32[]{:S(2)}) collective-permute-start(f32[2,4,32,128]{3,2,1,0:T(8,128)S(1)} %get-tuple-element.68), channel_id=1, source_target_pairs={{0,120},{8,16},{16,8},{24,32},{32,24},{40,48},{48,40},{56,64},{64,... | collective-permute-start | bytes 393224 | tf_op jit(solution)/shard_map/ppermute | solution.py:541
  80.3 2.0 %collective-permute-start.14 = (f32[2,16,512]{2,1,0:T(8,128)S(1)}, f32[2,16,512]{2,1,0:T(8,128)S(1)}, u32[]{:S(2)}, u32[]{:S(2)}) collective-permute-start(f32[2,16,512]{2,1,0:T(8,128)S(1)} %get-tuple-element.70), channel_id=1, source_target_pairs={{0,7},{1,2},{2,1},{3,4},{4,3},{5,6},{6,5},{7,0},{8,15},{9,10},{10,... | collective-permute-start | bytes 196616 | tf_op jit(solution)/shard_map/ppermute | solution.py:541
  82.3 1.6 %collective-permute-start.15 = (f32[2,16,512]{2,1,0:T(8,128)S(1)}, f32[2,16,512]{2,1,0:T(8,128)S(1)}, u32[]{:S(2)}, u32[]{:S(2)}) collective-permute-start(f32[2,16,512]{2,1,0:T(8,128)S(1)} %get-tuple-element.71), channel_id=1, source_target_pairs={{0,1},{1,0},{2,3},{3,2},{4,5},{5,4},{6,7},{7,6},{8,9},{9,8},{10,11... | collective-permute-start | bytes 196616 | tf_op jit(solution)/shard_map/ppermute | solution.py:541
  83.9 1.9 %collective-permute-done.14.z_from_outer = f32[2,16,512]{2,1,0:T(8,128)S(1)} collective-permute-done((f32[2,16,512]{2,1,0:T(8,128)S(1)}, f32[2,16,512]{2,1,0:T(8,128)S(1)}, u32[]{:S(2)}, u32[]{:S(2)}) %collective-permute-start.14) | collective-permute-done | bytes 65568 | tf_op jit(solution)/shard_map/ppermute | solution.py:541
  85.9 3.1 %collective-permute-done.12.x_from_outer = f32[2,4,32,128]{3,2,1,0:T(8,128)S(1)} collective-permute-done((f32[2,4,32,128]{3,2,1,0:T(8,128)S(1)}, f32[2,4,32,128]{3,2,1,0:T(8,128)S(1)}, u32[]{:S(2)}, u32[]{:S(2)}) %collective-permute-start.12) | collective-permute-done | bytes 131104 | tf_op jit(solution)/shard_map/ppermute | solution.py:541
  89.0 4.0 %finish.1 = (f32[32,16,512]{2,1,0:T(8,128)}, f32[32,16,512]{2,1,0:T(8,128)}) custom-call(f32[32,16,512]{2,1,0:T(8,128)} %get-tuple-element.64.field, f32[32,16,512]{2,1,0:T(8,128)} %get-tuple-element.65.adjoint, f32[32,16,512]{2,1,0:T(8,128)S(1)} %copy-done, f32[32,16,512]{2,1,0:T(8,128)S(1)} %copy-done, f32[4,32,128]{2,1,0:T(8,128)S(1)} %get-tuple-element.66.speed_low, ...), custom_call_target="tpu_custom_call" | custom-call | tf_op jit(solution)/shard_map/finish/pallas_call | solution.py:510
  (23 shorter events, 2.3 us)
Async XLA Ops:
  0.6 30.2 %copy-start.1 = (s32[1,128,1]{1,2,0:T(1,128)S(1)}, s32[1,128,1]{1,2,0:T(1,128)}, u32[]{:S(2)}) copy-start(s32[1,128,1]{1,2,0:T(1,128)} %param.17) | copy-start | bytes 1540
  5.5 25.4 %all-to-all-start = ((f32[128,8,128]{2,1,0:T(8,128)}), f32[128,8,128]{2,1,0:T(8,128)S(1)}, u32[]{:S(2)}, u32[]{:S(2)}) async-start(f32[128,8,128]{2,1,0:T(8,128)} %surface_rows.1), calls=%async_computation | async-start | bytes 1048576 | tf_op jit(solution)/shard_map/all_to_all | solution.py:562
  19.8 10.7 %collective-permute-start = (f32[2,4,32,128]{3,2,1,0:T(8,128)S(1)}, f32[2,4,32,128]{3,2,1,0:T(8,128)S(1)}, u32[]{:S(2)}, u32[]{:S(2)}) collective-permute-start(f32[2,4,32,128]{3,2,1,0:T(8,128)S(1)} %get-tuple-element.39), channel_id=1, source_target_pairs={{0,120},{8,16},{16,8},{24,32},{32,24},{40,48},{48,40},{56,64},{64,... | collective-permute-start | bytes 393224 | tf_op jit(solution)/shard_map/ppermute | solution.py:541
  24.7 5.8 %collective-permute-start.1 = (f32[2,4,32,128]{3,2,1,0:T(8,128)S(1)}, f32[2,4,32,128]{3,2,1,0:T(8,128)S(1)}, u32[]{:S(2)}, u32[]{:S(2)}) collective-permute-start(f32[2,4,32,128]{3,2,1,0:T(8,128)S(1)} %get-tuple-element.40), channel_id=1, source_target_pairs={{0,8},{8,0},{16,24},{24,16},{32,40},{40,32},{48,56},{56,48},{64,72... | collective-permute-start | bytes 393224 | tf_op jit(solution)/shard_map/ppermute | solution.py:541
  24.7 4.4 %collective-permute-start.2 = (f32[2,16,512]{2,1,0:T(8,128)S(1)}, f32[2,16,512]{2,1,0:T(8,128)S(1)}, u32[]{:S(2)}, u32[]{:S(2)}) collective-permute-start(f32[2,16,512]{2,1,0:T(8,128)S(1)} %get-tuple-element.41), channel_id=1, source_target_pairs={{0,7},{1,2},{2,1},{3,4},{4,3},{5,6},{6,5},{7,0},{8,15},{9,10},{10,... | collective-permute-start | bytes 196616 | tf_op jit(solution)/shard_map/ppermute | solution.py:541
  26.7 2.5 %collective-permute-start.3 = (f32[2,16,512]{2,1,0:T(8,128)S(1)}, f32[2,16,512]{2,1,0:T(8,128)S(1)}, u32[]{:S(2)}, u32[]{:S(2)}) collective-permute-start(f32[2,16,512]{2,1,0:T(8,128)S(1)} %get-tuple-element.42), channel_id=1, source_target_pairs={{0,1},{1,0},{2,3},{3,2},{4,5},{5,4},{6,7},{7,6},{8,9},{9,8},{10,11... | collective-permute-start | bytes 196616 | tf_op jit(solution)/shard_map/ppermute | solution.py:541
  37.1 7.2 %collective-permute-start.4 = (f32[2,4,32,128]{3,2,1,0:T(8,128)S(1)}, f32[2,4,32,128]{3,2,1,0:T(8,128)S(1)}, u32[]{:S(2)}, u32[]{:S(2)}) collective-permute-start(f32[2,4,32,128]{3,2,1,0:T(8,128)S(1)} %get-tuple-element.50), channel_id=1, source_target_pairs={{0,120},{8,16},{16,8},{24,32},{32,24},{40,48},{48,40},{56,64},{64,... | collective-permute-start | bytes 393224 | tf_op jit(solution)/shard_map/ppermute | solution.py:541
  39.2 5.2 %collective-permute-start.5 = (f32[2,4,32,128]{3,2,1,0:T(8,128)S(1)}, f32[2,4,32,128]{3,2,1,0:T(8,128)S(1)}, u32[]{:S(2)}, u32[]{:S(2)}) collective-permute-start(f32[2,4,32,128]{3,2,1,0:T(8,128)S(1)} %get-tuple-element.51), channel_id=1, source_target_pairs={{0,8},{8,0},{16,24},{24,16},{32,40},{40,32},{48,56},{56,48},{64,72... | collective-permute-start | bytes 393224 | tf_op jit(solution)/shard_map/ppermute | solution.py:541
  39.2 5.1 %collective-permute-start.6 = (f32[2,16,512]{2,1,0:T(8,128)S(1)}, f32[2,16,512]{2,1,0:T(8,128)S(1)}, u32[]{:S(2)}, u32[]{:S(2)}) collective-permute-start(f32[2,16,512]{2,1,0:T(8,128)S(1)} %get-tuple-element.52), channel_id=1, source_target_pairs={{0,7},{1,2},{2,1},{3,4},{4,3},{5,6},{6,5},{7,0},{8,15},{9,10},{10,... | collective-permute-start | bytes 196616 | tf_op jit(solution)/shard_map/ppermute | solution.py:541
  42.0 2.2 %collective-permute-start.7 = (f32[2,16,512]{2,1,0:T(8,128)S(1)}, f32[2,16,512]{2,1,0:T(8,128)S(1)}, u32[]{:S(2)}, u32[]{:S(2)}) collective-permute-start(f32[2,16,512]{2,1,0:T(8,128)S(1)} %get-tuple-element.53), channel_id=1, source_target_pairs={{0,1},{1,0},{2,3},{3,2},{4,5},{5,4},{6,7},{7,6},{8,9},{9,8},{10,11... | collective-permute-start | bytes 196616 | tf_op jit(solution)/shard_map/ppermute | solution.py:541
  48.9 40.1 %copy-start = (f32[32,16,512]{2,1,0:T(8,128)S(1)}, f32[32,16,512]{2,1,0:T(8,128)}, u32[]{:S(2)}) copy-start(f32[32,16,512]{2,1,0:T(8,128)} %speed_z_high.1) | copy-start | bytes 3145732
  48.9 8.2 %collective-permute-start.8 = (f32[2,4,32,128]{3,2,1,0:T(8,128)S(1)}, f32[2,4,32,128]{3,2,1,0:T(8,128)S(1)}, u32[]{:S(2)}, u32[]{:S(2)}) collective-permute-start(f32[2,4,32,128]{3,2,1,0:T(8,128)S(1)} %get-tuple-element.58), channel_id=1, source_target_pairs={{0,120},{8,16},{16,8},{24,32},{32,24},{40,48},{48,40},{56,64},{64,... | collective-permute-start | bytes 393224 | tf_op jit(solution)/shard_map/ppermute | solution.py:541
  50.9 6.2 %collective-permute-start.9 = (f32[2,4,32,128]{3,2,1,0:T(8,128)S(1)}, f32[2,4,32,128]{3,2,1,0:T(8,128)S(1)}, u32[]{:S(2)}, u32[]{:S(2)}) collective-permute-start(f32[2,4,32,128]{3,2,1,0:T(8,128)S(1)} %get-tuple-element.59), channel_id=1, source_target_pairs={{0,8},{8,0},{16,24},{24,16},{32,40},{40,32},{48,56},{56,48},{64,72... | collective-permute-start | bytes 393224 | tf_op jit(solution)/shard_map/ppermute | solution.py:541
  50.9 6.2 %collective-permute-start.10 = (f32[2,16,512]{2,1,0:T(8,128)S(1)}, f32[2,16,512]{2,1,0:T(8,128)S(1)}, u32[]{:S(2)}, u32[]{:S(2)}) collective-permute-start(f32[2,16,512]{2,1,0:T(8,128)S(1)} %get-tuple-element.60), channel_id=1, source_target_pairs={{0,7},{1,2},{2,1},{3,4},{4,3},{5,6},{6,5},{7,0},{8,15},{9,10},{10,... | collective-permute-start | bytes 196616 | tf_op jit(solution)/shard_map/ppermute | solution.py:541
  54.9 2.2 %collective-permute-start.11 = (f32[2,16,512]{2,1,0:T(8,128)S(1)}, f32[2,16,512]{2,1,0:T(8,128)S(1)}, u32[]{:S(2)}, u32[]{:S(2)}) collective-permute-start(f32[2,16,512]{2,1,0:T(8,128)S(1)} %get-tuple-element.61), channel_id=1, source_target_pairs={{0,1},{1,0},{2,3},{3,2},{4,5},{5,4},{6,7},{7,6},{8,9},{9,8},{10,11... | collective-permute-start | bytes 196616 | tf_op jit(solution)/shard_map/ppermute | solution.py:541
  66.9 26.0 %all-to-all-start.1 = ((f32[128,8,128]{2,1,0:T(8,128)}), f32[128,8,128]{2,1,0:T(8,128)S(1)}, u32[]{:S(2)}, u32[]{:S(2)}) async-start(f32[128,8,128]{2,1,0:T(8,128)} %bitcast.2), calls=%async_computation.1 | async-start | bytes 1048576 | tf_op jit(solution)/shard_map/all_to_all | solution.py:581
  75.4 13.5 %collective-permute-start.12 = (f32[2,4,32,128]{3,2,1,0:T(8,128)S(1)}, f32[2,4,32,128]{3,2,1,0:T(8,128)S(1)}, u32[]{:S(2)}, u32[]{:S(2)}) collective-permute-start(f32[2,4,32,128]{3,2,1,0:T(8,128)S(1)} %get-tuple-element.68), channel_id=1, source_target_pairs={{0,120},{8,16},{16,8},{24,32},{32,24},{40,48},{48,40},{56,64},{64,... | collective-permute-start | bytes 393224 | tf_op jit(solution)/shard_map/ppermute | solution.py:541
  80.3 8.6 %collective-permute-start.13 = (f32[2,4,32,128]{3,2,1,0:T(8,128)S(1)}, f32[2,4,32,128]{3,2,1,0:T(8,128)S(1)}, u32[]{:S(2)}, u32[]{:S(2)}) collective-permute-start(f32[2,4,32,128]{3,2,1,0:T(8,128)S(1)} %get-tuple-element.69), channel_id=1, source_target_pairs={{0,8},{8,0},{16,24},{24,16},{32,40},{40,32},{48,56},{56,48},{64,72... | collective-permute-start | bytes 393224 | tf_op jit(solution)/shard_map/ppermute | solution.py:541
  80.3 5.5 %collective-permute-start.14 = (f32[2,16,512]{2,1,0:T(8,128)S(1)}, f32[2,16,512]{2,1,0:T(8,128)S(1)}, u32[]{:S(2)}, u32[]{:S(2)}) collective-permute-start(f32[2,16,512]{2,1,0:T(8,128)S(1)} %get-tuple-element.70), channel_id=1, source_target_pairs={{0,7},{1,2},{2,1},{3,4},{4,3},{5,6},{6,5},{7,0},{8,15},{9,10},{10,... | collective-permute-start | bytes 196616 | tf_op jit(solution)/shard_map/ppermute | solution.py:541
  82.3 3.6 %collective-permute-start.15 = (f32[2,16,512]{2,1,0:T(8,128)S(1)}, f32[2,16,512]{2,1,0:T(8,128)S(1)}, u32[]{:S(2)}, u32[]{:S(2)}) collective-permute-start(f32[2,16,512]{2,1,0:T(8,128)S(1)} %get-tuple-element.71), channel_id=1, source_target_pairs={{0,1},{1,0},{2,3},{3,2},{4,5},{5,4},{6,7},{7,6},{8,9},{9,8},{10,11... | collective-permute-start | bytes 196616 | tf_op jit(solution)/shard_map/ppermute | solution.py:541

commit v3 on v2

v3 whole, which is shorter than its diff:
```python
import functools

import jax
import jax.numpy as jnp
from jax import lax
from jax.experimental import pallas as pl
from jax.experimental.pallas import tpu as pltpu
from jax.sharding import PartitionSpec as P

STEPS = 4
KAPPA = 0.5
BETA = 0.3
TERMS = STEPS + 1
LINES = 8
META = TERMS
MIB = 1 << 20
VMEM = pltpu.VMEM
SMEM = pltpu.SMEM
HBM = pltpu.HBM
UNROLL = 10


def in_hbm(*arrays):
    return [pltpu.with_memory_space_constraint(array, HBM) for array in arrays]


def params(mib):
    return pltpu.CompilerParams(vmem_limit_bytes=mib * MIB)


def surface_kernel(maps_hbm, patch_hbm, material_hbm, layer_hbm, out, maps, patch_ref, material_ref, layer, vectors, scalars, sems):
    mats, _, depth = maps.shape
    slots, _, width = layer.shape
    chunks = sems.shape[0] - 3
    block = slots // chunks
    small = [
        pltpu.make_async_copy(maps_hbm, maps, sems.at[chunks]),
        pltpu.make_async_copy(patch_hbm, patch_ref, sems.at[chunks + 1]),
        pltpu.make_async_copy(material_hbm, material_ref, sems.at[chunks + 2]),
    ]
    large = [
        pltpu.make_async_copy(
            layer_hbm.at[pl.ds(i * block, block)], layer.at[pl.ds(i * block, block)], sems.at[i]
        )
        for i in range(chunks)
    ]
    for copy in small + large:
        copy.start()

    lane = lax.broadcasted_iota(jnp.int32, (1, width), 1)
    first = lax.broadcasted_iota(jnp.int32, (depth, 1), 0) == 0
    small[0].wait()
    matrices = [maps[mat] for mat in range(mats)]
    turned = [matrix.T for matrix in matrices]
    rows = [matrix[0:1, :] for matrix in matrices]
    cols = [matrix[:, 0:1] for matrix in turned]
    kept = [jnp.zeros((1, width), jnp.float32)] * mats
    for n in range(TERMS):
        for mat in range(mats):
            if n > 0:
                rows[mat], cols[mat] = (
                    jnp.sum(matrices[mat] * cols[mat], axis=0, keepdims=True),
                    jnp.sum(turned[mat] * rows[mat], axis=1, keepdims=True),
                )
            scaled = jnp.where(first, (1.0 - KAPPA) * cols[mat], cols[mat])
            vectors[mat, n] = jnp.broadcast_to(scaled, (depth, width))
            kept[mat] = jnp.where(lane == n + 1, cols[mat][0:1, 0:1], kept[mat])
    for mat in range(mats):
        scalars[mat] = jnp.broadcast_to(kept[mat], (8, width))
    small[1].wait()
    small[2].wait()

    def one(j, carry):
        patch = patch_ref[j]
        mat = material_ref[patch]
        sums = [jnp.zeros((8, width), jnp.float32)] * TERMS
        for c in range(depth // 8):
            part = layer[j, pl.ds(8 * c, 8), :]
            sums = [
                s + vectors[mat, n, pl.ds(8 * c, 8), :] * part for n, s in enumerate(sums)
            ]
        rows = [jnp.sum(s, axis=0, keepdims=True) for s in sums]
        scalar_row = jnp.where(lane == 0, patch.astype(jnp.float32), scalars[mat][0:1, :])
        rows.append(scalar_row)
        rows.extend([jnp.zeros((1, width), jnp.float32)] * (LINES - len(rows)))
        out[j] = jnp.concatenate(rows, axis=0)
        return carry

    for i in range(chunks):
        large[i].wait()
        lax.fori_loop(i * block, (i + 1) * block, one, 0, unroll=4)


def surface_rows(layer_maps, slot_patch, patch_material, layer_state):
    slots, depth, width = layer_state.shape
    mats = layer_maps.shape[0]
    chunks = 4
    return pl.pallas_call(
        surface_kernel,
        in_specs=[pl.BlockSpec(memory_space=HBM)] * 4,
        out_specs=pl.BlockSpec(memory_space=VMEM),
        out_shape=jax.ShapeDtypeStruct((slots, LINES, width), jnp.float32),
        scratch_shapes=[
            pltpu.VMEM((mats, depth, depth), jnp.float32),
            pltpu.SMEM(slot_patch.shape, jnp.int32),
            pltpu.SMEM(patch_material.shape, jnp.int32),
            pltpu.VMEM((slots, depth, width), jnp.float32),
            pltpu.VMEM((mats, TERMS, depth, width), jnp.float32),
            pltpu.VMEM((mats, 8, width), jnp.float32),
            pltpu.SemaphoreType.DMA((chunks + 3,)),
        ],
        compiler_params=params(24),
        name="surface_rows",
    )(*in_hbm(layer_maps, slot_patch, patch_material, layer_state))


def place(index, cells_x, parts):
    low, middle = parts.bit_length() - 1, cells_x.bit_length() - 1
    return (
        jnp.right_shift(index, low + middle),
        jnp.bitwise_and(jnp.right_shift(index, low), cells_x - 1),
        jnp.bitwise_and(index, parts - 1),
    )


def pick(rows_ref, fields, picked, tiles):
    cells_x = fields[0].shape[1]
    slots, width = picked.shape[1:]
    parts = fields[0].shape[2] // width

    def fetch(k, carry):
        z, x, part = place(jnp.maximum(rows_ref[k], 0), cells_x, parts)
        lines = pl.ds(pl.multiple_of(jnp.bitwise_and(x, -8), 8), 8)
        lanes = pl.ds(pl.multiple_of(part * width, width), width)
        for side, field in enumerate(fields):
            tiles[side, pl.ds(pl.multiple_of(8 * k, 8), 8), :] = field[z, lines, lanes]
        return carry

    lax.fori_loop(0, slots, fetch, 0, unroll=8)

    def choose(k, carry):
        index = rows_ref[k]
        line = 8 * k + jnp.bitwise_and(place(jnp.maximum(index, 0), cells_x, parts)[1], 7)
        for side in range(len(fields)):
            row = tiles[side, pl.ds(line, 1), :]
            picked[side, pl.ds(k, 1), :] = jnp.where(index >= 0, row, 0.0)
        return carry

    lax.fori_loop(0, slots, choose, 0, unroll=8)


def even(axis):
    return lax.axis_index(axis) % 2 == 0


def at_start(axis):
    return lax.axis_index(axis) == 0


def at_end(axis):
    return lax.axis_index(axis) == lax.axis_size(axis) - 1


def outgoing(axis, low, high):
    choice = even(axis)
    return jnp.where(choice, low, high), jnp.where(choice, high, low)


def incoming(axis, outer, inner):
    choice = even(axis)
    before = jnp.where(at_start(axis), 0.0, jnp.where(choice, outer, inner))
    after = jnp.where(at_end(axis), 0.0, jnp.where(choice, inner, outer))
    return before, after


def keep_sides(cells, side, z, x_outer, x_inner):
    last_x, width = cells.shape[0] - 1, x_outer.shape[3]
    for part in range(x_outer.shape[1]):
        lanes = slice(part * width, (part + 1) * width)
        x_outer[side, part, pl.ds(z, 1), :], x_inner[side, part, pl.ds(z, 1), :] = outgoing(
            "gx", cells[0:1, lanes], cells[last_x : last_x + 1, lanes]
        )


def side_row(plane, side, z):
    parts = plane.shape[1]
    return jnp.concatenate([plane[side, part, pl.ds(z, 1), :] for part in range(parts)], axis=1)


def keep_edges(z_planes, side, z_outer, z_inner):
    z_outer[side], z_inner[side] = outgoing("gz", *z_planes)


def edges_kernel(field_hbm, adjoint_hbm, x_outer, x_inner, z_outer, z_inner, field, adjoint, sems):
    copies = [
        pltpu.make_async_copy(field_hbm, field, sems.at[0]),
        pltpu.make_async_copy(adjoint_hbm, adjoint, sems.at[1]),
    ]
    for copy in copies:
        copy.start()
    for side, array in enumerate((field, adjoint)):
        copies[side].wait()

        def one(z, carry):
            keep_sides(array[z], side, z, x_outer, x_inner)
            return carry

        lax.fori_loop(0, array.shape[0], one, 0, unroll=8)
        keep_edges((array[0], array[array.shape[0] - 1]), side, z_outer, z_inner)


def edge_shapes(field, width):
    cells_z, cells_x, along = field.shape
    f32 = jnp.float32
    x_shape = jax.ShapeDtypeStruct((2, along // width, cells_z, width), f32)
    z_shape = jax.ShapeDtypeStruct((2, cells_x, along), f32)
    return [x_shape, x_shape, z_shape, z_shape]


def first_edges(field, adjoint, width):
    return pl.pallas_call(
        edges_kernel,
        in_specs=[pl.BlockSpec(memory_space=HBM)] * 2,
        out_specs=[pl.BlockSpec(memory_space=VMEM)] * 4,
        out_shape=edge_shapes(field, width),
        scratch_shapes=[
            pltpu.VMEM(field.shape, jnp.float32),
            pltpu.VMEM(field.shape, jnp.float32),
            pltpu.SemaphoreType.DMA((2,)),
        ],
        compiler_params=params(8),
        name="edges",
    )(*in_hbm(field, adjoint))


def couple(rows_ref, change, coupling):
    parts, cells_z, cells_x = coupling.shape[0] // 2, coupling.shape[1] - 1, coupling.shape[2]

    def put(k, carry):
        index = rows_ref[k]
        z, x, part = place(jnp.maximum(index, 0), cells_x, parts)
        z = jnp.where(index >= 0, z, cells_z)
        for side in range(2):
            coupling[side * parts + part, z, pl.ds(x, 1), :] = change[side, pl.ds(k, 1), :]
        return carry

    lax.fori_loop(0, change.shape[1], put, 0, unroll=8)


def local_planes(fields, befores, outs, speed2, extra, sends=None):
    cells_z = speed2.shape[0]

    def plane(z, below, above):
        speed = speed2[z]
        for side in range(2):
            now = fields[side]
            beside = below(now) + above(now)
            outs[side][z] = stencil(now[z], befores[side][z], speed, beside, extra(side, z))

    def inner(z, carry):
        plane(z, lambda now: now[z - 1], lambda now: now[z + 1])
        return carry

    plane(0, lambda now: 0.0, lambda now: now[1])
    plane(cells_z - 1, lambda now: now[cells_z - 2], lambda now: 0.0)
    shares = len(sends) if sends else 1
    share = cells_z // shares
    for i in range(shares):
        start, stop = max(i * share, 1), min((i + 1) * share, cells_z - 1)
        lax.fori_loop(start, stop, inner, 0, unroll=(stop - start) // -(-(stop - start) // UNROLL))
        for send in sends[i] if sends else ():
            send.start()


def stencil(cells, before, speed, beside, extra):
    cells_x, along = cells.shape
    row_id = lax.broadcasted_iota(jnp.int32, cells.shape, 0)
    lane_id = lax.broadcasted_iota(jnp.int32, cells.shape, 1)
    beside = beside + jnp.where(row_id == 0, 0.0, pltpu.roll(cells, 1, axis=0))
    beside = beside + jnp.where(row_id == cells_x - 1, 0.0, pltpu.roll(cells, cells_x - 1, axis=0))
    beside = beside + jnp.where(lane_id == 0, 0.0, pltpu.roll(cells, 1, axis=1))
    beside = beside + jnp.where(lane_id == along - 1, 0.0, pltpu.roll(cells, along - 1, axis=1))
    return 2.0 * cells - before + speed * (beside - 6.0 * cells) + extra


def shares_of(source, target, sems, first, count):
    share = source.shape[0] // count
    return [
        pltpu.make_async_copy(
            source.at[pl.ds(i * share, share)], target.at[pl.ds(i * share, share)], sems.at[first + i]
        )
        for i in range(count)
    ]


class Lines:
    def __init__(self, ref, slots):
        self.ref, self.slots = ref, slots
        self.meta = self.row(META + 1)

    def row(self, n):
        return self.ref[pl.ds(n - 1, self.slots, stride=LINES), :]

    def scalar(self, n):
        return self.meta[:, n : n + 1]

    def surface(self, step, pushes, side):
        new = self.row(step + 1) if side == 0 else None
        for t in range(step + 1):
            term = self.scalar(step + 1 - t) * pushes[t][side]
            new = term if new is None else new + term
        return new


def extra_of(coupling, side, z):
    parts = coupling.shape[0] // 2
    return jnp.concatenate([coupling[side * parts + part, z] for part in range(parts)], axis=1)


def couple_step(rows_ref, lines, step, pushes, picked, surface, change, coupling):
    for side in range(2):
        surface[side] = lines.surface(step, pushes, side)
        change[side] = BETA * (surface[side] - picked[side])
    couple(rows_ref, change, coupling)


def x_added(speed_first, speed_last, from_outer, from_inner, side, z, shape):
    row_id = lax.broadcasted_iota(jnp.int32, shape, 0)
    low, high = incoming("gx", side_row(from_outer, side, z), side_row(from_inner, side, z))
    low, high = speed_first * low, speed_last * high
    return jnp.where(row_id == 0, low, jnp.where(row_id == shape[0] - 1, high, 0.0))


def border_planes(partials, speed2, halos, outs, edges, extra):
    x_from_outer, x_from_inner, z_from_outer, z_from_inner = halos
    x_outer, x_inner, z_outer, z_inner = edges
    cells_z, cells_x, along = speed2.shape

    def plane(z, side, more):
        first, last = speed2[z, 0:1, :], speed2[z, cells_x - 1 : cells_x, :]
        new = partials[side][z] + x_added(
            first, last, x_from_outer, x_from_inner, side, z, (cells_x, along)
        )
        if extra is not None:
            new = new + extra(side, z)
        if more is not None:
            new = new + speed2[z] * more
        outs[side][z] = new
        keep_sides(new, side, z, x_outer, x_inner)
        return new

    for side in range(2):
        before, after = incoming("gz", z_from_outer[side], z_from_inner[side])
        ends = plane(0, side, before), plane(cells_z - 1, side, after)
        keep_edges(ends, side, z_outer, z_inner)

    def inner(z, carry):
        for side in range(2):
            plane(z, side, None)
        return carry

    lax.fori_loop(1, cells_z - 1, inner, 0, unroll=UNROLL)


def first_local_kernel(rows_hbm, field_hbm, field_prev_hbm, adjoint_hbm, adjoint_prev_hbm, speed2_hbm, out_hbm, adjoint_out_hbm, push, picked, rows_ref, field, field_prev, adjoint, adjoint_prev, speed2, out, adjoint_out, tiles, sems):
    loads = [
        pltpu.make_async_copy(source, target, sems.at[i])
        for i, (source, target) in enumerate(
            (
                (rows_hbm, rows_ref),
                (field_hbm, field),
                (adjoint_hbm, adjoint),
                (speed2_hbm, speed2),
                (field_prev_hbm, field_prev),
                (adjoint_prev_hbm, adjoint_prev),
            )
        )
    ]
    for copy in loads:
        copy.start()
    for copy in loads[:3]:
        copy.wait()
    pick(rows_ref, (field, adjoint), picked, tiles)
    push[...] = KAPPA * picked[...]
    for copy in loads[3:]:
        copy.wait()
    sends = list(
        zip(
            shares_of(out, out_hbm, sems, 6, 4), shares_of(adjoint_out, adjoint_out_hbm, sems, 10, 4)
        )
    )
    local_planes(
        (field, adjoint),
        (field_prev, adjoint_prev),
        (out, adjoint_out),
        speed2,
        lambda side, z: 0.0,
        sends,
    )
    for pair in sends:
        for send in pair:
            send.wait()


def first_local(rows, field, field_prev, adjoint, adjoint_prev, speed2, slots, width):
    rows_shape = jax.ShapeDtypeStruct((2, slots, width), jnp.float32)
    return pl.pallas_call(
        first_local_kernel,
        in_specs=[pl.BlockSpec(memory_space=HBM)] * 6,
        out_specs=[pl.BlockSpec(memory_space=HBM)] * 2 + [pl.BlockSpec(memory_space=VMEM)] * 2,
        out_shape=[HBM(field.shape, jnp.float32)] * 2 + [rows_shape] * 2,
        scratch_shapes=[pltpu.SMEM((slots,), jnp.int32)]
        + [pltpu.VMEM(field.shape, jnp.float32)] * 7
        + [pltpu.VMEM((2, 8 * slots, width), jnp.float32), pltpu.SemaphoreType.DMA((14,))],
        compiler_params=params(16),
        cost_estimate=pl.CostEstimate(flops=8 << 20, bytes_accessed=12 << 20, transcendentals=0),
        name="local0",
    )(*in_hbm(rows, field, field_prev, adjoint, adjoint_prev, speed2))


def first_border_kernel(rows_ref, partial_hbm, partial_adjoint_hbm, field_hbm, adjoint_hbm, speed2_hbm, x_from_outer, x_from_inner, z_from_outer, z_from_inner, lines_ref, push, picked, out, adjoint_out, field, adjoint, speed2, x_outer, x_inner, z_outer, z_inner, surface, partial, partial_adjoint, coupling, change, sems):
    loads = [
        pltpu.make_async_copy(source, target, sems.at[i])
        for i, (source, target) in enumerate(
            (
                (speed2_hbm, speed2),
                (partial_hbm, partial),
                (partial_adjoint_hbm, partial_adjoint),
                (field_hbm, field),
                (adjoint_hbm, adjoint),
            )
        )
    ]
    for copy in loads:
        copy.start()
    coupling[...] = jnp.zeros_like(coupling)
    lines = Lines(lines_ref, change.shape[1])
    couple_step(rows_ref, lines, 0, [push], picked, surface, change, coupling)
    for copy in loads[:3]:
        copy.wait()
    border_planes(
        (partial, partial_adjoint),
        speed2,
        (x_from_outer, x_from_inner, z_from_outer, z_from_inner),
        (out, adjoint_out),
        (x_outer, x_inner, z_outer, z_inner),
        functools.partial(extra_of, coupling),
    )
    for copy in loads[3:]:
        copy.wait()


def coupling_scratch(field, slots, width):
    cells_z, cells_x, along = field.shape
    return [
        pltpu.VMEM((2 * (along // width), cells_z + 1, cells_x, width), jnp.float32),
        pltpu.VMEM((2, slots, width), jnp.float32),
    ]


def first_border(rows, partials, field, adjoint, speed2, halos, lines, push, picked):
    _, slots, width = push.shape
    whole = jax.ShapeDtypeStruct(field.shape, jnp.float32)
    in_vmem = pl.BlockSpec(memory_space=VMEM)
    return pl.pallas_call(
        first_border_kernel,
        in_specs=[pl.BlockSpec(memory_space=SMEM)]
        + [pl.BlockSpec(memory_space=HBM)] * 5
        + [in_vmem] * 7,
        out_specs=[in_vmem] * 10,
        out_shape=[whole] * 5
        + edge_shapes(field, width)
        + [jax.ShapeDtypeStruct((2, slots, width), jnp.float32)],
        scratch_shapes=[pltpu.VMEM(field.shape, jnp.float32)] * 2
        + coupling_scratch(field, slots, width)
        + [pltpu.SemaphoreType.DMA((5,))],
        compiler_params=params(12),
        name="border0",
    )(rows, *in_hbm(*partials, field, adjoint, speed2), *halos, lines, push, picked)


def local_kernel(step, rows_ref, field, field_prev, adjoint, adjoint_prev, speed2, lines_ref, surface, *refs):
    pushes, refs = list(refs[:step]), refs[step:]
    out, adjoint_out, push, next_surface, coupling, change, tiles, picked = refs
    pick(rows_ref, (field, adjoint), picked, tiles)
    push[...] = KAPPA * (picked[...] - surface[...])
    coupling[...] = jnp.zeros_like(coupling)
    lines = Lines(lines_ref, change.shape[1])
    couple_step(rows_ref, lines, step, pushes + [push], picked, next_surface, change, coupling)
    local_planes(
        (field, adjoint),
        (field_prev, adjoint_prev),
        (out, adjoint_out),
        speed2,
        functools.partial(extra_of, coupling),
    )


def local_step(step, rows, field, field_prev, adjoint, adjoint_prev, speed2, lines, surface, pushes):
    _, slots, width = surface.shape
    whole = jax.ShapeDtypeStruct(field.shape, jnp.float32)
    rows_shape = jax.ShapeDtypeStruct(surface.shape, jnp.float32)
    in_vmem = pl.BlockSpec(memory_space=VMEM)
    return pl.pallas_call(
        functools.partial(local_kernel, step),
        in_specs=[pl.BlockSpec(memory_space=SMEM)] + [in_vmem] * (7 + step),
        out_specs=[in_vmem] * 4,
        out_shape=[whole, whole, rows_shape, rows_shape],
        scratch_shapes=coupling_scratch(field, slots, width)
        + [
            pltpu.VMEM((2, 8 * slots, width), jnp.float32),
            pltpu.VMEM((2, slots, width), jnp.float32),
        ],
        compiler_params=params(8),
        cost_estimate=pl.CostEstimate(flops=8 << 20, bytes_accessed=12 << 20, transcendentals=0),
        name=f"local{step}",
    )(rows, field, field_prev, adjoint, adjoint_prev, speed2, lines, surface, *pushes)


def border_kernel(partial, partial_adjoint, speed2, x_from_outer, x_from_inner, z_from_outer, z_from_inner, out, adjoint_out, *edges):
    border_planes(
        (partial, partial_adjoint),
        speed2,
        (x_from_outer, x_from_inner, z_from_outer, z_from_inner),
        (out, adjoint_out),
        edges,
        None,
    )


def border_step(step, partials, speed2, halos, width):
    field = partials[0]
    whole = jax.ShapeDtypeStruct(field.shape, jnp.float32)
    in_vmem = pl.BlockSpec(memory_space=VMEM)
    return pl.pallas_call(
        border_kernel,
        in_specs=[in_vmem] * 7,
        out_specs=[in_vmem] * 6,
        out_shape=[whole, whole] + edge_shapes(field, width),
        compiler_params=params(8),
        name=f"border{step}",
    )(*partials, speed2, *halos)


def ahead_kernel(rows_ref, partial, partial_adjoint, field_prev, adjoint_prev, speed2, x_from_outer, x_from_inner, z_from_outer, z_from_inner, lines_ref, surface, *refs):
    pushes, refs = list(refs[: STEPS - 1]), refs[STEPS - 1 :]
    x_outer, x_inner, z_outer, z_inner, speed_first, speed_last, speed_ends, gradient = refs[:8]
    next_hbm, next_adjoint_hbm, coupling, change, tiles, picked, push, next_surface = refs[8:16]
    field, adjoint, out, adjoint_out, sems = refs[16:]
    cells_z, cells_x, _ = speed2.shape
    coupling[...] = jnp.zeros_like(coupling)
    border_planes(
        (partial, partial_adjoint),
        speed2,
        (x_from_outer, x_from_inner, z_from_outer, z_from_inner),
        (field, adjoint),
        (x_outer, x_inner, z_outer, z_inner),
        None,
    )
    speed_ends[0], speed_ends[1] = speed2[0], speed2[cells_z - 1]

    def sides(z, carry):
        keep_side(speed2[z], z, speed_first, speed_last)
        return carry

    lax.fori_loop(0, cells_z, sides, 0, unroll=8)
    pick(rows_ref, (field, adjoint), picked, tiles)
    push[...] = KAPPA * (picked[...] - surface[...])

    slots = change.shape[1]
    lines = Lines(lines_ref, slots)
    known = pushes + [push]
    total = jnp.zeros(change.shape[1:], jnp.float32)
    for late in range(STEPS):
        inside = (STEPS - late) * lines.row(TERMS - late)
        for t in range(STEPS - late):
            scale = (STEPS - late - t) * lines.scalar(TERMS - late - t)
            inside = inside + scale * known[t][0]
        total = total + known[late][1] * inside
    ids = lines.scalar(0).astype(jnp.int32)
    owners = lax.broadcasted_iota(jnp.int32, (slots, gradient.shape[0]), 1) == ids
    gradient[...] = lax.dot_general(
        owners.astype(jnp.float32),
        total,
        (((0,), (0,)), ((), ())),
        precision=lax.Precision.HIGHEST,
        preferred_element_type=jnp.float32,
    )

    couple_step(rows_ref, lines, STEPS - 1, known, picked, next_surface, change, coupling)
    sends = list(
        zip(shares_of(out, next_hbm, sems, 0, 4), shares_of(adjoint_out, next_adjoint_hbm, sems, 4, 4))
    )
    local_planes(
        (field, adjoint),
        (field_prev, adjoint_prev),
        (out, adjoint_out),
        speed2,
        functools.partial(extra_of, coupling),
        sends,
    )
    for pair in sends:
        for send in pair:
            send.wait()


def ahead_step(rows, partials, field_prev, adjoint_prev, speed2, halos, lines, surface, pushes, patches):
    _, slots, width = surface.shape
    cells_z, cells_x, along = field_prev.shape
    in_vmem = pl.BlockSpec(memory_space=VMEM)
    f32 = jnp.float32
    sides = jax.ShapeDtypeStruct((along // width, cells_z, width), f32)
    return pl.pallas_call(
        ahead_kernel,
        in_specs=[pl.BlockSpec(memory_space=SMEM)] + [in_vmem] * (11 + len(pushes)),
        out_specs=[in_vmem] * 8 + [pl.BlockSpec(memory_space=HBM)] * 2,
        out_shape=edge_shapes(field_prev, width)
        + [sides, sides, jax.ShapeDtypeStruct((2, cells_x, along), f32)]
        + [jax.ShapeDtypeStruct((patches, width), f32)]
        + [HBM(field_prev.shape, f32)] * 2,
        scratch_shapes=coupling_scratch(field_prev, slots, width)
        + [pltpu.VMEM((2, 8 * slots, width), f32)]
        + [pltpu.VMEM((2, slots, width), f32)] * 3
        + [pltpu.VMEM(field_prev.shape, f32)] * 4
        + [pltpu.SemaphoreType.DMA((8,))],
        compiler_params=params(16),
        name="ahead",
    )(rows, *partials, field_prev, adjoint_prev, speed2, *halos, lines, surface, *pushes)


def keep_side(cells, z, first, last):
    last_x, width = cells.shape[0] - 1, first.shape[2]
    for part in range(first.shape[0]):
        lanes = slice(part * width, (part + 1) * width)
        first[part, pl.ds(z, 1), :] = cells[0:1, lanes]
        last[part, pl.ds(z, 1), :] = cells[last_x : last_x + 1, lanes]


def finish_kernel(field_hbm, adjoint_hbm, speed_first, speed_last, speed_ends, x_from_outer, x_from_inner, z_from_outer, z_from_inner, out_hbm, adjoint_out_hbm, field, adjoint, sems):
    cells_z, cells_x, along = field.shape
    parts = speed_first.shape[0]
    shares = 4
    share = cells_z // shares
    loads, sends = [], []
    for side, (source, held, target) in enumerate(
        ((field_hbm, field, out_hbm), (adjoint_hbm, adjoint, adjoint_out_hbm))
    ):
        loads.append(shares_of(source, held, sems, 2 * side * shares, shares))
        sends.append(shares_of(held, target, sems, (2 * side + 1) * shares, shares))
    for i in range(shares):
        for side in range(2):
            loads[side][i].start()
    for i in range(shares):
        for side, held in enumerate((field, adjoint)):
            loads[side][i].wait()

            def one(z, carry):
                first, last = (
                    jnp.concatenate([ref[p, pl.ds(z, 1), :] for p in range(parts)], axis=1)
                    for ref in (speed_first, speed_last)
                )
                held[z] = held[z] + x_added(
                    first, last, x_from_outer, x_from_inner, side, z, (cells_x, along)
                )
                return carry

            lax.fori_loop(i * share, (i + 1) * share, one, 0, unroll=share)
            before, after = incoming("gz", z_from_outer[side], z_from_inner[side])
            if i == 0:
                held[0] = held[0] + speed_ends[0] * before
            if i == shares - 1:
                held[cells_z - 1] = held[cells_z - 1] + speed_ends[1] * after
            sends[side][i].start()
    for side in range(2):
        for send in sends[side]:
            send.wait()


def finish_call(field, adjoint, speed_first, speed_last, speed_ends, halos):
    return pl.pallas_call(
        finish_kernel,
        in_specs=[pl.BlockSpec(memory_space=HBM)] * 2 + [pl.BlockSpec(memory_space=VMEM)] * 7,
        out_specs=[pl.BlockSpec(memory_space=HBM)] * 2,
        out_shape=[HBM(field.shape, jnp.float32)] * 2,
        scratch_shapes=[pltpu.VMEM(field.shape, jnp.float32)] * 2 + [pltpu.SemaphoreType.DMA((16,))],
        compiler_params=params(8),
        name="finish",
    )(*in_hbm(field, adjoint), speed_first, speed_last, speed_ends, *halos)


def swaps(axis, first):
    count = lax.axis_size(axis)
    if first:
        return [(i, i ^ 1) for i in range(count)]
    return [(i, (i + 1 if i % 2 else i - 1) % count) for i in range(count)]


def exchange(edges):
    axes = (("gx", False), ("gx", True), ("gz", False), ("gz", True))
    return [lax.ppermute(edge, axis, swaps(axis, first)) for edge, (axis, first) in zip(edges, axes)]


def body(
    pressure_now,
    pressure_prev,
    adjoint_now,
    adjoint_prev,
    speed2,
    layer_state,
    layer_maps,
    send_rows,
    slot_patch,
    patch_material,
):
    slots, _, width = layer_state.shape
    patches = patch_material.shape[0]
    devices = lax.axis_size(("gx", "gz"))
    rows = send_rows.reshape(-1)

    lines = surface_rows(layer_maps, slot_patch, patch_material, layer_state)
    lines = lax.all_to_all(lines, ("gx", "gz"), split_axis=0, concat_axis=0, tiled=True)
    lines = lines.reshape(slots * LINES, width)

    halos = exchange(first_edges(pressure_now, adjoint_now, width))
    *partials, push, picked = first_local(
        rows, pressure_now, pressure_prev, adjoint_now, adjoint_prev, speed2, slots, width
    )
    pushes = [push]
    results = first_border(
        rows, partials, pressure_now, adjoint_now, speed2, halos, lines, push, picked
    )
    field, adjoint, field_prev, adjoint_prev, speed = results[:5]
    edges, surface = results[5:9], results[9]
    for step in range(1, STEPS - 1):
        halos = exchange(edges)
        *partials, push, surface = local_step(
            step, rows, field, field_prev, adjoint, adjoint_prev, speed, lines, surface, pushes
        )
        pushes.append(push)
        field_prev, adjoint_prev = field, adjoint
        if step < STEPS - 2:
            field, adjoint, *edges = border_step(step, partials, speed, halos, width)
    results = ahead_step(
        rows, partials, field_prev, adjoint_prev, speed, halos, lines, surface, pushes, patches
    )
    edges, speeds, gradient, partials = results[:4], results[4:7], results[7], results[8:]
    parts = gradient.reshape(devices, patches // devices, width)
    parts = lax.all_to_all(parts, ("gx", "gz"), split_axis=0, concat_axis=0, tiled=True)
    halos = exchange(edges)
    field, adjoint = finish_call(*partials, *speeds, halos)
    return field, adjoint, jnp.sum(parts, axis=0)


def solution(mesh):
    grid = P("gz", "gx", None)
    split = P(("gx", "gz"), None, None)
    in_specs = (grid, grid, grid, grid, grid, split, P(), split, P(("gx", "gz")), P())
    out_specs = (grid, grid, P(("gx", "gz"), None))
    return jax.shard_map(body, mesh=mesh, in_specs=in_specs, out_specs=out_specs, check_vma=False)
```

time: 94 us -> 84.5 us (0.90)
  starting transfers between devices: 48.8 us -> 43.1 us
  waiting for transfers between devices: 11.2 us -> 6.23 us
  Pallas kernels: 32.2 us -> 33.4 us
    ppermute x16, starting transfers between devices: 28.8 us -> 24 us  [exchange(): lax.ppermute(edge, axis, swaps(axis, first))]
    ppermute x16, waiting for transfers between devices: 10.8 us -> 6.23 us  [exchange(): lax.ppermute(edge, axis, swaps(axis, first))]
    pallas_call x4 -> x7, Pallas kernels: 24.6 us -> 26.9 us  [the longest x2 8.27 us: local_step(): pl.pallas_call(functools.partial(local_kernel, step), in_specs=[pl.BlockS...]
    pallas_call x1, Pallas kernels: 2.83 us -> 1.69 us  [first_edges(): pl.pallas_call(edges_kernel, in_specs=[pl.BlockSpec(memory_space=HBM)] *...]
  transfers between devices with their start and end apart: 18 -> 18, of which waited for: 9 -> 3; matrix products, arithmetic and copies ran while one was open for 0% -> 0% of each run, Pallas kernels for 7% -> 21%
where the time goes in v3:
time: 84.5 us; the launch traced here: 84.3 us
  starting transfers between devices  43.1 us (51%)
  Pallas kernels  33.4 us (40%)
  waiting for transfers between devices  6.23 us (7%)
    ppermute x16, starting transfers between devices, exchange(): lax.ppermute(edge, axis, swaps(axis, first))  24 us
    all_to_all x1, starting transfers between devices, body(): lax.all_to_all(lines, ('gx', 'gz'), split_axis=0, concat_axis=0, tiled=True)  11.5 us
    pallas_call x2, Pallas kernels, local_step(): pl.pallas_call(functools.partial(local_kernel, step), in_specs=[pl.BlockS...  8.27 us
    all_to_all x1, starting transfers between devices, body(): lax.all_to_all(parts, ('gx', 'gz'), split_axis=0, concat_axis=0, tiled=True)  7.56 us
    pallas_call x1, Pallas kernels, ahead_step(): pl.pallas_call(ahead_kernel, in_specs=[pl.BlockSpec(memory_space=SMEM)] +...  7.23 us
    ppermute x16, waiting for transfers between devices, exchange(): lax.ppermute(edge, axis, swaps(axis, first))  6.23 us
    pallas_call x1, Pallas kernels, first_local(): pl.pallas_call(first_local_kernel, in_specs=[pl.BlockSpec(memory_space=HB...  4.87 us
    pallas_call x1, Pallas kernels, surface_rows(): pl.pallas_call(surface_kernel, in_specs=[pl.BlockSpec(memory_space=HBM)]...  4.84 us
  transfers between devices with their start and end apart: 18, of which 3 were waited for; matrix products, arithmetic and copies ran while one was open for 0% of the time, Pallas kernels for 21%

profile of v3, /device:TPU:1, one launch (start us, length us, event | category | flops | bytes accessed | tf_op | source)
XLA Modules:
  0.0 84.3 jit_solution(13250488157852192460)
XLA Ops:
  0.6 4.8 %surface_rows.1 = f32[128,8,128]{2,1,0:T(8,128)} custom-call(f32[8,64,64]{2,1,0:T(8,128)} %maps_hbm.1, s32[128]{0:T(128)} %patch_hbm.1, s32[1024]{0:T(1024)} %material_hbm.1, f32[128,64,128]{2,1,0:T(8,128)} %layer_hbm.1), custom_call_target="tpu_custom_call" | custom-call | tf_op jit(solution)/shard_map/surface_rows/pallas_call | solution.py:98
  5.5 11.5 %all-to-all-start = ((f32[128,8,128]{2,1,0:T(8,128)}), f32[128,8,128]{2,1,0:T(8,128)S(1)}, u32[]{:S(2)}, u32[]{:S(2)}) async-start(f32[128,8,128]{2,1,0:T(8,128)} %surface_rows.1), calls=%async_computation | async-start | bytes 1048576 | tf_op jit(solution)/shard_map/all_to_all | solution.py:721
  17.0 1.7 %edges.1 = (f32[2,4,32,128]{3,2,1,0:T(8,128)S(1)}, f32[2,4,32,128]{3,2,1,0:T(8,128)S(1)}, f32[2,16,512]{2,1,0:T(8,128)S(1)}, f32[2,16,512]{2,1,0:T(8,128)S(1)}) custom-call(f32[32,16,512]{2,1,0:T(8,128)} %field_hbm.5, f32[32,16,512]{2,1,0:T(8,128)} %adjoint_hbm.5), custom_call_target="tpu_custom_call" | custom-call | tf_op jit(solution)/shard_map/edges/pallas_call | solution.py:221
  18.7 4.9 %collective-permute-start = (f32[2,4,32,128]{3,2,1,0:T(8,128)S(1)}, f32[2,4,32,128]{3,2,1,0:T(8,128)S(1)}, u32[]{:S(2)}, u32[]{:S(2)}) collective-permute-start(f32[2,4,32,128]{3,2,1,0:T(8,128)S(1)} %get-tuple-element.49), channel_id=1, source_target_pairs={{0,120},{8,16},{16,8},{24,32},{32,24},{40,48},{48,40},{56,64},{64,... | collective-permute-start | bytes 393224 | tf_op jit(solution)/shard_map/ppermute | solution.py:700
  23.6 2.0 %collective-permute-start.2 = (f32[2,16,512]{2,1,0:T(8,128)S(1)}, f32[2,16,512]{2,1,0:T(8,128)S(1)}, u32[]{:S(2)}, u32[]{:S(2)}) collective-permute-start(f32[2,16,512]{2,1,0:T(8,128)S(1)} %get-tuple-element.51), channel_id=1, source_target_pairs={{0,7},{1,2},{2,1},{3,4},{4,3},{5,6},{6,5},{7,0},{8,15},{9,10},{10,... | collective-permute-start | bytes 196616 | tf_op jit(solution)/shard_map/ppermute | solution.py:700
  25.6 1.6 %collective-permute-start.3 = (f32[2,16,512]{2,1,0:T(8,128)S(1)}, f32[2,16,512]{2,1,0:T(8,128)S(1)}, u32[]{:S(2)}, u32[]{:S(2)}) collective-permute-start(f32[2,16,512]{2,1,0:T(8,128)S(1)} %get-tuple-element.52), channel_id=1, source_target_pairs={{0,1},{1,0},{2,3},{3,2},{4,5},{5,4},{6,7},{7,6},{8,9},{9,8},{10,11... | collective-permute-start | bytes 196616 | tf_op jit(solution)/shard_map/ppermute | solution.py:700
  27.2 4.9 %local0.1 = (f32[32,16,512]{2,1,0:T(8,128)}, f32[32,16,512]{2,1,0:T(8,128)}, f32[2,128,128]{2,1,0:T(8,128)S(1)}, f32[2,128,128]{2,1,0:T(8,128)S(1)}) custom-call(s32[128]{0:T(128)} %bitcast.7, f32[32,16,512]{2,1,0:T(8,128)} %field_hbm.5, f32[32,16,512]{2,1,0:T(8,128)} %field_prev_hbm.1, f32[32,16,512]{2,1,0:T(8,128)} %adjoint_hbm.5, ...), custom_call_target="tpu_custom_call" | custom-call | flops 8388608 | bytes 12582912 | tf_op jit(solution)/shard_map/local0/pallas_call | solution.py:407
  32.1 3.3 %border0.1 = (f32[32,16,512]{2,1,0:T(8,128)S(1)}, f32[32,16,512]{2,1,0:T(8,128)S(1)}, f32[32,16,512]{2,1,0:T(8,128)S(1)}, f32[32,16,512]{2,1,0:T(8,128)S(1)}, f3...) custom-call(s32[128]{0:T(128)S(1)} %bitcast.8, ...), custom_call_target="tpu_custom_call" | custom-call | tf_op jit(solution)/shard_map/border0/pallas_call | solution.py:465
  35.5 0.8 collective-permute-start.4
  36.3 0.8 collective-permute-start.5
  37.1 0.9 %collective-permute-start.6 = (f32[2,16,512]{2,1,0:T(8,128)S(1)}, f32[2,16,512]{2,1,0:T(8,128)S(1)}, u32[]{:S(2)}, u32[]{:S(2)}) collective-permute-start(f32[2,16,512]{2,1,0:T(8,128)S(1)} %get-tuple-element.65), channel_id=1, source_target_pairs={{0,7},{1,2},{2,1},{3,4},{4,3},{5,6},{6,5},{7,0},{8,15},{9,10},{10,... | collective-permute-start | bytes 196616 | tf_op jit(solution)/shard_map/ppermute | solution.py:700
  38.7 4.1 %local1.1 = (f32[32,16,512]{2,1,0:T(8,128)S(1)}, f32[32,16,512]{2,1,0:T(8,128)S(1)}, f32[2,128,128]{2,1,0:T(8,128)S(1)}, f32[2,128,128]{2,1,0:T(8,128)S(1)}) custom-call(s32[128]{0:T(128)S(1)} %bitcast.9, f32[32,16,512]{2,1,0:T(8,128)S(1)} %get-tuple-element.55.field.field_prev, f32[32,16,512]{2,1,0:T(8,128)S(1)} %get-tuple-element.56.field_prev, ...), custom_call_target="tpu_custom_call" | custom-call | flops 8388608 | bytes 12582912 | tf_op jit(solution)/shard_map/local1/pallas_call | solution.py:504
  42.8 1.2 %collective-permute-done.4.x_from_outer = f32[2,4,32,128]{3,2,1,0:T(8,128)S(1)} collective-permute-done((f32[2,4,32,128]{3,2,1,0:T(8,128)S(1)}, f32[2,4,32,128]{3,2,1,0:T(8,128)S(1)}, u32[]{:S(2)}, u32[]{:S(2)}) %collective-permute-start.4) | collective-permute-done | bytes 131104 | tf_op jit(solution)/shard_map/ppermute | solution.py:700
  44.7 2.5 %collective-permute-start.8 = (f32[2,4,32,128]{3,2,1,0:T(8,128)S(1)}, f32[2,4,32,128]{3,2,1,0:T(8,128)S(1)}, u32[]{:S(2)}, u32[]{:S(2)}) collective-permute-start(f32[2,4,32,128]{3,2,1,0:T(8,128)S(1)} %get-tuple-element.73), channel_id=1, source_target_pairs={{0,120},{8,16},{16,8},{24,32},{32,24},{40,48},{48,40},{56,64},{64,... | collective-permute-start | bytes 393224 | tf_op jit(solution)/shard_map/ppermute | solution.py:700
  47.2 0.9 %collective-permute-start.10 = (f32[2,16,512]{2,1,0:T(8,128)S(1)}, f32[2,16,512]{2,1,0:T(8,128)S(1)}, u32[]{:S(2)}, u32[]{:S(2)}) collective-permute-start(f32[2,16,512]{2,1,0:T(8,128)S(1)} %get-tuple-element.75), channel_id=1, source_target_pairs={{0,7},{1,2},{2,1},{3,4},{4,3},{5,6},{6,5},{7,0},{8,15},{9,10},{10,... | collective-permute-start | bytes 196616 | tf_op jit(solution)/shard_map/ppermute | solution.py:700
  48.5 4.1 %local2.1 = (f32[32,16,512]{2,1,0:T(8,128)S(1)}, f32[32,16,512]{2,1,0:T(8,128)S(1)}, f32[2,128,128]{2,1,0:T(8,128)S(1)}, f32[2,128,128]{2,1,0:T(8,128)S(1)}) custom-call(s32[128]{0:T(128)S(1)} %bitcast.10, f32[32,16,512]{2,1,0:T(8,128)S(1)} %get-tuple-element.67.field.field_prev, f32[32,16,512]{2,1,0:T(8,128)S(1)} %get-tuple-element.55.field.field_prev, ...), custom_call_target="tpu_custom_call" | custom-call | flops 8388608 | bytes 12582912 | tf_op jit(solution)/shard_map/local2/pallas_call | solution.py:504
  52.7 7.2 %ahead.1 = (f32[2,4,32,128]{3,2,1,0:T(8,128)S(1)}, f32[2,4,32,128]{3,2,1,0:T(8,128)S(1)}, f32[2,16,512]{2,1,0:T(8,128)S(1)}, f32[2,16,512]{2,1,0:T(8,128)S(1)}, ...) custom-call(s32[128]{0:T(128)S(1)} %bitcast.11, ...), custom_call_target="tpu_custom_call" | custom-call | tf_op jit(solution)/shard_map/ahead/pallas_call | solution.py:613
  60.0 7.6 %all-to-all-start.1 = ((f32[128,8,128]{2,1,0:T(8,128)}), f32[128,8,128]{2,1,0:T(8,128)S(1)}, u32[]{:S(2)}, u32[]{:S(2)}) async-start(f32[128,8,128]{2,1,0:T(8,128)} %bitcast.2), calls=%async_computation.1 | async-start | bytes 1048576 | tf_op jit(solution)/shard_map/all_to_all | solution.py:748
  67.5 4.9 %collective-permute-start.12 = (f32[2,4,32,128]{3,2,1,0:T(8,128)S(1)}, f32[2,4,32,128]{3,2,1,0:T(8,128)S(1)}, u32[]{:S(2)}, u32[]{:S(2)}) collective-permute-start(f32[2,4,32,128]{3,2,1,0:T(8,128)S(1)} %get-tuple-element.84), channel_id=1, source_target_pairs={{0,120},{8,16},{16,8},{24,32},{32,24},{40,48},{48,40},{56,64},{64,... | collective-permute-start | bytes 393224 | tf_op jit(solution)/shard_map/ppermute | solution.py:700
  72.4 2.0 %collective-permute-start.14 = (f32[2,16,512]{2,1,0:T(8,128)S(1)}, f32[2,16,512]{2,1,0:T(8,128)S(1)}, u32[]{:S(2)}, u32[]{:S(2)}) collective-permute-start(f32[2,16,512]{2,1,0:T(8,128)S(1)} %get-tuple-element.86), channel_id=1, source_target_pairs={{0,7},{1,2},{2,1},{3,4},{4,3},{5,6},{6,5},{7,0},{8,15},{9,10},{10,... | collective-permute-start | bytes 196616 | tf_op jit(solution)/shard_map/ppermute | solution.py:700
  74.4 1.6 %collective-permute-start.15 = (f32[2,16,512]{2,1,0:T(8,128)S(1)}, f32[2,16,512]{2,1,0:T(8,128)S(1)}, u32[]{:S(2)}, u32[]{:S(2)}) collective-permute-start(f32[2,16,512]{2,1,0:T(8,128)S(1)} %get-tuple-element.87), channel_id=1, source_target_pairs={{0,1},{1,0},{2,3},{3,2},{4,5},{5,4},{6,7},{7,6},{8,9},{9,8},{10,11... | collective-permute-start | bytes 196616 | tf_op jit(solution)/shard_map/ppermute | solution.py:700
  76.0 1.9 %collective-permute-done.14.z_from_outer = f32[2,16,512]{2,1,0:T(8,128)S(1)} collective-permute-done((f32[2,16,512]{2,1,0:T(8,128)S(1)}, f32[2,16,512]{2,1,0:T(8,128)S(1)}, u32[]{:S(2)}, u32[]{:S(2)}) %collective-permute-start.14) | collective-permute-done | bytes 65568 | tf_op jit(solution)/shard_map/ppermute | solution.py:700
  78.0 3.1 %collective-permute-done.12.x_from_outer = f32[2,4,32,128]{3,2,1,0:T(8,128)S(1)} collective-permute-done((f32[2,4,32,128]{3,2,1,0:T(8,128)S(1)}, f32[2,4,32,128]{3,2,1,0:T(8,128)S(1)}, u32[]{:S(2)}, u32[]{:S(2)}) %collective-permute-start.12) | collective-permute-done | bytes 131104 | tf_op jit(solution)/shard_map/ppermute | solution.py:700
  81.0 2.5 %finish.1 = (f32[32,16,512]{2,1,0:T(8,128)}, f32[32,16,512]{2,1,0:T(8,128)}) custom-call(f32[32,16,512]{2,1,0:T(8,128)} %get-tuple-element.79.field_hbm, f32[32,16,512]{2,1,0:T(8,128)} %get-tuple-element.80.adjoint_hbm, f32[4,32,128]{2,1,0:T(8,128)S(1)} %get-tuple-element.81.speed_first, f32[4,32,128]{2,1,0:T(8,128)S(1)} %get-tuple-element.82.speed_last, ...), custom_call_target="tpu_custom_call" | custom-call | tf_op jit(solution)/shard_map/finish/pallas_call | solution.py:680
  (24 shorter events, 2.6 us)
Async XLA Ops:
  5.5 26.6 %copy-start = (s32[1,128,1]{1,2,0:T(1,128)S(1)}, s32[1,128,1]{1,2,0:T(1,128)}, u32[]{:S(2)}) copy-start(s32[1,128,1]{1,2,0:T(1,128)} %param.17) | copy-start | bytes 1540
  5.5 26.6 %all-to-all-start = ((f32[128,8,128]{2,1,0:T(8,128)}), f32[128,8,128]{2,1,0:T(8,128)S(1)}, u32[]{:S(2)}, u32[]{:S(2)}) async-start(f32[128,8,128]{2,1,0:T(8,128)} %surface_rows.1), calls=%async_computation | async-start | bytes 1048576 | tf_op jit(solution)/shard_map/all_to_all | solution.py:721
  18.7 13.4 %collective-permute-start = (f32[2,4,32,128]{3,2,1,0:T(8,128)S(1)}, f32[2,4,32,128]{3,2,1,0:T(8,128)S(1)}, u32[]{:S(2)}, u32[]{:S(2)}) collective-permute-start(f32[2,4,32,128]{3,2,1,0:T(8,128)S(1)} %get-tuple-element.49), channel_id=1, source_target_pairs={{0,120},{8,16},{16,8},{24,32},{32,24},{40,48},{48,40},{56,64},{64,... | collective-permute-start | bytes 393224 | tf_op jit(solution)/shard_map/ppermute | solution.py:700
  23.6 8.5 %collective-permute-start.1 = (f32[2,4,32,128]{3,2,1,0:T(8,128)S(1)}, f32[2,4,32,128]{3,2,1,0:T(8,128)S(1)}, u32[]{:S(2)}, u32[]{:S(2)}) collective-permute-start(f32[2,4,32,128]{3,2,1,0:T(8,128)S(1)} %get-tuple-element.50), channel_id=1, source_target_pairs={{0,8},{8,0},{16,24},{24,16},{32,40},{40,32},{48,56},{56,48},{64,72... | collective-permute-start | bytes 393224 | tf_op jit(solution)/shard_map/ppermute | solution.py:700
  23.6 8.5 %collective-permute-start.2 = (f32[2,16,512]{2,1,0:T(8,128)S(1)}, f32[2,16,512]{2,1,0:T(8,128)S(1)}, u32[]{:S(2)}, u32[]{:S(2)}) collective-permute-start(f32[2,16,512]{2,1,0:T(8,128)S(1)} %get-tuple-element.51), channel_id=1, source_target_pairs={{0,7},{1,2},{2,1},{3,4},{4,3},{5,6},{6,5},{7,0},{8,15},{9,10},{10,... | collective-permute-start | bytes 196616 | tf_op jit(solution)/shard_map/ppermute | solution.py:700
  25.6 6.5 %collective-permute-start.3 = (f32[2,16,512]{2,1,0:T(8,128)S(1)}, f32[2,16,512]{2,1,0:T(8,128)S(1)}, u32[]{:S(2)}, u32[]{:S(2)}) collective-permute-start(f32[2,16,512]{2,1,0:T(8,128)S(1)} %get-tuple-element.52), channel_id=1, source_target_pairs={{0,1},{1,0},{2,3},{3,2},{4,5},{5,4},{6,7},{7,6},{8,9},{9,8},{10,11... | collective-permute-start | bytes 196616 | tf_op jit(solution)/shard_map/ppermute | solution.py:700
  35.5 8.5 %collective-permute-start.4 = (f32[2,4,32,128]{3,2,1,0:T(8,128)S(1)}, f32[2,4,32,128]{3,2,1,0:T(8,128)S(1)}, u32[]{:S(2)}, u32[]{:S(2)}) collective-permute-start(f32[2,4,32,128]{3,2,1,0:T(8,128)S(1)} %get-tuple-element.63), channel_id=1, source_target_pairs={{0,120},{8,16},{16,8},{24,32},{32,24},{40,48},{48,40},{56,64},{64,... | collective-permute-start | bytes 393224 | tf_op jit(solution)/shard_map/ppermute | solution.py:700
  36.3 7.7 %collective-permute-start.5 = (f32[2,4,32,128]{3,2,1,0:T(8,128)S(1)}, f32[2,4,32,128]{3,2,1,0:T(8,128)S(1)}, u32[]{:S(2)}, u32[]{:S(2)}) collective-permute-start(f32[2,4,32,128]{3,2,1,0:T(8,128)S(1)} %get-tuple-element.64), channel_id=1, source_target_pairs={{0,8},{8,0},{16,24},{24,16},{32,40},{40,32},{48,56},{56,48},{64,72... | collective-permute-start | bytes 393224 | tf_op jit(solution)/shard_map/ppermute | solution.py:700
  37.1 5.7 %collective-permute-start.6 = (f32[2,16,512]{2,1,0:T(8,128)S(1)}, f32[2,16,512]{2,1,0:T(8,128)S(1)}, u32[]{:S(2)}, u32[]{:S(2)}) collective-permute-start(f32[2,16,512]{2,1,0:T(8,128)S(1)} %get-tuple-element.65), channel_id=1, source_target_pairs={{0,7},{1,2},{2,1},{3,4},{4,3},{5,6},{6,5},{7,0},{8,15},{9,10},{10,... | collective-permute-start | bytes 196616 | tf_op jit(solution)/shard_map/ppermute | solution.py:700
  38.0 4.8 %collective-permute-start.7 = (f32[2,16,512]{2,1,0:T(8,128)S(1)}, f32[2,16,512]{2,1,0:T(8,128)S(1)}, u32[]{:S(2)}, u32[]{:S(2)}) collective-permute-start(f32[2,16,512]{2,1,0:T(8,128)S(1)} %get-tuple-element.66), channel_id=1, source_target_pairs={{0,1},{1,0},{2,3},{3,2},{4,5},{5,4},{6,7},{7,6},{8,9},{9,8},{10,11... | collective-permute-start | bytes 196616 | tf_op jit(solution)/shard_map/ppermute | solution.py:700
  44.7 8.0 %collective-permute-start.8 = (f32[2,4,32,128]{3,2,1,0:T(8,128)S(1)}, f32[2,4,32,128]{3,2,1,0:T(8,128)S(1)}, u32[]{:S(2)}, u32[]{:S(2)}) collective-permute-start(f32[2,4,32,128]{3,2,1,0:T(8,128)S(1)} %get-tuple-element.73), channel_id=1, source_target_pairs={{0,120},{8,16},{16,8},{24,32},{32,24},{40,48},{48,40},{56,64},{64,... | collective-permute-start | bytes 393224 | tf_op jit(solution)/shard_map/ppermute | solution.py:700
  47.2 5.5 %collective-permute-start.9 = (f32[2,4,32,128]{3,2,1,0:T(8,128)S(1)}, f32[2,4,32,128]{3,2,1,0:T(8,128)S(1)}, u32[]{:S(2)}, u32[]{:S(2)}) collective-permute-start(f32[2,4,32,128]{3,2,1,0:T(8,128)S(1)} %get-tuple-element.74), channel_id=1, source_target_pairs={{0,8},{8,0},{16,24},{24,16},{32,40},{40,32},{48,56},{56,48},{64,72... | collective-permute-start | bytes 393224 | tf_op jit(solution)/shard_map/ppermute | solution.py:700
  47.2 5.4 %collective-permute-start.10 = (f32[2,16,512]{2,1,0:T(8,128)S(1)}, f32[2,16,512]{2,1,0:T(8,128)S(1)}, u32[]{:S(2)}, u32[]{:S(2)}) collective-permute-start(f32[2,16,512]{2,1,0:T(8,128)S(1)} %get-tuple-element.75), channel_id=1, source_target_pairs={{0,7},{1,2},{2,1},{3,4},{4,3},{5,6},{6,5},{7,0},{8,15},{9,10},{10,... | collective-permute-start | bytes 196616 | tf_op jit(solution)/shard_map/ppermute | solution.py:700
  48.1 4.6 %collective-permute-start.11 = (f32[2,16,512]{2,1,0:T(8,128)S(1)}, f32[2,16,512]{2,1,0:T(8,128)S(1)}, u32[]{:S(2)}, u32[]{:S(2)}) collective-permute-start(f32[2,16,512]{2,1,0:T(8,128)S(1)} %get-tuple-element.76), channel_id=1, source_target_pairs={{0,1},{1,0},{2,3},{3,2},{4,5},{5,4},{6,7},{7,6},{8,9},{9,8},{10,11... | collective-permute-start | bytes 196616 | tf_op jit(solution)/shard_map/ppermute | solution.py:700
  60.0 23.6 %all-to-all-start.1 = ((f32[128,8,128]{2,1,0:T(8,128)}), f32[128,8,128]{2,1,0:T(8,128)S(1)}, u32[]{:S(2)}, u32[]{:S(2)}) async-start(f32[128,8,128]{2,1,0:T(8,128)} %bitcast.2), calls=%async_computation.1 | async-start | bytes 1048576 | tf_op jit(solution)/shard_map/all_to_all | solution.py:748
  67.5 13.5 %collective-permute-start.12 = (f32[2,4,32,128]{3,2,1,0:T(8,128)S(1)}, f32[2,4,32,128]{3,2,1,0:T(8,128)S(1)}, u32[]{:S(2)}, u32[]{:S(2)}) collective-permute-start(f32[2,4,32,128]{3,2,1,0:T(8,128)S(1)} %get-tuple-element.84), channel_id=1, source_target_pairs={{0,120},{8,16},{16,8},{24,32},{32,24},{40,48},{48,40},{56,64},{64,... | collective-permute-start | bytes 393224 | tf_op jit(solution)/shard_map/ppermute | solution.py:700
  72.4 8.6 %collective-permute-start.13 = (f32[2,4,32,128]{3,2,1,0:T(8,128)S(1)}, f32[2,4,32,128]{3,2,1,0:T(8,128)S(1)}, u32[]{:S(2)}, u32[]{:S(2)}) collective-permute-start(f32[2,4,32,128]{3,2,1,0:T(8,128)S(1)} %get-tuple-element.85), channel_id=1, source_target_pairs={{0,8},{8,0},{16,24},{24,16},{32,40},{40,32},{48,56},{56,48},{64,72... | collective-permute-start | bytes 393224 | tf_op jit(solution)/shard_map/ppermute | solution.py:700
  72.4 5.5 %collective-permute-start.14 = (f32[2,16,512]{2,1,0:T(8,128)S(1)}, f32[2,16,512]{2,1,0:T(8,128)S(1)}, u32[]{:S(2)}, u32[]{:S(2)}) collective-permute-start(f32[2,16,512]{2,1,0:T(8,128)S(1)} %get-tuple-element.86), channel_id=1, source_target_pairs={{0,7},{1,2},{2,1},{3,4},{4,3},{5,6},{6,5},{7,0},{8,15},{9,10},{10,... | collective-permute-start | bytes 196616 | tf_op jit(solution)/shard_map/ppermute | solution.py:700
  74.4 3.6 %collective-permute-start.15 = (f32[2,16,512]{2,1,0:T(8,128)S(1)}, f32[2,16,512]{2,1,0:T(8,128)S(1)}, u32[]{:S(2)}, u32[]{:S(2)}) collective-permute-start(f32[2,16,512]{2,1,0:T(8,128)S(1)} %get-tuple-element.87), channel_id=1, source_target_pairs={{0,1},{1,0},{2,3},{3,2},{4,5},{5,4},{6,7},{7,6},{8,9},{9,8},{10,11... | collective-permute-start | bytes 196616 | tf_op jit(solution)/shard_map/ppermute | solution.py:700

commit v4 on v3

--- a/solution.py
+++ b/solution.py
@@ -28,15 +28,15 @@
     return pltpu.CompilerParams(vmem_limit_bytes=mib * MIB)
 
 
-def surface_kernel(maps_hbm, patch_hbm, material_hbm, layer_hbm, out, maps, patch_ref, material_ref, layer, vectors, scalars, sems):
+def surface_kernel(maps_hbm, patch_hbm, material_hbm, layer_hbm, out_hbm, out, maps, patch_ref, material_ref, layer, vectors, scalars, sems):
     mats, _, depth = maps.shape
     slots, _, width = layer.shape
-    chunks = sems.shape[0] - 3
+    chunks = (sems.shape[0] - 3) // 2
     block = slots // chunks
     small = [
-        pltpu.make_async_copy(maps_hbm, maps, sems.at[chunks]),
-        pltpu.make_async_copy(patch_hbm, patch_ref, sems.at[chunks + 1]),
-        pltpu.make_async_copy(material_hbm, material_ref, sems.at[chunks + 2]),
+        pltpu.make_async_copy(maps_hbm, maps, sems.at[2 * chunks]),
+        pltpu.make_async_copy(patch_hbm, patch_ref, sems.at[2 * chunks + 1]),
+        pltpu.make_async_copy(material_hbm, material_ref, sems.at[2 * chunks + 2]),
     ]
     large = [
         pltpu.make_async_copy(
@@ -86,28 +86,33 @@
         out[j] = jnp.concatenate(rows, axis=0)
         return carry
 
+    sends = shares_of(out, out_hbm, sems, chunks, chunks)
     for i in range(chunks):
         large[i].wait()
         lax.fori_loop(i * block, (i + 1) * block, one, 0, unroll=4)
+        sends[i].start()
+    for send in sends:
+        send.wait()
 
 
 def surface_rows(layer_maps, slot_patch, patch_material, layer_state):
     slots, depth, width = layer_state.shape
     mats = layer_maps.shape[0]
-    chunks = 4
+    chunks = 8
     return pl.pallas_call(
         surface_kernel,
         in_specs=[pl.BlockSpec(memory_space=HBM)] * 4,
-        out_specs=pl.BlockSpec(memory_space=VMEM),
-        out_shape=jax.ShapeDtypeStruct((slots, LINES, width), jnp.float32),
+        out_specs=pl.BlockSpec(memory_space=HBM),
+        out_shape=HBM((slots, LINES, width), jnp.float32),
         scratch_shapes=[
+            pltpu.VMEM((slots, LINES, width), jnp.float32),
             pltpu.VMEM((mats, depth, depth), jnp.float32),
             pltpu.SMEM(slot_patch.shape, jnp.int32),
             pltpu.SMEM(patch_material.shape, jnp.int32),
             pltpu.VMEM((slots, depth, width), jnp.float32),
             pltpu.VMEM((mats, TERMS, depth, width), jnp.float32),
             pltpu.VMEM((mats, 8, width), jnp.float32),
-            pltpu.SemaphoreType.DMA((chunks + 3,)),
+            pltpu.SemaphoreType.DMA((2 * chunks + 3,)),
         ],
         compiler_params=params(24),
         name="surface_rows",
@@ -418,17 +423,11 @@
     )(*in_hbm(rows, field, field_prev, adjoint, adjoint_prev, speed2))
 
 
-def first_border_kernel(rows_ref, partial_hbm, partial_adjoint_hbm, field_hbm, adjoint_hbm, speed2_hbm, x_from_outer, x_from_inner, z_from_outer, z_from_inner, lines_ref, push, picked, out, adjoint_out, field, adjoint, speed2, x_outer, x_inner, z_outer, z_inner, surface, partial, partial_adjoint, coupling, change, sems):
+def first_border_kernel(rows_ref, partial_hbm, partial_adjoint_hbm, speed2_hbm, x_from_outer, x_from_inner, z_from_outer, z_from_inner, lines_ref, push, picked, out, adjoint_out, speed2, x_outer, x_inner, z_outer, z_inner, surface, partial, partial_adjoint, coupling, change, sems):
     loads = [
         pltpu.make_async_copy(source, target, sems.at[i])
         for i, (source, target) in enumerate(
-            (
-                (speed2_hbm, speed2),
-                (partial_hbm, partial),
-                (partial_adjoint_hbm, partial_adjoint),
-                (field_hbm, field),
-                (adjoint_hbm, adjoint),
-            )
+            ((speed2_hbm, speed2), (partial_hbm, partial), (partial_adjoint_hbm, partial_adjoint))
         )
     ]
     for copy in loads:
@@ -436,7 +435,7 @@
     coupling[...] = jnp.zeros_like(coupling)
     lines = Lines(lines_ref, change.shape[1])
     couple_step(rows_ref, lines, 0, [push], picked, surface, change, coupling)
-    for copy in loads[:3]:
+    for copy in loads:
         copy.wait()
     border_planes(
         (partial, partial_adjoint),
@@ -446,8 +445,6 @@
         (x_outer, x_inner, z_outer, z_inner),
         functools.partial(extra_of, coupling),
     )
-    for copy in loads[3:]:
-        copy.wait()
 
 
 def coupling_scratch(field, slots, width):
@@ -458,35 +455,48 @@
     ]
 
 
-def first_border(rows, partials, field, adjoint, speed2, halos, lines, push, picked):
+def first_border(rows, partials, speed2, halos, lines, push, picked):
     _, slots, width = push.shape
+    field = partials[0]
     whole = jax.ShapeDtypeStruct(field.shape, jnp.float32)
     in_vmem = pl.BlockSpec(memory_space=VMEM)
     return pl.pallas_call(
         first_border_kernel,
         in_specs=[pl.BlockSpec(memory_space=SMEM)]
-        + [pl.BlockSpec(memory_space=HBM)] * 5
+        + [pl.BlockSpec(memory_space=HBM)] * 3
         + [in_vmem] * 7,
-        out_specs=[in_vmem] * 10,
-        out_shape=[whole] * 5
+        out_specs=[in_vmem] * 8,
+        out_shape=[whole] * 3
         + edge_shapes(field, width)
         + [jax.ShapeDtypeStruct((2, slots, width), jnp.float32)],
         scratch_shapes=[pltpu.VMEM(field.shape, jnp.float32)] * 2
         + coupling_scratch(field, slots, width)
-        + [pltpu.SemaphoreType.DMA((5,))],
+        + [pltpu.SemaphoreType.DMA((3,))],
         compiler_params=params(12),
         name="border0",
-    )(rows, *in_hbm(*partials, field, adjoint, speed2), *halos, lines, push, picked)
+    )(rows, *in_hbm(*partials, speed2), *halos, lines, push, picked)
 
 
 def local_kernel(step, rows_ref, field, field_prev, adjoint, adjoint_prev, speed2, lines_ref, surface, *refs):
     pushes, refs = list(refs[:step]), refs[step:]
-    out, adjoint_out, push, next_surface, coupling, change, tiles, picked = refs
+    out, adjoint_out, push, next_surface, coupling, change, tiles, picked = refs[:8]
+    loads = []
+    if step == 1:
+        *held, sems = refs[8:]
+        loads = [
+            pltpu.make_async_copy(source, target, sems.at[i])
+            for i, (source, target) in enumerate(zip((field_prev, adjoint_prev), held))
+        ]
+        field_prev, adjoint_prev = held
+    for copy in loads:
+        copy.start()
     pick(rows_ref, (field, adjoint), picked, tiles)
     push[...] = KAPPA * (picked[...] - surface[...])
     coupling[...] = jnp.zeros_like(coupling)
     lines = Lines(lines_ref, change.shape[1])
     couple_step(rows_ref, lines, step, pushes + [push], picked, next_surface, change, coupling)
+    for copy in loads:
+        copy.wait()
     local_planes(
         (field, adjoint),
         (field_prev, adjoint_prev),
@@ -501,17 +511,24 @@
     whole = jax.ShapeDtypeStruct(field.shape, jnp.float32)
     rows_shape = jax.ShapeDtypeStruct(surface.shape, jnp.float32)
     in_vmem = pl.BlockSpec(memory_space=VMEM)
+    before, held = in_vmem, []
+    if step == 1:
+        before = pl.BlockSpec(memory_space=HBM)
+        held = [pltpu.VMEM(field.shape, jnp.float32)] * 2 + [pltpu.SemaphoreType.DMA((2,))]
+        field_prev, adjoint_prev = in_hbm(field_prev, adjoint_prev)
     return pl.pallas_call(
         functools.partial(local_kernel, step),
-        in_specs=[pl.BlockSpec(memory_space=SMEM)] + [in_vmem] * (7 + step),
+        in_specs=[pl.BlockSpec(memory_space=SMEM), in_vmem, before, in_vmem, before]
+        + [in_vmem] * (3 + step),
         out_specs=[in_vmem] * 4,
         out_shape=[whole, whole, rows_shape, rows_shape],
         scratch_shapes=coupling_scratch(field, slots, width)
         + [
             pltpu.VMEM((2, 8 * slots, width), jnp.float32),
             pltpu.VMEM((2, slots, width), jnp.float32),
-        ],
-        compiler_params=params(8),
+        ]
+        + held,
+        compiler_params=params(10),
         cost_estimate=pl.CostEstimate(flops=8 << 20, bytes_accessed=12 << 20, transcendentals=0),
         name=f"local{step}",
     )(rows, field, field_prev, adjoint, adjoint_prev, speed2, lines, surface, *pushes)
@@ -542,90 +559,135 @@
     )(*partials, speed2, *halos)
 
 
-def ahead_kernel(rows_ref, partial, partial_adjoint, field_prev, adjoint_prev, speed2, x_from_outer, x_from_inner, z_from_outer, z_from_inner, lines_ref, surface, *refs):
+def correlation_kernel(rows_ref, field, field_prev, adjoint, adjoint_prev, lines_ref, surface, *refs):
     pushes, refs = list(refs[: STEPS - 1]), refs[STEPS - 1 :]
-    x_outer, x_inner, z_outer, z_inner, speed_first, speed_last, speed_ends, gradient = refs[:8]
-    next_hbm, next_adjoint_hbm, coupling, change, tiles, picked, push, next_surface = refs[8:16]
-    field, adjoint, out, adjoint_out, sems = refs[16:]
-    cells_z, cells_x, _ = speed2.shape
-    coupling[...] = jnp.zeros_like(coupling)
-    border_planes(
-        (partial, partial_adjoint),
-        speed2,
-        (x_from_outer, x_from_inner, z_from_outer, z_from_inner),
-        (field, adjoint),
-        (x_outer, x_inner, z_outer, z_inner),
-        None,
-    )
-    speed_ends[0], speed_ends[1] = speed2[0], speed2[cells_z - 1]
-
-    def sides(z, carry):
-        keep_side(speed2[z], z, speed_first, speed_last)
-        return carry
-
-    lax.fori_loop(0, cells_z, sides, 0, unroll=8)
+    gradient_hbm, change = refs[:2]
+    targets, (gradient, tiles, picked, push, sems) = refs[2:6], refs[6:]
+    sends = [
+        pltpu.make_async_copy(source, target, sems.at[i])
+        for i, (source, target) in enumerate(
+            zip((field, field_prev, adjoint, adjoint_prev), targets)
+        )
+    ]
+    for send in sends:
+        send.start()
     pick(rows_ref, (field, adjoint), picked, tiles)
     push[...] = KAPPA * (picked[...] - surface[...])
 
-    slots = change.shape[1]
+    slots, width = change.shape[1:]
     lines = Lines(lines_ref, slots)
     known = pushes + [push]
-    total = jnp.zeros(change.shape[1:], jnp.float32)
+    total = jnp.zeros((slots, width), jnp.float32)
     for late in range(STEPS):
         inside = (STEPS - late) * lines.row(TERMS - late)
         for t in range(STEPS - late):
             scale = (STEPS - late - t) * lines.scalar(TERMS - late - t)
             inside = inside + scale * known[t][0]
         total = total + known[late][1] * inside
-    ids = lines.scalar(0).astype(jnp.int32)
-    owners = lax.broadcasted_iota(jnp.int32, (slots, gradient.shape[0]), 1) == ids
-    gradient[...] = lax.dot_general(
-        owners.astype(jnp.float32),
-        total,
-        (((0,), (0,)), ((), ())),
-        precision=lax.Precision.HIGHEST,
+    patches = gradient.shape[0]
+    parts, rest = [], total
+    for _ in range(3):
+        parts.append(rest.astype(jnp.bfloat16))
+        rest = rest - parts[-1].astype(jnp.float32)
+    ids = lines.meta.T[0:1, :].astype(jnp.int32)
+    owners = lax.broadcasted_iota(jnp.int32, (patches, slots), 0) == ids
+    sums = jnp.dot(
+        jnp.where(owners, 1.0, 0.0).astype(jnp.bfloat16),
+        jnp.concatenate(parts, axis=1),
         preferred_element_type=jnp.float32,
     )
-
-    couple_step(rows_ref, lines, STEPS - 1, known, picked, next_surface, change, coupling)
-    sends = list(
-        zip(shares_of(out, next_hbm, sems, 0, 4), shares_of(adjoint_out, next_adjoint_hbm, sems, 4, 4))
-    )
+    gradient[...] = sums[:, :width] + (sums[:, width : 2 * width] + sums[:, 2 * width :])
+    sends.append(pltpu.make_async_copy(gradient, gradient_hbm, sems.at[4]))
+    sends[-1].start()
+
+    for side in range(2):
+        change[side] = BETA * (lines.surface(STEPS - 1, known, side) - picked[side])
+    for send in sends:
+        send.wait()
+
+
+def correlate(rows, field, field_prev, adjoint, adjoint_prev, lines, surface, pushes, patches):
+    _, slots, width = surface.shape
+    f32 = jnp.float32
+    in_vmem = pl.BlockSpec(memory_space=VMEM)
+    return pl.pallas_call(
+        correlation_kernel,
+        in_specs=[pl.BlockSpec(memory_space=SMEM)] + [in_vmem] * (6 + len(pushes)),
+        out_specs=[pl.BlockSpec(memory_space=HBM), in_vmem] + [pl.BlockSpec(memory_space=HBM)] * 4,
+        out_shape=[
+            HBM((patches, width), f32),
+            jax.ShapeDtypeStruct(surface.shape, f32),
+        ]
+        + [HBM(field.shape, f32)] * 4,
+        scratch_shapes=[
+            pltpu.VMEM((patches, width), f32),
+            pltpu.VMEM((2, 8 * slots, width), f32),
+        ]
+        + [pltpu.VMEM((2, slots, width), f32)] * 2
+        + [pltpu.SemaphoreType.DMA((5,))],
+        compiler_params=params(10),
+        name="correlation",
+    )(rows, field, field_prev, adjoint, adjoint_prev, lines, surface, *pushes)
+
+
+def last_local_kernel(rows_hbm, field_hbm, field_prev_hbm, adjoint_hbm, adjoint_prev_hbm, speed2_hbm, change, out, adjoint_out, speed_first, speed_last, speed_ends, rows_ref, field, field_prev, adjoint, adjoint_prev, speed2, coupling, sems):
+    loads = [
+        pltpu.make_async_copy(source, target, sems.at[i])
+        for i, (source, target) in enumerate(
+            (
+                (rows_hbm, rows_ref),
+                (speed2_hbm, speed2),
+                (field_hbm, field),
+                (adjoint_hbm, adjoint),
+                (field_prev_hbm, field_prev),
+                (adjoint_prev_hbm, adjoint_prev),
+            )
+        )
+    ]
+    for copy in loads:
+        copy.start()
+    coupling[...] = jnp.zeros_like(coupling)
+    loads[0].wait()
+    couple(rows_ref, change, coupling)
+    loads[1].wait()
+    cells_z = speed2.shape[0]
+    speed_ends[0], speed_ends[1] = speed2[0], speed2[cells_z - 1]
+
+    def sides(z, carry):
+        keep_side(speed2[z], z, speed_first, speed_last)
+        return carry
+
+    lax.fori_loop(0, cells_z, sides, 0, unroll=8)
+    for copy in loads[2:]:
+        copy.wait()
     local_planes(
         (field, adjoint),
         (field_prev, adjoint_prev),
         (out, adjoint_out),
         speed2,
         functools.partial(extra_of, coupling),
-        sends,
-    )
-    for pair in sends:
-        for send in pair:
-            send.wait()
-
-
-def ahead_step(rows, partials, field_prev, adjoint_prev, speed2, halos, lines, surface, pushes, patches):
-    _, slots, width = surface.shape
-    cells_z, cells_x, along = field_prev.shape
+    )
+
+
+def last_local(rows, field, field_prev, adjoint, adjoint_prev, speed2, change):
+    _, slots, width = change.shape
+    cells_z, cells_x, along = field.shape
+    sides = jax.ShapeDtypeStruct((along // width, cells_z, width), jnp.float32)
     in_vmem = pl.BlockSpec(memory_space=VMEM)
-    f32 = jnp.float32
-    sides = jax.ShapeDtypeStruct((along // width, cells_z, width), f32)
     return pl.pallas_call(
-        ahead_kernel,
-        in_specs=[pl.BlockSpec(memory_space=SMEM)] + [in_vmem] * (11 + len(pushes)),
-        out_specs=[in_vmem] * 8 + [pl.BlockSpec(memory_space=HBM)] * 2,
-        out_shape=edge_shapes(field_prev, width)
-        + [sides, sides, jax.ShapeDtypeStruct((2, cells_x, along), f32)]
-        + [jax.ShapeDtypeStruct((patches, width), f32)]
-        + [HBM(field_prev.shape, f32)] * 2,
-        scratch_shapes=coupling_scratch(field_prev, slots, width)
-        + [pltpu.VMEM((2, 8 * slots, width), f32)]
-        + [pltpu.VMEM((2, slots, width), f32)] * 3
-        + [pltpu.VMEM(field_prev.shape, f32)] * 4
-        + [pltpu.SemaphoreType.DMA((8,))],
+        last_local_kernel,
+        in_specs=[pl.BlockSpec(memory_space=HBM)] * 6 + [in_vmem],
+        out_specs=[in_vmem] * 5,
+        out_shape=[jax.ShapeDtypeStruct(field.shape, jnp.float32)] * 2
+        + [sides, sides, jax.ShapeDtypeStruct((2, cells_x, along), jnp.float32)],
+        scratch_shapes=[pltpu.SMEM((slots,), jnp.int32)]
+        + [pltpu.VMEM(field.shape, jnp.float32)] * 5
+        + coupling_scratch(field, slots, width)[:1]
+        + [pltpu.SemaphoreType.DMA((6,))],
         compiler_params=params(16),
-        name="ahead",
-    )(rows, *partials, field_prev, adjoint_prev, speed2, *halos, lines, surface, *pushes)
+        cost_estimate=pl.CostEstimate(flops=8 << 20, bytes_accessed=12 << 20, transcendentals=0),
+        name=f"local{STEPS - 1}",
+    )(*in_hbm(rows, field, field_prev, adjoint, adjoint_prev, speed2), change)
 
 
 def keep_side(cells, z, first, last):
@@ -636,30 +698,24 @@
         last[part, pl.ds(z, 1), :] = cells[last_x : last_x + 1, lanes]
 
 
-def finish_kernel(field_hbm, adjoint_hbm, speed_first, speed_last, speed_ends, x_from_outer, x_from_inner, z_from_outer, z_from_inner, out_hbm, adjoint_out_hbm, field, adjoint, sems):
+def finish_kernel(field_in, adjoint_in, speed_first, speed_last, speed_ends, x_from_outer, x_from_inner, z_from_outer, z_from_inner, out_hbm, adjoint_out_hbm, field, adjoint, sems):
     cells_z, cells_x, along = field.shape
     parts = speed_first.shape[0]
     shares = 4
     share = cells_z // shares
-    loads, sends = [], []
-    for side, (source, held, target) in enumerate(
-        ((field_hbm, field, out_hbm), (adjoint_hbm, adjoint, adjoint_out_hbm))
-    ):
-        loads.append(shares_of(source, held, sems, 2 * side * shares, shares))
-        sends.append(shares_of(held, target, sems, (2 * side + 1) * shares, shares))
+    sends = [
+        shares_of(field, out_hbm, sems, 0, shares),
+        shares_of(adjoint, adjoint_out_hbm, sems, shares, shares),
+    ]
     for i in range(shares):
-        for side in range(2):
-            loads[side][i].start()
-    for i in range(shares):
-        for side, held in enumerate((field, adjoint)):
-            loads[side][i].wait()
+        for side, (source, held) in enumerate(((field_in, field), (adjoint_in, adjoint))):
 
             def one(z, carry):
                 first, last = (
                     jnp.concatenate([ref[p, pl.ds(z, 1), :] for p in range(parts)], axis=1)
                     for ref in (speed_first, speed_last)
                 )
-                held[z] = held[z] + x_added(
+                held[z] = source[z] + x_added(
                     first, last, x_from_outer, x_from_inner, side, z, (cells_x, along)
                 )
                 return carry
@@ -679,13 +735,13 @@
 def finish_call(field, adjoint, speed_first, speed_last, speed_ends, halos):
     return pl.pallas_call(
         finish_kernel,
-        in_specs=[pl.BlockSpec(memory_space=HBM)] * 2 + [pl.BlockSpec(memory_space=VMEM)] * 7,
+        in_specs=[pl.BlockSpec(memory_space=VMEM)] * 9,
         out_specs=[pl.BlockSpec(memory_space=HBM)] * 2,
         out_shape=[HBM(field.shape, jnp.float32)] * 2,
-        scratch_shapes=[pltpu.VMEM(field.shape, jnp.float32)] * 2 + [pltpu.SemaphoreType.DMA((16,))],
+        scratch_shapes=[pltpu.VMEM(field.shape, jnp.float32)] * 2 + [pltpu.SemaphoreType.DMA((8,))],
         compiler_params=params(8),
         name="finish",
-    )(*in_hbm(field, adjoint), speed_first, speed_last, speed_ends, *halos)
+    )(field, adjoint, speed_first, speed_last, speed_ends, *halos)
 
 
 def swaps(axis, first):
@@ -717,20 +773,20 @@
     devices = lax.axis_size(("gx", "gz"))
     rows = send_rows.reshape(-1)
 
+    edges = first_edges(pressure_now, adjoint_now, width)
+    halos = exchange(edges)
     lines = surface_rows(layer_maps, slot_patch, patch_material, layer_state)
     lines = lax.all_to_all(lines, ("gx", "gz"), split_axis=0, concat_axis=0, tiled=True)
     lines = lines.reshape(slots * LINES, width)
 
-    halos = exchange(first_edges(pressure_now, adjoint_now, width))
     *partials, push, picked = first_local(
         rows, pressure_now, pressure_prev, adjoint_now, adjoint_prev, speed2, slots, width
     )
     pushes = [push]
-    results = first_border(
-        rows, partials, pressure_now, adjoint_now, speed2, halos, lines, push, picked
-    )
-    field, adjoint, field_prev, adjoint_prev, speed = results[:5]
-    edges, surface = results[5:9], results[9]
+    field, adjoint, speed, *edges, surface = first_border(
+        rows, partials, speed2, halos, lines, push, picked
+    )
+    field_prev, adjoint_prev = pressure_now, adjoint_now
     for step in range(1, STEPS - 1):
         halos = exchange(edges)
         *partials, push, surface = local_step(
@@ -738,16 +794,15 @@
         )
         pushes.append(push)
         field_prev, adjoint_prev = field, adjoint
-        if step < STEPS - 2:
-            field, adjoint, *edges = border_step(step, partials, speed, halos, width)
-    results = ahead_step(
-        rows, partials, field_prev, adjoint_prev, speed, halos, lines, surface, pushes, patches
-    )
-    edges, speeds, gradient, partials = results[:4], results[4:7], results[7], results[8:]
+        field, adjoint, *edges = border_step(step, partials, speed, halos, width)
+    halos = exchange(edges)
+    gradient, change, *held = correlate(
+        rows, field, field_prev, adjoint, adjoint_prev, lines, surface, pushes, patches
+    )
     parts = gradient.reshape(devices, patches // devices, width)
     parts = lax.all_to_all(parts, ("gx", "gz"), split_axis=0, concat_axis=0, tiled=True)
-    halos = exchange(edges)
-    field, adjoint = finish_call(*partials, *speeds, halos)
+    *partials, first, last, ends = last_local(rows, *held, speed2, change)
+    field, adjoint = finish_call(*partials, first, last, ends, halos)
     return field, adjoint, jnp.sum(parts, axis=0)
 
 

time: 84.5 us -> 80.1 us (0.948)
  waiting for transfers between devices: 6.23 us -> 1.96 us
    ppermute x16, waiting for transfers between devices: 6.23 us -> 1.95 us  [exchange(): lax.ppermute(edge, axis, swaps(axis, first))]
    pallas_call x2 -> x3, Pallas kernels: 9.7 us -> 8.78 us  [the longest x1 4.22 us: last_local(): pl.pallas_call(last_local_kernel, in_specs=[pl.BlockSpec(memory_space=HBM...]
  transfers between devices with their start and end apart: 18 -> 18, of which waited for: 3 -> 2; matrix products, arithmetic and copies ran while one was open for 0% -> 0% of each run, Pallas kernels for 21% -> 26%
where the time goes in v4:
time: 80.1 us; the launch traced here: 79.8 us
  starting transfers between devices  43.1 us (54%)
  Pallas kernels  33.2 us (41%)
  waiting for transfers between devices  1.96 us (2%)
  between operations  0.87 us (1%)
    ppermute x16, starting transfers between devices, exchange(): lax.ppermute(edge, axis, swaps(axis, first))  24 us
    all_to_all x1, starting transfers between devices, body(): lax.all_to_all(lines, ('gx', 'gz'), split_axis=0, concat_axis=0, tiled=True)  11.5 us
    pallas_call x2, Pallas kernels, local_step(): pl.pallas_call(functools.partial(local_kernel, step), in_specs=[pl.BlockS...  8.35 us
    all_to_all x1, starting transfers between devices, body(): lax.all_to_all(parts, ('gx', 'gz'), split_axis=0, concat_axis=0, tiled=True)  7.52 us
    pallas_call x1, Pallas kernels, first_local(): pl.pallas_call(first_local_kernel, in_specs=[pl.BlockSpec(memory_space=HB...  4.87 us
    pallas_call x1, Pallas kernels, surface_rows(): pl.pallas_call(surface_kernel, in_specs=[pl.BlockSpec(memory_space=HBM)]...  4.8 us
    pallas_call x1, Pallas kernels, last_local(): pl.pallas_call(last_local_kernel, in_specs=[pl.BlockSpec(memory_space=HBM...  4.22 us
    pallas_call x1, Pallas kernels, first_border(): pl.pallas_call(first_border_kernel, in_specs=[pl.BlockSpec(memory_space=S...  3.28 us
  transfers between devices with their start and end apart: 18, of which 2 were waited for; matrix products, arithmetic and copies ran while one was open for 0% of the time, Pallas kernels for 26%

profile of v4, /device:TPU:1, one launch (start us, length us, event | category | flops | bytes accessed | tf_op | source)
XLA Modules:
  0.0 79.8 jit_solution(9925629226909011231)
XLA Ops:
  0.6 4.8 %surface_rows.1 = f32[128,8,128]{2,1,0:T(8,128)} custom-call(f32[8,64,64]{2,1,0:T(8,128)} %maps_hbm.1, s32[128]{0:T(128)} %patch_hbm.1, s32[1024]{0:T(1024)} %material_hbm.1, f32[128,64,128]{2,1,0:T(8,128)} %layer_hbm.1), custom_call_target="tpu_custom_call" | custom-call | tf_op jit(solution)/shard_map/surface_rows/pallas_call | solution.py:102
  5.4 11.5 %all-to-all-start = ((f32[128,8,128]{2,1,0:T(8,128)}), f32[128,8,128]{2,1,0:T(8,128)S(1)}, u32[]{:S(2)}, u32[]{:S(2)}) async-start(f32[128,8,128]{2,1,0:T(8,128)} %surface_rows.1), calls=%async_computation | async-start | bytes 1048576 | tf_op jit(solution)/shard_map/all_to_all | solution.py:779
  17.0 1.7 %edges.1 = (f32[2,4,32,128]{3,2,1,0:T(8,128)S(1)}, f32[2,4,32,128]{3,2,1,0:T(8,128)S(1)}, f32[2,16,512]{2,1,0:T(8,128)S(1)}, f32[2,16,512]{2,1,0:T(8,128)S(1)}) custom-call(f32[32,16,512]{2,1,0:T(8,128)} %field_prev.1, f32[32,16,512]{2,1,0:T(8,128)} %adjoint_prev.1), custom_call_target="tpu_custom_call" | custom-call | tf_op jit(solution)/shard_map/edges/pallas_call | solution.py:226
  18.7 4.9 %collective-permute-start = (f32[2,4,32,128]{3,2,1,0:T(8,128)S(1)}, f32[2,4,32,128]{3,2,1,0:T(8,128)S(1)}, u32[]{:S(2)}, u32[]{:S(2)}) collective-permute-start(f32[2,4,32,128]{3,2,1,0:T(8,128)S(1)} %get-tuple-element.54), channel_id=1, source_target_pairs={{0,120},{8,16},{16,8},{24,32},{32,24},{40,48},{48,40},{56,64},{64,... | collective-permute-start | bytes 393224 | tf_op jit(solution)/shard_map/ppermute | solution.py:756
  23.5 2.0 %collective-permute-start.2 = (f32[2,16,512]{2,1,0:T(8,128)S(1)}, f32[2,16,512]{2,1,0:T(8,128)S(1)}, u32[]{:S(2)}, u32[]{:S(2)}) collective-permute-start(f32[2,16,512]{2,1,0:T(8,128)S(1)} %get-tuple-element.56), channel_id=1, source_target_pairs={{0,7},{1,2},{2,1},{3,4},{4,3},{5,6},{6,5},{7,0},{8,15},{9,10},{10,... | collective-permute-start | bytes 196616 | tf_op jit(solution)/shard_map/ppermute | solution.py:756
  25.5 1.6 %collective-permute-start.3 = (f32[2,16,512]{2,1,0:T(8,128)S(1)}, f32[2,16,512]{2,1,0:T(8,128)S(1)}, u32[]{:S(2)}, u32[]{:S(2)}) collective-permute-start(f32[2,16,512]{2,1,0:T(8,128)S(1)} %get-tuple-element.57), channel_id=1, source_target_pairs={{0,1},{1,0},{2,3},{3,2},{4,5},{5,4},{6,7},{7,6},{8,9},{9,8},{10,11... | collective-permute-start | bytes 196616 | tf_op jit(solution)/shard_map/ppermute | solution.py:756
  27.1 4.9 %local0.1 = (f32[32,16,512]{2,1,0:T(8,128)}, f32[32,16,512]{2,1,0:T(8,128)}, f32[2,128,128]{2,1,0:T(8,128)S(1)}, f32[2,128,128]{2,1,0:T(8,128)S(1)}) custom-call(s32[128]{0:T(128)} %bitcast.7, f32[32,16,512]{2,1,0:T(8,128)} %field_prev.1, f32[32,16,512]{2,1,0:T(8,128)} %field_prev_hbm.1, f32[32,16,512]{2,1,0:T(8,128)} %adjoint_prev.1, ...), custom_call_target="tpu_custom_call" | custom-call | flops 8388608 | bytes 12582912 | tf_op jit(solution)/shard_map/local0/pallas_call | solution.py:412
  32.1 3.3 %border0.1 = (f32[32,16,512]{2,1,0:T(8,128)S(1)}, f32[32,16,512]{2,1,0:T(8,128)S(1)}, f32[32,16,512]{2,1,0:T(8,128)S(1)}, f32[2,4,32,128]{3,2,1,0:T(8,128)S(1)},...) custom-call(s32[128]{0:T(128)S(1)} %bitcast.9, ...), custom_call_target="tpu_custom_call" | custom-call | tf_op jit(solution)/shard_map/border0/pallas_call | solution.py:463
  35.4 0.8 %collective-permute-start.4 = (f32[2,4,32,128]{3,2,1,0:T(8,128)S(1)}, f32[2,4,32,128]{3,2,1,0:T(8,128)S(1)}, u32[]{:S(2)}, u32[]{:S(2)}) collective-permute-start(f32[2,4,32,128]{3,2,1,0:T(8,128)S(1)} %get-tuple-element.66), channel_id=1, source_target_pairs={{0,120},{8,16},{16,8},{24,32},{32,24},{40,48},{48,40},{56,64},{64,... | collective-permute-start | bytes 393224 | tf_op jit(solution)/shard_map/ppermute | solution.py:756
  36.2 0.8 %collective-permute-start.5 = (f32[2,4,32,128]{3,2,1,0:T(8,128)S(1)}, f32[2,4,32,128]{3,2,1,0:T(8,128)S(1)}, u32[]{:S(2)}, u32[]{:S(2)}) collective-permute-start(f32[2,4,32,128]{3,2,1,0:T(8,128)S(1)} %get-tuple-element.67), channel_id=1, source_target_pairs={{0,8},{8,0},{16,24},{24,16},{32,40},{40,32},{48,56},{56,48},{64,72... | collective-permute-start | bytes 393224 | tf_op jit(solution)/shard_map/ppermute | solution.py:756
  37.0 0.9 %collective-permute-start.6 = (f32[2,16,512]{2,1,0:T(8,128)S(1)}, f32[2,16,512]{2,1,0:T(8,128)S(1)}, u32[]{:S(2)}, u32[]{:S(2)}) collective-permute-start(f32[2,16,512]{2,1,0:T(8,128)S(1)} %get-tuple-element.68), channel_id=1, source_target_pairs={{0,7},{1,2},{2,1},{3,4},{4,3},{5,6},{6,5},{7,0},{8,15},{9,10},{10,... | collective-permute-start | bytes 196616 | tf_op jit(solution)/shard_map/ppermute | solution.py:756
  38.6 4.2 %local1.1 = (f32[32,16,512]{2,1,0:T(8,128)S(1)}, f32[32,16,512]{2,1,0:T(8,128)S(1)}, f32[2,128,128]{2,1,0:T(8,128)S(1)}, f32[2,128,128]{2,1,0:T(8,128)S(1)}) custom-call(s32[128]{0:T(128)S(1)} %bitcast.10, f32[32,16,512]{2,1,0:T(8,128)S(1)} %get-tuple-element.60.field.field_prev, f32[32,16,512]{2,1,0:T(8,128)} %field_prev.1, ...), custom_call_target="tpu_custom_call" | custom-call | flops 8388608 | bytes 12582912 | tf_op jit(solution)/shard_map/local1/pallas_call | solution.py:519
  42.8 1.1 %collective-permute-done.4.x_from_outer = f32[2,4,32,128]{3,2,1,0:T(8,128)S(1)} collective-permute-done((f32[2,4,32,128]{3,2,1,0:T(8,128)S(1)}, f32[2,4,32,128]{3,2,1,0:T(8,128)S(1)}, u32[]{:S(2)}, u32[]{:S(2)}) %collective-permute-start.4) | collective-permute-done | bytes 131104 | tf_op jit(solution)/shard_map/ppermute | solution.py:756
  44.6 2.6 %collective-permute-start.8 = (f32[2,4,32,128]{3,2,1,0:T(8,128)S(1)}, f32[2,4,32,128]{3,2,1,0:T(8,128)S(1)}, u32[]{:S(2)}, u32[]{:S(2)}) collective-permute-start(f32[2,4,32,128]{3,2,1,0:T(8,128)S(1)} %get-tuple-element.76), channel_id=1, source_target_pairs={{0,120},{8,16},{16,8},{24,32},{32,24},{40,48},{48,40},{56,64},{64,... | collective-permute-start | bytes 393224 | tf_op jit(solution)/shard_map/ppermute | solution.py:756
  47.2 0.9 %collective-permute-start.10 = (f32[2,16,512]{2,1,0:T(8,128)S(1)}, f32[2,16,512]{2,1,0:T(8,128)S(1)}, u32[]{:S(2)}, u32[]{:S(2)}) collective-permute-start(f32[2,16,512]{2,1,0:T(8,128)S(1)} %get-tuple-element.78), channel_id=1, source_target_pairs={{0,7},{1,2},{2,1},{3,4},{4,3},{5,6},{6,5},{7,0},{8,15},{9,10},{10,... | collective-permute-start | bytes 196616 | tf_op jit(solution)/shard_map/ppermute | solution.py:756
  48.5 4.2 %local2.1 = (f32[32,16,512]{2,1,0:T(8,128)S(1)}, f32[32,16,512]{2,1,0:T(8,128)S(1)}, f32[2,128,128]{2,1,0:T(8,128)S(1)}, f32[2,128,128]{2,1,0:T(8,128)S(1)}) custom-call(s32[128]{0:T(128)S(1)} %bitcast.11, f32[32,16,512]{2,1,0:T(8,128)S(1)} %get-tuple-element.70.field.field_prev, f32[32,16,512]{2,1,0:T(8,128)S(1)} %get-tuple-element.60.field.field_prev, ...), custom_call_target="tpu_custom_call" | custom-call | flops 8388608 | bytes 12582912 | tf_op jit(solution)/shard_map/local2/pallas_call | solution.py:519
  53.5 3.1 %correlation.1 = (f32[1024,128]{1,0:T(8,128)}, f32[2,128,128]{2,1,0:T(8,128)S(1)}, f32[32,16,512]{2,1,0:T(8,128)}, f32[32,16,512]{2,1,0:T(8,128)}, f32[32,16,512]{2,1,0:T(8,128)}, /*index=5*/f32[32,16,512]{2,1,0:T(8,128)}) custom-call(s32[128]{0:T(128)S(1)} %bitcast.12, f32[32,16,512]{2,1,0:T(8,128)S(1)} %get-tuple-element.80.field, ...), custom_call_target="tpu_custom_call" | custom-call | tf_op jit(solution)/shard_map/correlation/pallas_call | solution.py:613
  56.6 7.5 %all-to-all-start.1 = ((f32[128,8,128]{2,1,0:T(8,128)}), f32[128,8,128]{2,1,0:T(8,128)S(1)}, u32[]{:S(2)}, u32[]{:S(2)}) async-start(f32[128,8,128]{2,1,0:T(8,128)} %bitcast.13), calls=%async_computation.1 | async-start | bytes 1048576 | tf_op jit(solution)/shard_map/all_to_all | solution.py:803
  64.1 4.9 %collective-permute-start.12 = (f32[2,4,32,128]{3,2,1,0:T(8,128)S(1)}, f32[2,4,32,128]{3,2,1,0:T(8,128)S(1)}, u32[]{:S(2)}, u32[]{:S(2)}) collective-permute-start(f32[2,4,32,128]{3,2,1,0:T(8,128)S(1)} %get-tuple-element.94), channel_id=1, source_target_pairs={{0,120},{8,16},{16,8},{24,32},{32,24},{40,48},{48,40},{56,64},{64,... | collective-permute-start | bytes 393224 | tf_op jit(solution)/shard_map/ppermute | solution.py:756
  69.0 2.0 %collective-permute-start.14 = (f32[2,16,512]{2,1,0:T(8,128)S(1)}, f32[2,16,512]{2,1,0:T(8,128)S(1)}, u32[]{:S(2)}, u32[]{:S(2)}) collective-permute-start(f32[2,16,512]{2,1,0:T(8,128)S(1)} %get-tuple-element.96), channel_id=1, source_target_pairs={{0,7},{1,2},{2,1},{3,4},{4,3},{5,6},{6,5},{7,0},{8,15},{9,10},{10,... | collective-permute-start | bytes 196616 | tf_op jit(solution)/shard_map/ppermute | solution.py:756
  71.0 1.6 %collective-permute-start.15 = (f32[2,16,512]{2,1,0:T(8,128)S(1)}, f32[2,16,512]{2,1,0:T(8,128)S(1)}, u32[]{:S(2)}, u32[]{:S(2)}) collective-permute-start(f32[2,16,512]{2,1,0:T(8,128)S(1)} %get-tuple-element.97), channel_id=1, source_target_pairs={{0,1},{1,0},{2,3},{3,2},{4,5},{5,4},{6,7},{7,6},{8,9},{9,8},{10,11... | collective-permute-start | bytes 196616 | tf_op jit(solution)/shard_map/ppermute | solution.py:756
  72.6 4.2 %local3.1 = (f32[32,16,512]{2,1,0:T(8,128)S(1)}, f32[32,16,512]{2,1,0:T(8,128)S(1)}, f32[4,32,128]{2,1,0:T(8,128)S(1)}, f32[4,32,128]{2,1,0:T(8,128)S(1)}, f32[2,16,512]{2,1,0:T(8,128)S(1)}) custom-call(s32[128]{0:T(128)} %bitcast.8, f32[32,16,512]{2,1,0:T(8,128)} %get-tuple-element.84.field_hbm, f32[32,16,512]{2,1,0:T(8,128)} %get-tuple-element.85.field_prev_hbm, ...), custom_call_target="tpu_custom_call" | custom-call | flops 8388608 | bytes 12582912 | tf_op jit(solution)/shard_map/local3/pallas_call | solution.py:677
  76.9 0.8 collective-permute-done.12.x_from_outer
  77.6 1.5 %finish.1 = (f32[32,16,512]{2,1,0:T(8,128)}, f32[32,16,512]{2,1,0:T(8,128)}) custom-call(f32[32,16,512]{2,1,0:T(8,128)S(1)} %get-tuple-element.89.field_in, f32[32,16,512]{2,1,0:T(8,128)S(1)} %get-tuple-element.90.adjoint_in, f32[4,32,128]{2,1,0:T(8,128)S(1)} %get-tuple-element.91.speed_first, f32[4,32,128]{2,1,0:T(8,128)S(1)} %get-tuple-element.92.speed_last, ...), custom_call_target="tpu_custom_call" | custom-call | tf_op jit(solution)/shard_map/finish/pallas_call | solution.py:736
  (26 shorter events, 3.3 us)
Async XLA Ops:
  5.4 26.6 %copy-start = (s32[1,128,1]{1,2,0:T(1,128)S(1)}, s32[1,128,1]{1,2,0:T(1,128)}, u32[]{:S(2)}) copy-start(s32[1,128,1]{1,2,0:T(1,128)} %param.17) | copy-start | bytes 1540
  5.4 26.6 %all-to-all-start = ((f32[128,8,128]{2,1,0:T(8,128)}), f32[128,8,128]{2,1,0:T(8,128)S(1)}, u32[]{:S(2)}, u32[]{:S(2)}) async-start(f32[128,8,128]{2,1,0:T(8,128)} %surface_rows.1), calls=%async_computation | async-start | bytes 1048576 | tf_op jit(solution)/shard_map/all_to_all | solution.py:779
  18.7 13.4 %collective-permute-start = (f32[2,4,32,128]{3,2,1,0:T(8,128)S(1)}, f32[2,4,32,128]{3,2,1,0:T(8,128)S(1)}, u32[]{:S(2)}, u32[]{:S(2)}) collective-permute-start(f32[2,4,32,128]{3,2,1,0:T(8,128)S(1)} %get-tuple-element.54), channel_id=1, source_target_pairs={{0,120},{8,16},{16,8},{24,32},{32,24},{40,48},{48,40},{56,64},{64,... | collective-permute-start | bytes 393224 | tf_op jit(solution)/shard_map/ppermute | solution.py:756
  23.5 8.5 %collective-permute-start.1 = (f32[2,4,32,128]{3,2,1,0:T(8,128)S(1)}, f32[2,4,32,128]{3,2,1,0:T(8,128)S(1)}, u32[]{:S(2)}, u32[]{:S(2)}) collective-permute-start(f32[2,4,32,128]{3,2,1,0:T(8,128)S(1)} %get-tuple-element.55), channel_id=1, source_target_pairs={{0,8},{8,0},{16,24},{24,16},{32,40},{40,32},{48,56},{56,48},{64,72... | collective-permute-start | bytes 393224 | tf_op jit(solution)/shard_map/ppermute | solution.py:756
  23.5 8.5 %collective-permute-start.2 = (f32[2,16,512]{2,1,0:T(8,128)S(1)}, f32[2,16,512]{2,1,0:T(8,128)S(1)}, u32[]{:S(2)}, u32[]{:S(2)}) collective-permute-start(f32[2,16,512]{2,1,0:T(8,128)S(1)} %get-tuple-element.56), channel_id=1, source_target_pairs={{0,7},{1,2},{2,1},{3,4},{4,3},{5,6},{6,5},{7,0},{8,15},{9,10},{10,... | collective-permute-start | bytes 196616 | tf_op jit(solution)/shard_map/ppermute | solution.py:756
  25.5 6.5 %collective-permute-start.3 = (f32[2,16,512]{2,1,0:T(8,128)S(1)}, f32[2,16,512]{2,1,0:T(8,128)S(1)}, u32[]{:S(2)}, u32[]{:S(2)}) collective-permute-start(f32[2,16,512]{2,1,0:T(8,128)S(1)} %get-tuple-element.57), channel_id=1, source_target_pairs={{0,1},{1,0},{2,3},{3,2},{4,5},{5,4},{6,7},{7,6},{8,9},{9,8},{10,11... | collective-permute-start | bytes 196616 | tf_op jit(solution)/shard_map/ppermute | solution.py:756
  35.4 8.5 %collective-permute-start.4 = (f32[2,4,32,128]{3,2,1,0:T(8,128)S(1)}, f32[2,4,32,128]{3,2,1,0:T(8,128)S(1)}, u32[]{:S(2)}, u32[]{:S(2)}) collective-permute-start(f32[2,4,32,128]{3,2,1,0:T(8,128)S(1)} %get-tuple-element.66), channel_id=1, source_target_pairs={{0,120},{8,16},{16,8},{24,32},{32,24},{40,48},{48,40},{56,64},{64,... | collective-permute-start | bytes 393224 | tf_op jit(solution)/shard_map/ppermute | solution.py:756
  36.2 7.7 %collective-permute-start.5 = (f32[2,4,32,128]{3,2,1,0:T(8,128)S(1)}, f32[2,4,32,128]{3,2,1,0:T(8,128)S(1)}, u32[]{:S(2)}, u32[]{:S(2)}) collective-permute-start(f32[2,4,32,128]{3,2,1,0:T(8,128)S(1)} %get-tuple-element.67), channel_id=1, source_target_pairs={{0,8},{8,0},{16,24},{24,16},{32,40},{40,32},{48,56},{56,48},{64,72... | collective-permute-start | bytes 393224 | tf_op jit(solution)/shard_map/ppermute | solution.py:756
  37.0 5.7 %collective-permute-start.6 = (f32[2,16,512]{2,1,0:T(8,128)S(1)}, f32[2,16,512]{2,1,0:T(8,128)S(1)}, u32[]{:S(2)}, u32[]{:S(2)}) collective-permute-start(f32[2,16,512]{2,1,0:T(8,128)S(1)} %get-tuple-element.68), channel_id=1, source_target_pairs={{0,7},{1,2},{2,1},{3,4},{4,3},{5,6},{6,5},{7,0},{8,15},{9,10},{10,... | collective-permute-start | bytes 196616 | tf_op jit(solution)/shard_map/ppermute | solution.py:756
  37.9 4.9 %collective-permute-start.7 = (f32[2,16,512]{2,1,0:T(8,128)S(1)}, f32[2,16,512]{2,1,0:T(8,128)S(1)}, u32[]{:S(2)}, u32[]{:S(2)}) collective-permute-start(f32[2,16,512]{2,1,0:T(8,128)S(1)} %get-tuple-element.69), channel_id=1, source_target_pairs={{0,1},{1,0},{2,3},{3,2},{4,5},{5,4},{6,7},{7,6},{8,9},{9,8},{10,11... | collective-permute-start | bytes 196616 | tf_op jit(solution)/shard_map/ppermute | solution.py:756
  44.6 8.1 %collective-permute-start.8 = (f32[2,4,32,128]{3,2,1,0:T(8,128)S(1)}, f32[2,4,32,128]{3,2,1,0:T(8,128)S(1)}, u32[]{:S(2)}, u32[]{:S(2)}) collective-permute-start(f32[2,4,32,128]{3,2,1,0:T(8,128)S(1)} %get-tuple-element.76), channel_id=1, source_target_pairs={{0,120},{8,16},{16,8},{24,32},{32,24},{40,48},{48,40},{56,64},{64,... | collective-permute-start | bytes 393224 | tf_op jit(solution)/shard_map/ppermute | solution.py:756
  47.2 5.5 %collective-permute-start.9 = (f32[2,4,32,128]{3,2,1,0:T(8,128)S(1)}, f32[2,4,32,128]{3,2,1,0:T(8,128)S(1)}, u32[]{:S(2)}, u32[]{:S(2)}) collective-permute-start(f32[2,4,32,128]{3,2,1,0:T(8,128)S(1)} %get-tuple-element.77), channel_id=1, source_target_pairs={{0,8},{8,0},{16,24},{24,16},{32,40},{40,32},{48,56},{56,48},{64,72... | collective-permute-start | bytes 393224 | tf_op jit(solution)/shard_map/ppermute | solution.py:756
  47.2 5.5 %collective-permute-start.10 = (f32[2,16,512]{2,1,0:T(8,128)S(1)}, f32[2,16,512]{2,1,0:T(8,128)S(1)}, u32[]{:S(2)}, u32[]{:S(2)}) collective-permute-start(f32[2,16,512]{2,1,0:T(8,128)S(1)} %get-tuple-element.78), channel_id=1, source_target_pairs={{0,7},{1,2},{2,1},{3,4},{4,3},{5,6},{6,5},{7,0},{8,15},{9,10},{10,... | collective-permute-start | bytes 196616 | tf_op jit(solution)/shard_map/ppermute | solution.py:756
  48.1 4.6 %collective-permute-start.11 = (f32[2,16,512]{2,1,0:T(8,128)S(1)}, f32[2,16,512]{2,1,0:T(8,128)S(1)}, u32[]{:S(2)}, u32[]{:S(2)}) collective-permute-start(f32[2,16,512]{2,1,0:T(8,128)S(1)} %get-tuple-element.79), channel_id=1, source_target_pairs={{0,1},{1,0},{2,3},{3,2},{4,5},{5,4},{6,7},{7,6},{8,9},{9,8},{10,11... | collective-permute-start | bytes 196616 | tf_op jit(solution)/shard_map/ppermute | solution.py:756
  56.6 22.5 %all-to-all-start.1 = ((f32[128,8,128]{2,1,0:T(8,128)}), f32[128,8,128]{2,1,0:T(8,128)S(1)}, u32[]{:S(2)}, u32[]{:S(2)}) async-start(f32[128,8,128]{2,1,0:T(8,128)} %bitcast.13), calls=%async_computation.1 | async-start | bytes 1048576 | tf_op jit(solution)/shard_map/all_to_all | solution.py:803
  64.1 13.5 %collective-permute-start.12 = (f32[2,4,32,128]{3,2,1,0:T(8,128)S(1)}, f32[2,4,32,128]{3,2,1,0:T(8,128)S(1)}, u32[]{:S(2)}, u32[]{:S(2)}) collective-permute-start(f32[2,4,32,128]{3,2,1,0:T(8,128)S(1)} %get-tuple-element.94), channel_id=1, source_target_pairs={{0,120},{8,16},{16,8},{24,32},{32,24},{40,48},{48,40},{56,64},{64,... | collective-permute-start | bytes 393224 | tf_op jit(solution)/shard_map/ppermute | solution.py:756
  69.0 8.6 %collective-permute-start.13 = (f32[2,4,32,128]{3,2,1,0:T(8,128)S(1)}, f32[2,4,32,128]{3,2,1,0:T(8,128)S(1)}, u32[]{:S(2)}, u32[]{:S(2)}) collective-permute-start(f32[2,4,32,128]{3,2,1,0:T(8,128)S(1)} %get-tuple-element.95), channel_id=1, source_target_pairs={{0,8},{8,0},{16,24},{24,16},{32,40},{40,32},{48,56},{56,48},{64,72... | collective-permute-start | bytes 393224 | tf_op jit(solution)/shard_map/ppermute | solution.py:756
  69.0 7.8 %collective-permute-start.14 = (f32[2,16,512]{2,1,0:T(8,128)S(1)}, f32[2,16,512]{2,1,0:T(8,128)S(1)}, u32[]{:S(2)}, u32[]{:S(2)}) collective-permute-start(f32[2,16,512]{2,1,0:T(8,128)S(1)} %get-tuple-element.96), channel_id=1, source_target_pairs={{0,7},{1,2},{2,1},{3,4},{4,3},{5,6},{6,5},{7,0},{8,15},{9,10},{10,... | collective-permute-start | bytes 196616 | tf_op jit(solution)/shard_map/ppermute | solution.py:756
  71.0 5.9 %collective-permute-start.15 = (f32[2,16,512]{2,1,0:T(8,128)S(1)}, f32[2,16,512]{2,1,0:T(8,128)S(1)}, u32[]{:S(2)}, u32[]{:S(2)}) collective-permute-start(f32[2,16,512]{2,1,0:T(8,128)S(1)} %get-tuple-element.97), channel_id=1, source_target_pairs={{0,1},{1,0},{2,3},{3,2},{4,5},{5,4},{6,7},{7,6},{8,9},{9,8},{10,11... | collective-permute-start | bytes 196616 | tf_op jit(solution)/shard_map/ppermute | solution.py:756

commit v5 on v4

--- a/solution.py
+++ b/solution.py
@@ -11,7 +11,7 @@
 KAPPA = 0.5
 BETA = 0.3
 TERMS = STEPS + 1
-LINES = 8
+LINES = TERMS + 1
 META = TERMS
 MIB = 1 << 20
 VMEM = pltpu.VMEM
@@ -81,9 +81,8 @@
             ]
         rows = [jnp.sum(s, axis=0, keepdims=True) for s in sums]
         scalar_row = jnp.where(lane == 0, patch.astype(jnp.float32), scalars[mat][0:1, :])
-        rows.append(scalar_row)
-        rows.extend([jnp.zeros((1, width), jnp.float32)] * (LINES - len(rows)))
-        out[j] = jnp.concatenate(rows, axis=0)
+        for n, row in enumerate([*rows, scalar_row]):
+            out[pl.ds(LINES * j + n, 1), :] = row
         return carry
 
     sends = shares_of(out, out_hbm, sems, chunks, chunks)
@@ -103,9 +102,9 @@
         surface_kernel,
         in_specs=[pl.BlockSpec(memory_space=HBM)] * 4,
         out_specs=pl.BlockSpec(memory_space=HBM),
-        out_shape=HBM((slots, LINES, width), jnp.float32),
+        out_shape=HBM((slots * LINES, width), jnp.float32),
         scratch_shapes=[
-            pltpu.VMEM((slots, LINES, width), jnp.float32),
+            pltpu.VMEM((slots * LINES, width), jnp.float32),
             pltpu.VMEM((mats, depth, depth), jnp.float32),
             pltpu.SMEM(slot_patch.shape, jnp.int32),
             pltpu.SMEM(patch_material.shape, jnp.int32),
@@ -119,39 +118,54 @@
     )(*in_hbm(layer_maps, slot_patch, patch_material, layer_state))
 
 
-def place(index, cells_x, parts):
-    low, middle = parts.bit_length() - 1, cells_x.bit_length() - 1
-    return (
-        jnp.right_shift(index, low + middle),
-        jnp.bitwise_and(jnp.right_shift(index, low), cells_x - 1),
-        jnp.bitwise_and(index, parts - 1),
-    )
+def bits(index, low, count):
+    return jnp.bitwise_and(jnp.right_shift(index, low), (1 << count) - 1)
+
+
+class Place:
+    def __init__(self, cells_z, cells_x, parts):
+        self.parts, self.x, self.z = (n.bit_length() - 1 for n in (parts, cells_x, cells_z))
+
+    def part(self, index):
+        return bits(index, 0, self.parts)
+
+    def x_of(self, index):
+        return bits(index, self.parts, self.x)
+
+    def x_low(self, index):
+        return bits(index, self.parts, 3)
+
+    def tile(self, index):
+        group = bits(index, self.parts + 3, self.x - 3)
+        return bits(index, self.parts + self.x, self.z), jnp.left_shift(group, 3)
+
+    def z_or_past(self, index):
+        return bits(index, self.parts + self.x, self.z + 1)
 
 
 def pick(rows_ref, fields, picked, tiles):
-    cells_x = fields[0].shape[1]
     slots, width = picked.shape[1:]
-    parts = fields[0].shape[2] // width
+    cells_z, cells_x, along = fields[0].shape
+    place = Place(cells_z, cells_x, along // width)
 
     def fetch(k, carry):
-        z, x, part = place(jnp.maximum(rows_ref[k], 0), cells_x, parts)
-        lines = pl.ds(pl.multiple_of(jnp.bitwise_and(x, -8), 8), 8)
-        lanes = pl.ds(pl.multiple_of(part * width, width), width)
+        index = rows_ref[k]
+        z, first = place.tile(index)
+        lines = pl.ds(pl.multiple_of(first, 8), 8)
+        lanes = pl.ds(pl.multiple_of(place.part(index) * width, width), width)
         for side, field in enumerate(fields):
             tiles[side, pl.ds(pl.multiple_of(8 * k, 8), 8), :] = field[z, lines, lanes]
         return carry
 
-    lax.fori_loop(0, slots, fetch, 0, unroll=8)
+    lax.fori_loop(0, slots, fetch, 0, unroll=16)
 
     def choose(k, carry):
-        index = rows_ref[k]
-        line = 8 * k + jnp.bitwise_and(place(jnp.maximum(index, 0), cells_x, parts)[1], 7)
+        line = 8 * k + place.x_low(rows_ref[k])
         for side in range(len(fields)):
-            row = tiles[side, pl.ds(line, 1), :]
-            picked[side, pl.ds(k, 1), :] = jnp.where(index >= 0, row, 0.0)
+            picked[side, pl.ds(k, 1), :] = tiles[side, pl.ds(line, 1), :]
         return carry
 
-    lax.fori_loop(0, slots, choose, 0, unroll=8)
+    lax.fori_loop(0, slots, choose, 0, unroll=16)
 
 
 def even(axis):
@@ -196,7 +210,7 @@
     z_outer[side], z_inner[side] = outgoing("gz", *z_planes)
 
 
-def edges_kernel(field_hbm, adjoint_hbm, x_outer, x_inner, z_outer, z_inner, field, adjoint, sems):
+def edges_kernel(field_hbm, adjoint_hbm, field, adjoint, x_outer, x_inner, z_outer, z_inner, sems):
     copies = [
         pltpu.make_async_copy(field_hbm, field, sems.at[0]),
         pltpu.make_async_copy(adjoint_hbm, adjoint, sems.at[1]),
@@ -226,30 +240,31 @@
     return pl.pallas_call(
         edges_kernel,
         in_specs=[pl.BlockSpec(memory_space=HBM)] * 2,
-        out_specs=[pl.BlockSpec(memory_space=VMEM)] * 4,
-        out_shape=edge_shapes(field, width),
-        scratch_shapes=[
-            pltpu.VMEM(field.shape, jnp.float32),
-            pltpu.VMEM(field.shape, jnp.float32),
-            pltpu.SemaphoreType.DMA((2,)),
-        ],
+        out_specs=[pl.BlockSpec(memory_space=VMEM)] * 6,
+        out_shape=[jax.ShapeDtypeStruct(field.shape, jnp.float32)] * 2 + edge_shapes(field, width),
+        scratch_shapes=[pltpu.SemaphoreType.DMA((2,))],
         compiler_params=params(8),
         name="edges",
     )(*in_hbm(field, adjoint))
 
 
 def couple(rows_ref, change, coupling):
-    parts, cells_z, cells_x = coupling.shape[0] // 2, coupling.shape[1] - 1, coupling.shape[2]
+    parts, heights, cells_x = coupling.shape[0] // 2, coupling.shape[1], coupling.shape[2]
+    place = Place(heights // 2, cells_x, parts)
 
     def put(k, carry):
         index = rows_ref[k]
-        z, x, part = place(jnp.maximum(index, 0), cells_x, parts)
-        z = jnp.where(index >= 0, z, cells_z)
+        z, x, part = place.z_or_past(index), place.x_of(index), place.part(index)
         for side in range(2):
             coupling[side * parts + part, z, pl.ds(x, 1), :] = change[side, pl.ds(k, 1), :]
         return carry
 
-    lax.fori_loop(0, change.shape[1], put, 0, unroll=8)
+    lax.fori_loop(0, change.shape[1], put, 0, unroll=16)
+
+
+def clear(coupling):
+    heights = coupling.shape[1] // 2
+    coupling[:, :heights] = jnp.zeros((coupling.shape[0], heights, *coupling.shape[2:]), jnp.float32)
 
 
 def local_planes(fields, befores, outs, speed2, extra, sends=None):
@@ -336,10 +351,11 @@
     return jnp.where(row_id == 0, low, jnp.where(row_id == shape[0] - 1, high, 0.0))
 
 
-def border_planes(partials, speed2, halos, outs, edges, extra):
+def border_planes(partials, speed2, halos, outs, edges, extra, arrivals=((),)):
     x_from_outer, x_from_inner, z_from_outer, z_from_inner = halos
     x_outer, x_inner, z_outer, z_inner = edges
     cells_z, cells_x, along = speed2.shape
+    z_halos = [incoming("gz", z_from_outer[side], z_from_inner[side]) for side in range(2)]
 
     def plane(z, side, more):
         first, last = speed2[z, 0:1, :], speed2[z, cells_x - 1 : cells_x, :]
@@ -352,29 +368,34 @@
             new = new + speed2[z] * more
         outs[side][z] = new
         keep_sides(new, side, z, x_outer, x_inner)
-        return new
-
-    for side in range(2):
-        before, after = incoming("gz", z_from_outer[side], z_from_inner[side])
-        ends = plane(0, side, before), plane(cells_z - 1, side, after)
-        keep_edges(ends, side, z_outer, z_inner)
 
     def inner(z, carry):
         for side in range(2):
             plane(z, side, None)
         return carry
 
-    lax.fori_loop(1, cells_z - 1, inner, 0, unroll=UNROLL)
-
-
-def first_local_kernel(rows_hbm, field_hbm, field_prev_hbm, adjoint_hbm, adjoint_prev_hbm, speed2_hbm, out_hbm, adjoint_out_hbm, push, picked, rows_ref, field, field_prev, adjoint, adjoint_prev, speed2, out, adjoint_out, tiles, sems):
+    shares = len(arrivals)
+    share = cells_z // shares
+    for i, copies in enumerate(arrivals):
+        for copy in copies:
+            copy.wait()
+        start, stop = max(i * share, 1), min((i + 1) * share, cells_z - 1)
+        for side in range(2):
+            if i == 0:
+                plane(0, side, z_halos[side][0])
+            if i == shares - 1:
+                plane(cells_z - 1, side, z_halos[side][1])
+        lax.fori_loop(start, stop, inner, 0, unroll=min(stop - start, UNROLL))
+    for side in range(2):
+        keep_edges((outs[side][0], outs[side][cells_z - 1]), side, z_outer, z_inner)
+
+
+def first_local_kernel(rows_hbm, field_prev_hbm, adjoint_prev_hbm, speed2_hbm, field, adjoint, out_hbm, adjoint_out_hbm, push, picked, rows_ref, field_prev, adjoint_prev, speed2, out, adjoint_out, tiles, sems):
     loads = [
         pltpu.make_async_copy(source, target, sems.at[i])
         for i, (source, target) in enumerate(
             (
                 (rows_hbm, rows_ref),
-                (field_hbm, field),
-                (adjoint_hbm, adjoint),
                 (speed2_hbm, speed2),
                 (field_prev_hbm, field_prev),
                 (adjoint_prev_hbm, adjoint_prev),
@@ -383,11 +404,10 @@
     ]
     for copy in loads:
         copy.start()
-    for copy in loads[:3]:
-        copy.wait()
+    loads[0].wait()
     pick(rows_ref, (field, adjoint), picked, tiles)
     push[...] = KAPPA * picked[...]
-    for copy in loads[3:]:
+    for copy in loads[1:]:
         copy.wait()
     sends = list(
         zip(
@@ -411,32 +431,33 @@
     rows_shape = jax.ShapeDtypeStruct((2, slots, width), jnp.float32)
     return pl.pallas_call(
         first_local_kernel,
-        in_specs=[pl.BlockSpec(memory_space=HBM)] * 6,
+        in_specs=[pl.BlockSpec(memory_space=HBM)] * 4 + [pl.BlockSpec(memory_space=VMEM)] * 2,
         out_specs=[pl.BlockSpec(memory_space=HBM)] * 2 + [pl.BlockSpec(memory_space=VMEM)] * 2,
         out_shape=[HBM(field.shape, jnp.float32)] * 2 + [rows_shape] * 2,
         scratch_shapes=[pltpu.SMEM((slots,), jnp.int32)]
-        + [pltpu.VMEM(field.shape, jnp.float32)] * 7
+        + [pltpu.VMEM(field.shape, jnp.float32)] * 5
         + [pltpu.VMEM((2, 8 * slots, width), jnp.float32), pltpu.SemaphoreType.DMA((14,))],
         compiler_params=params(16),
         cost_estimate=pl.CostEstimate(flops=8 << 20, bytes_accessed=12 << 20, transcendentals=0),
         name="local0",
-    )(*in_hbm(rows, field, field_prev, adjoint, adjoint_prev, speed2))
+    )(*in_hbm(rows, field_prev, adjoint_prev, speed2), field, adjoint)
 
 
 def first_border_kernel(rows_ref, partial_hbm, partial_adjoint_hbm, speed2_hbm, x_from_outer, x_from_inner, z_from_outer, z_from_inner, lines_ref, push, picked, out, adjoint_out, speed2, x_outer, x_inner, z_outer, z_inner, surface, partial, partial_adjoint, coupling, change, sems):
+    shares = 4
     loads = [
-        pltpu.make_async_copy(source, target, sems.at[i])
+        shares_of(source, target, sems, shares * i, shares)
         for i, (source, target) in enumerate(
             ((speed2_hbm, speed2), (partial_hbm, partial), (partial_adjoint_hbm, partial_adjoint))
         )
     ]
-    for copy in loads:
-        copy.start()
-    coupling[...] = jnp.zeros_like(coupling)
+    arrivals = [[copies[i] for copies in loads] for i in range(shares)]
+    for copies in arrivals:
+        for copy in copies:
+            copy.start()
+    clear(coupling)
     lines = Lines(lines_ref, change.shape[1])
     couple_step(rows_ref, lines, 0, [push], picked, surface, change, coupling)
-    for copy in loads:
-        copy.wait()
     border_planes(
         (partial, partial_adjoint),
         speed2,
@@ -444,13 +465,14 @@
         (out, adjoint_out),
         (x_outer, x_inner, z_outer, z_inner),
         functools.partial(extra_of, coupling),
+        arrivals,
     )
 
 
 def coupling_scratch(field, slots, width):
     cells_z, cells_x, along = field.shape
     return [
-        pltpu.VMEM((2 * (along // width), cells_z + 1, cells_x, width), jnp.float32),
+        pltpu.VMEM((2 * (along // width), 2 * cells_z, cells_x, width), jnp.float32),
         pltpu.VMEM((2, slots, width), jnp.float32),
     ]
 
@@ -471,15 +493,25 @@
         + [jax.ShapeDtypeStruct((2, slots, width), jnp.float32)],
         scratch_shapes=[pltpu.VMEM(field.shape, jnp.float32)] * 2
         + coupling_scratch(field, slots, width)
-        + [pltpu.SemaphoreType.DMA((3,))],
-        compiler_params=params(12),
+        + [pltpu.SemaphoreType.DMA((12,))],
+        compiler_params=params(14),
         name="border0",
     )(rows, *in_hbm(*partials, speed2), *halos, lines, push, picked)
 
 
 def local_kernel(step, rows_ref, field, field_prev, adjoint, adjoint_prev, speed2, lines_ref, surface, *refs):
     pushes, refs = list(refs[:step]), refs[step:]
-    out, adjoint_out, push, next_surface, coupling, change, tiles, picked = refs[:8]
+    out, adjoint_out, push, next_surface = refs[:4]
+    sends = []
+    if step == STEPS - 2:
+        sends = [
+            pltpu.make_async_copy(source, target, refs[-1].at[i])
+            for i, (source, target) in enumerate(zip((field, adjoint), refs[4:6]))
+        ]
+        refs = refs[:4] + refs[6:-1]
+    for send in sends:
+        send.start()
+    coupling, change, tiles, picked = refs[4:8]
     loads = []
     if step == 1:
         *held, sems = refs[8:]
@@ -492,7 +524,7 @@
         copy.start()
     pick(rows_ref, (field, adjoint), picked, tiles)
     push[...] = KAPPA * (picked[...] - surface[...])
-    coupling[...] = jnp.zeros_like(coupling)
+    clear(coupling)
     lines = Lines(lines_ref, change.shape[1])
     couple_step(rows_ref, lines, step, pushes + [push], picked, next_surface, change, coupling)
     for copy in loads:
@@ -504,6 +536,8 @@
         speed2,
         functools.partial(extra_of, coupling),
     )
+    for send in sends:
+        send.wait()
 
 
 def local_step(step, rows, field, field_prev, adjoint, adjoint_prev, speed2, lines, surface, pushes):
@@ -511,7 +545,10 @@
     whole = jax.ShapeDtypeStruct(field.shape, jnp.float32)
     rows_shape = jax.ShapeDtypeStruct(surface.shape, jnp.float32)
     in_vmem = pl.BlockSpec(memory_space=VMEM)
-    before, held = in_vmem, []
+    before, held, kept = in_vmem, [], []
+    if step == STEPS - 2:
+        kept = [HBM(field.shape, jnp.float32)] * 2
+        held = [pltpu.SemaphoreType.DMA((2,))]
     if step == 1:
         before = pl.BlockSpec(memory_space=HBM)
         held = [pltpu.VMEM(field.shape, jnp.float32)] * 2 + [pltpu.SemaphoreType.DMA((2,))]
@@ -520,15 +557,15 @@
         functools.partial(local_kernel, step),
         in_specs=[pl.BlockSpec(memory_space=SMEM), in_vmem, before, in_vmem, before]
         + [in_vmem] * (3 + step),
-        out_specs=[in_vmem] * 4,
-        out_shape=[whole, whole, rows_shape, rows_shape],
+        out_specs=[in_vmem] * 4 + [pl.BlockSpec(memory_space=HBM)] * len(kept),
+        out_shape=[whole, whole, rows_shape, rows_shape, *kept],
         scratch_shapes=coupling_scratch(field, slots, width)
         + [
             pltpu.VMEM((2, 8 * slots, width), jnp.float32),
             pltpu.VMEM((2, slots, width), jnp.float32),
         ]
         + held,
-        compiler_params=params(10),
+        compiler_params=params(12),
         cost_estimate=pl.CostEstimate(flops=8 << 20, bytes_accessed=12 << 20, transcendentals=0),
         name=f"local{step}",
     )(rows, field, field_prev, adjoint, adjoint_prev, speed2, lines, surface, *pushes)
@@ -559,15 +596,13 @@
     )(*partials, speed2, *halos)
 
 
-def correlation_kernel(rows_ref, field, field_prev, adjoint, adjoint_prev, lines_ref, surface, *refs):
+def correlation_kernel(rows_ref, used, field, adjoint, lines_ref, surface, *refs):
     pushes, refs = list(refs[: STEPS - 1]), refs[STEPS - 1 :]
     gradient_hbm, change = refs[:2]
-    targets, (gradient, tiles, picked, push, sems) = refs[2:6], refs[6:]
+    targets, (gradient, tiles, picked, push, sems) = refs[2:4], refs[4:]
     sends = [
         pltpu.make_async_copy(source, target, sems.at[i])
-        for i, (source, target) in enumerate(
-            zip((field, field_prev, adjoint, adjoint_prev), targets)
-        )
+        for i, (source, target) in enumerate(zip((field, adjoint), targets))
     ]
     for send in sends:
         send.start()
@@ -590,6 +625,7 @@
         parts.append(rest.astype(jnp.bfloat16))
         rest = rest - parts[-1].astype(jnp.float32)
     ids = lines.meta.T[0:1, :].astype(jnp.int32)
+    ids = jnp.where(used[...] >= 0, ids, -1)
     owners = lax.broadcasted_iota(jnp.int32, (patches, slots), 0) == ids
     sums = jnp.dot(
         jnp.where(owners, 1.0, 0.0).astype(jnp.bfloat16),
@@ -597,7 +633,7 @@
         preferred_element_type=jnp.float32,
     )
     gradient[...] = sums[:, :width] + (sums[:, width : 2 * width] + sums[:, 2 * width :])
-    sends.append(pltpu.make_async_copy(gradient, gradient_hbm, sems.at[4]))
+    sends.append(pltpu.make_async_copy(gradient, gradient_hbm, sems.at[2]))
     sends[-1].start()
 
     for side in range(2):
@@ -606,28 +642,28 @@
         send.wait()
 
 
-def correlate(rows, field, field_prev, adjoint, adjoint_prev, lines, surface, pushes, patches):
+def correlate(rows, field, adjoint, lines, surface, pushes, patches):
     _, slots, width = surface.shape
     f32 = jnp.float32
     in_vmem = pl.BlockSpec(memory_space=VMEM)
     return pl.pallas_call(
         correlation_kernel,
-        in_specs=[pl.BlockSpec(memory_space=SMEM)] + [in_vmem] * (6 + len(pushes)),
-        out_specs=[pl.BlockSpec(memory_space=HBM), in_vmem] + [pl.BlockSpec(memory_space=HBM)] * 4,
+        in_specs=[pl.BlockSpec(memory_space=SMEM)] + [in_vmem] * (5 + len(pushes)),
+        out_specs=[pl.BlockSpec(memory_space=HBM), in_vmem] + [pl.BlockSpec(memory_space=HBM)] * 2,
         out_shape=[
             HBM((patches, width), f32),
             jax.ShapeDtypeStruct(surface.shape, f32),
         ]
-        + [HBM(field.shape, f32)] * 4,
+        + [HBM(field.shape, f32)] * 2,
         scratch_shapes=[
             pltpu.VMEM((patches, width), f32),
             pltpu.VMEM((2, 8 * slots, width), f32),
         ]
         + [pltpu.VMEM((2, slots, width), f32)] * 2
-        + [pltpu.SemaphoreType.DMA((5,))],
+        + [pltpu.SemaphoreType.DMA((3,))],
         compiler_params=params(10),
         name="correlation",
-    )(rows, field, field_prev, adjoint, adjoint_prev, lines, surface, *pushes)
+    )(rows, rows.reshape(1, slots), field, adjoint, lines, surface, *pushes)
 
 
 def last_local_kernel(rows_hbm, field_hbm, field_prev_hbm, adjoint_hbm, adjoint_prev_hbm, speed2_hbm, change, out, adjoint_out, speed_first, speed_last, speed_ends, rows_ref, field, field_prev, adjoint, adjoint_prev, speed2, coupling, sems):
@@ -646,7 +682,7 @@
     ]
     for copy in loads:
         copy.start()
-    coupling[...] = jnp.zeros_like(coupling)
+    clear(coupling)
     loads[0].wait()
     couple(rows_ref, change, coupling)
     loads[1].wait()
@@ -773,14 +809,15 @@
     devices = lax.axis_size(("gx", "gz"))
     rows = send_rows.reshape(-1)
 
-    edges = first_edges(pressure_now, adjoint_now, width)
+    field, adjoint, *edges = first_edges(pressure_now, adjoint_now, width)
     halos = exchange(edges)
     lines = surface_rows(layer_maps, slot_patch, patch_material, layer_state)
+    lines = lines.reshape(slots, 1, LINES * width)
     lines = lax.all_to_all(lines, ("gx", "gz"), split_axis=0, concat_axis=0, tiled=True)
     lines = lines.reshape(slots * LINES, width)
 
     *partials, push, picked = first_local(
-        rows, pressure_now, pressure_prev, adjoint_now, adjoint_prev, speed2, slots, width
+        rows, field, pressure_prev, adjoint, adjoint_prev, speed2, slots, width
     )
     pushes = [push]
     field, adjoint, speed, *edges, surface = first_border(
@@ -789,19 +826,22 @@
     field_prev, adjoint_prev = pressure_now, adjoint_now
     for step in range(1, STEPS - 1):
         halos = exchange(edges)
-        *partials, push, surface = local_step(
+        field_next, adjoint_next, push, surface, *sent = local_step(
             step, rows, field, field_prev, adjoint, adjoint_prev, speed, lines, surface, pushes
         )
+        partials = (field_next, adjoint_next)
         pushes.append(push)
         field_prev, adjoint_prev = field, adjoint
         field, adjoint, *edges = border_step(step, partials, speed, halos, width)
     halos = exchange(edges)
     gradient, change, *held = correlate(
-        rows, field, field_prev, adjoint, adjoint_prev, lines, surface, pushes, patches
+        rows, field, adjoint, lines, surface, pushes, patches
     )
     parts = gradient.reshape(devices, patches // devices, width)
     parts = lax.all_to_all(parts, ("gx", "gz"), split_axis=0, concat_axis=0, tiled=True)
-    *partials, first, last, ends = last_local(rows, *held, speed2, change)
+    *partials, first, last, ends = last_local(
+        rows, held[0], sent[0], held[1], sent[1], speed2, change
+    )
     field, adjoint = finish_call(*partials, first, last, ends, halos)
     return field, adjoint, jnp.sum(parts, axis=0)
 

time: 80.1 us -> 77.8 us (0.971)
  Pallas kernels: 33.2 us -> 30.4 us
    pallas_call x2, Pallas kernels: 8.35 us -> 7.4 us  [local_step(): pl.pallas_call(functools.partial(local_kernel, step), in_specs=[pl.BlockS...]
    pallas_call x1, Pallas kernels: 4.87 us -> 4.05 us  [first_local(): pl.pallas_call(first_local_kernel, in_specs=[pl.BlockSpec(memory_space=HB...]
  transfers between devices with their start and end apart: 18 -> 18, of which waited for: 2 -> 3; matrix products, arithmetic and copies ran while one was open for 0% -> 0% of each run, Pallas kernels for 26% -> 24%
where the time goes in v5:
time: 77.8 us; the launch traced here: 77.5 us
  starting transfers between devices  43.5 us (56%)
  Pallas kernels  30.4 us (39%)
  waiting for transfers between devices  1.97 us (3%)
  between operations  0.86 us (1%)
    ppermute x16, starting transfers between devices, exchange(): lax.ppermute(edge, axis, swaps(axis, first))  24.6 us
    all_to_all x1, starting transfers between devices, body(): lax.all_to_all(lines, ('gx', 'gz'), split_axis=0, concat_axis=0, tiled=True)  11.5 us
    all_to_all x1, starting transfers between devices, body(): lax.all_to_all(parts, ('gx', 'gz'), split_axis=0, concat_axis=0, tiled=True)  7.45 us
    pallas_call x2, Pallas kernels, local_step(): pl.pallas_call(functools.partial(local_kernel, step), in_specs=[pl.BlockS...  7.4 us
    pallas_call x1, Pallas kernels, surface_rows(): pl.pallas_call(surface_kernel, in_specs=[pl.BlockSpec(memory_space=HBM)]...  4.73 us
    pallas_call x1, Pallas kernels, last_local(): pl.pallas_call(last_local_kernel, in_specs=[pl.BlockSpec(memory_space=HBM...  4.15 us
    pallas_call x1, Pallas kernels, first_local(): pl.pallas_call(first_local_kernel, in_specs=[pl.BlockSpec(memory_space=HB...  4.05 us
    pallas_call x1, Pallas kernels, correlate(): pl.pallas_call(correlation_kernel, in_specs=[pl.BlockSpec(memory_space=SM...  2.83 us
  transfers between devices with their start and end apart: 18, of which 3 were waited for; matrix products, arithmetic and copies ran while one was open for 0% of the time, Pallas kernels for 24%

profile of v5, /device:TPU:1, one launch (start us, length us, event | category | flops | bytes accessed | tf_op | source)
XLA Modules:
  0.0 77.5 jit_solution(479874690567743625)
XLA Ops:
  0.6 4.7 %surface_rows.1 = f32[768,128]{1,0:T(8,128)} custom-call(f32[8,64,64]{2,1,0:T(8,128)} %maps_hbm.1, s32[128]{0:T(128)} %patch_hbm.1, s32[1024]{0:T(1024)} %material_hbm.1, f32[128,64,128]{2,1,0:T(8,128)} %layer_hbm.1), custom_call_target="tpu_custom_call" | custom-call | tf_op jit(solution)/shard_map/surface_rows/pallas_call | solution.py:101
  5.4 11.5 %all-to-all-start = ((f32[128,1,768]{2,1,0:T(1,128)}), f32[128,1,768]{2,1,0:T(1,128)S(1)}, u32[]{:S(2)}, u32[]{:S(2)}) async-start(f32[128,1,768]{2,1,0:T(1,128)} %bitcast.16), calls=%async_computation | async-start | bytes 786432 | tf_op jit(solution)/shard_map/all_to_all | solution.py:816
  16.9 1.7 %edges.1 = (f32[32,16,512]{2,1,0:T(8,128)S(1)}, f32[32,16,512]{2,1,0:T(8,128)S(1)}, f32[2,4,32,128]{3,2,1,0:T(8,128)S(1)}, f32[2,4,32,128]{3,2,1,0:T(8,128)S(1)}...) custom-call(f32[32,16,512]{2,1,0:T(8,128)} %field_prev.1, f32[32,16,512]{2,1,0:T(8,128)} %adjoint_prev.1), custom_call_target="tpu_custom_call" | custom-call | tf_op jit(solution)/shard_map/edges/pallas_call | solution.py:240
  18.6 4.9 %collective-permute-start = (f32[2,4,32,128]{3,2,1,0:T(8,128)S(1)}, f32[2,4,32,128]{3,2,1,0:T(8,128)S(1)}, u32[]{:S(2)}, u32[]{:S(2)}) collective-permute-start(f32[2,4,32,128]{3,2,1,0:T(8,128)S(1)} %get-tuple-element.58), channel_id=1, source_target_pairs={{0,120},{8,16},{16,8},{24,32},{32,24},{40,48},{48,40},{56,64},{64,... | collective-permute-start | bytes 393224 | tf_op jit(solution)/shard_map/ppermute | solution.py:792
  23.5 2.0 %collective-permute-start.2 = (f32[2,16,512]{2,1,0:T(8,128)S(1)}, f32[2,16,512]{2,1,0:T(8,128)S(1)}, u32[]{:S(2)}, u32[]{:S(2)}) collective-permute-start(f32[2,16,512]{2,1,0:T(8,128)S(1)} %get-tuple-element.60), channel_id=1, source_target_pairs={{0,7},{1,2},{2,1},{3,4},{4,3},{5,6},{6,5},{7,0},{8,15},{9,10},{10,... | collective-permute-start | bytes 196616 | tf_op jit(solution)/shard_map/ppermute | solution.py:792
  25.5 1.6 %collective-permute-start.3 = (f32[2,16,512]{2,1,0:T(8,128)S(1)}, f32[2,16,512]{2,1,0:T(8,128)S(1)}, u32[]{:S(2)}, u32[]{:S(2)}) collective-permute-start(f32[2,16,512]{2,1,0:T(8,128)S(1)} %get-tuple-element.61), channel_id=1, source_target_pairs={{0,1},{1,0},{2,3},{3,2},{4,5},{5,4},{6,7},{7,6},{8,9},{9,8},{10,11... | collective-permute-start | bytes 196616 | tf_op jit(solution)/shard_map/ppermute | solution.py:792
  27.1 4.1 %local0.1 = (f32[32,16,512]{2,1,0:T(8,128)}, f32[32,16,512]{2,1,0:T(8,128)}, f32[2,128,128]{2,1,0:T(8,128)S(1)}, f32[2,128,128]{2,1,0:T(8,128)S(1)}) custom-call(s32[128]{0:T(128)} %bitcast.9, f32[32,16,512]{2,1,0:T(8,128)} %field_prev_hbm.1, f32[32,16,512]{2,1,0:T(8,128)} %adjoint_prev_hbm.1, f32[32,16,512]{2,1,0:T(8,128)} %speed2_hbm.5, ...), custom_call_target="tpu_custom_call" | custom-call | flops 8388608 | bytes 12582912 | tf_op jit(solution)/shard_map/local0/pallas_call | solution.py:432
  31.2 2.7 %border0.1 = (f32[32,16,512]{2,1,0:T(8,128)S(1)}, f32[32,16,512]{2,1,0:T(8,128)S(1)}, f32[32,16,512]{2,1,0:T(8,128)S(1)}, f32[2,4,32,128]{3,2,1,0:T(8,128)S(1)},...) custom-call(s32[128]{0:T(128)S(1)} %bitcast.11, ...), custom_call_target="tpu_custom_call" | custom-call | tf_op jit(solution)/shard_map/border0/pallas_call | solution.py:485
  33.9 0.8 %collective-permute-start.4 = (f32[2,4,32,128]{3,2,1,0:T(8,128)S(1)}, f32[2,4,32,128]{3,2,1,0:T(8,128)S(1)}, u32[]{:S(2)}, u32[]{:S(2)}) collective-permute-start(f32[2,4,32,128]{3,2,1,0:T(8,128)S(1)} %get-tuple-element.70), channel_id=1, source_target_pairs={{0,120},{8,16},{16,8},{24,32},{32,24},{40,48},{48,40},{56,64},{64,... | collective-permute-start | bytes 393224 | tf_op jit(solution)/shard_map/ppermute | solution.py:792
  34.7 0.8 %collective-permute-start.5 = (f32[2,4,32,128]{3,2,1,0:T(8,128)S(1)}, f32[2,4,32,128]{3,2,1,0:T(8,128)S(1)}, u32[]{:S(2)}, u32[]{:S(2)}) collective-permute-start(f32[2,4,32,128]{3,2,1,0:T(8,128)S(1)} %get-tuple-element.71), channel_id=1, source_target_pairs={{0,8},{8,0},{16,24},{24,16},{32,40},{40,32},{48,56},{56,48},{64,72... | collective-permute-start | bytes 393224 | tf_op jit(solution)/shard_map/ppermute | solution.py:792
  35.5 1.6 %collective-permute-start.6 = (f32[2,16,512]{2,1,0:T(8,128)S(1)}, f32[2,16,512]{2,1,0:T(8,128)S(1)}, u32[]{:S(2)}, u32[]{:S(2)}) collective-permute-start(f32[2,16,512]{2,1,0:T(8,128)S(1)} %get-tuple-element.72), channel_id=1, source_target_pairs={{0,7},{1,2},{2,1},{3,4},{4,3},{5,6},{6,5},{7,0},{8,15},{9,10},{10,... | collective-permute-start | bytes 196616 | tf_op jit(solution)/shard_map/ppermute | solution.py:792
  37.1 0.8 %collective-permute-start.7 = (f32[2,16,512]{2,1,0:T(8,128)S(1)}, f32[2,16,512]{2,1,0:T(8,128)S(1)}, u32[]{:S(2)}, u32[]{:S(2)}) collective-permute-start(f32[2,16,512]{2,1,0:T(8,128)S(1)} %get-tuple-element.73), channel_id=1, source_target_pairs={{0,1},{1,0},{2,3},{3,2},{4,5},{5,4},{6,7},{7,6},{8,9},{9,8},{10,11... | collective-permute-start | bytes 196616 | tf_op jit(solution)/shard_map/ppermute | solution.py:792
  37.9 3.7 %local1.1 = (f32[32,16,512]{2,1,0:T(8,128)S(1)}, f32[32,16,512]{2,1,0:T(8,128)S(1)}, f32[2,128,128]{2,1,0:T(8,128)S(1)}, f32[2,128,128]{2,1,0:T(8,128)S(1)}) custom-call(s32[128]{0:T(128)S(1)} %bitcast.12, f32[32,16,512]{2,1,0:T(8,128)S(1)} %get-tuple-element.64.field.field_prev, f32[32,16,512]{2,1,0:T(8,128)} %field_prev.1, ...), custom_call_target="tpu_custom_call" | custom-call | flops 8388608 | bytes 12582912 | tf_op jit(solution)/shard_map/local1/pallas_call | solution.py:556
  41.6 0.8 %collective-permute-done.4.x_from_outer = f32[2,4,32,128]{3,2,1,0:T(8,128)S(1)} collective-permute-done((f32[2,4,32,128]{3,2,1,0:T(8,128)S(1)}, f32[2,4,32,128]{3,2,1,0:T(8,128)S(1)}, u32[]{:S(2)}, u32[]{:S(2)}) %collective-permute-start.4) | collective-permute-done | bytes 131104 | tf_op jit(solution)/shard_map/ppermute | solution.py:792
  43.2 1.5 %collective-permute-start.8 = (f32[2,4,32,128]{3,2,1,0:T(8,128)S(1)}, f32[2,4,32,128]{3,2,1,0:T(8,128)S(1)}, u32[]{:S(2)}, u32[]{:S(2)}) collective-permute-start(f32[2,4,32,128]{3,2,1,0:T(8,128)S(1)} %get-tuple-element.80), channel_id=1, source_target_pairs={{0,120},{8,16},{16,8},{24,32},{32,24},{40,48},{48,40},{56,64},{64,... | collective-permute-start | bytes 393224 | tf_op jit(solution)/shard_map/ppermute | solution.py:792
  44.7 1.6 %collective-permute-start.10 = (f32[2,16,512]{2,1,0:T(8,128)S(1)}, f32[2,16,512]{2,1,0:T(8,128)S(1)}, u32[]{:S(2)}, u32[]{:S(2)}) collective-permute-start(f32[2,16,512]{2,1,0:T(8,128)S(1)} %get-tuple-element.82), channel_id=1, source_target_pairs={{0,7},{1,2},{2,1},{3,4},{4,3},{5,6},{6,5},{7,0},{8,15},{9,10},{10,... | collective-permute-start | bytes 196616 | tf_op jit(solution)/shard_map/ppermute | solution.py:792
  46.6 3.7 %local2.1 = (f32[32,16,512]{2,1,0:T(8,128)S(1)}, f32[32,16,512]{2,1,0:T(8,128)S(1)}, f32[2,128,128]{2,1,0:T(8,128)S(1)}, f32[2,128,128]{2,1,0:T(8,128)S(1)}, f32...) custom-call(s32[128]{0:T(128)S(1)} %bitcast.13, f32[32,16,512]{2,1,0:T(8,128)S(1)} %get-tuple-element.74.field, ...), custom_call_target="tpu_custom_call" | custom-call | flops 8388608 | bytes 12582912 | tf_op jit(solution)/shard_map/local2/pallas_call | solution.py:556
  51.5 2.8 %correlation.1 = (f32[1024,128]{1,0:T(8,128)}, f32[2,128,128]{2,1,0:T(8,128)S(1)}, f32[32,16,512]{2,1,0:T(8,128)}, f32[32,16,512]{2,1,0:T(8,128)}) custom-call(s32[128]{0:T(128)S(1)} %bitcast.14, s32[1,128]{1,0:T(1,128)S(1)} %bitcast.15, f32[32,16,512]{2,1,0:T(8,128)S(1)} %get-tuple-element.84.field, f32[32,16,512]{2,1,0:T(8,128)S(1)} %get-tuple-element.85.adjoint, ...), custom_call_target="tpu_custom_call" | custom-call | tf_op jit(solution)/shard_map/correlation/pallas_call | solution.py:649
  54.4 7.5 %all-to-all-start.1 = ((f32[128,8,128]{2,1,0:T(8,128)}), f32[128,8,128]{2,1,0:T(8,128)S(1)}, u32[]{:S(2)}, u32[]{:S(2)}) async-start(f32[128,8,128]{2,1,0:T(8,128)} %bitcast.17), calls=%async_computation.1 | async-start | bytes 1048576 | tf_op jit(solution)/shard_map/all_to_all | solution.py:841
  61.8 5.1 %collective-permute-start.12 = (f32[2,4,32,128]{3,2,1,0:T(8,128)S(1)}, f32[2,4,32,128]{3,2,1,0:T(8,128)S(1)}, u32[]{:S(2)}, u32[]{:S(2)}) collective-permute-start(f32[2,4,32,128]{3,2,1,0:T(8,128)S(1)} %get-tuple-element.98), channel_id=1, source_target_pairs={{0,120},{8,16},{16,8},{24,32},{32,24},{40,48},{48,40},{56,64},{64,... | collective-permute-start | bytes 393224 | tf_op jit(solution)/shard_map/ppermute | solution.py:792
  66.9 2.0 %collective-permute-start.14 = (f32[2,16,512]{2,1,0:T(8,128)S(1)}, f32[2,16,512]{2,1,0:T(8,128)S(1)}, u32[]{:S(2)}, u32[]{:S(2)}) collective-permute-start(f32[2,16,512]{2,1,0:T(8,128)S(1)} %get-tuple-element.100), channel_id=1, source_target_pairs={{0,7},{1,2},{2,1},{3,4},{4,3},{5,6},{6,5},{7,0},{8,15},{9,10},{10,... | collective-permute-start | bytes 196616 | tf_op jit(solution)/shard_map/ppermute | solution.py:792
  68.9 1.6 %collective-permute-start.15 = (f32[2,16,512]{2,1,0:T(8,128)S(1)}, f32[2,16,512]{2,1,0:T(8,128)S(1)}, u32[]{:S(2)}, u32[]{:S(2)}) collective-permute-start(f32[2,16,512]{2,1,0:T(8,128)S(1)} %get-tuple-element.101), channel_id=1, source_target_pairs={{0,1},{1,0},{2,3},{3,2},{4,5},{5,4},{6,7},{7,6},{8,9},{9,8},{10,11... | collective-permute-start | bytes 196616 | tf_op jit(solution)/shard_map/ppermute | solution.py:792
  70.5 4.1 %local3.1 = (f32[32,16,512]{2,1,0:T(8,128)S(1)}, f32[32,16,512]{2,1,0:T(8,128)S(1)}, f32[4,32,128]{2,1,0:T(8,128)S(1)}, f32[4,32,128]{2,1,0:T(8,128)S(1)}, f32[2,16,512]{2,1,0:T(8,128)S(1)}) custom-call(s32[128]{0:T(128)} %bitcast.10, f32[32,16,512]{2,1,0:T(8,128)} %get-tuple-element.88.field_hbm, f32[32,16,512]{2,1,0:T(8,128)} %get-tuple-element.89.field_prev_hbm, ...), custom_call_target="tpu_custom_call" | custom-call | flops 8388608 | bytes 12582912 | tf_op jit(solution)/shard_map/local3/pallas_call | solution.py:713
  75.3 1.5 %finish.1 = (f32[32,16,512]{2,1,0:T(8,128)}, f32[32,16,512]{2,1,0:T(8,128)}) custom-call(f32[32,16,512]{2,1,0:T(8,128)S(1)} %get-tuple-element.93.field_in, f32[32,16,512]{2,1,0:T(8,128)S(1)} %get-tuple-element.94.adjoint_in, f32[4,32,128]{2,1,0:T(8,128)S(1)} %get-tuple-element.95.speed_first, f32[4,32,128]{2,1,0:T(8,128)S(1)} %get-tuple-element.96.speed_last, ...), custom_call_target="tpu_custom_call" | custom-call | tf_op jit(solution)/shard_map/finish/pallas_call | solution.py:772
  (26 shorter events, 3.7 us)
Async XLA Ops:
  5.4 25.8 %copy-start = (s32[1,128,1]{1,2,0:T(1,128)S(1)}, s32[1,128,1]{1,2,0:T(1,128)}, u32[]{:S(2)}) copy-start(s32[1,128,1]{1,2,0:T(1,128)} %param.17) | copy-start | bytes 1540
  5.4 25.8 %all-to-all-start = ((f32[128,1,768]{2,1,0:T(1,128)}), f32[128,1,768]{2,1,0:T(1,128)S(1)}, u32[]{:S(2)}, u32[]{:S(2)}) async-start(f32[128,1,768]{2,1,0:T(1,128)} %bitcast.16), calls=%async_computation | async-start | bytes 786432 | tf_op jit(solution)/shard_map/all_to_all | solution.py:816
  18.6 12.6 %collective-permute-start = (f32[2,4,32,128]{3,2,1,0:T(8,128)S(1)}, f32[2,4,32,128]{3,2,1,0:T(8,128)S(1)}, u32[]{:S(2)}, u32[]{:S(2)}) collective-permute-start(f32[2,4,32,128]{3,2,1,0:T(8,128)S(1)} %get-tuple-element.58), channel_id=1, source_target_pairs={{0,120},{8,16},{16,8},{24,32},{32,24},{40,48},{48,40},{56,64},{64,... | collective-permute-start | bytes 393224 | tf_op jit(solution)/shard_map/ppermute | solution.py:792
  23.5 7.7 %collective-permute-start.1 = (f32[2,4,32,128]{3,2,1,0:T(8,128)S(1)}, f32[2,4,32,128]{3,2,1,0:T(8,128)S(1)}, u32[]{:S(2)}, u32[]{:S(2)}) collective-permute-start(f32[2,4,32,128]{3,2,1,0:T(8,128)S(1)} %get-tuple-element.59), channel_id=1, source_target_pairs={{0,8},{8,0},{16,24},{24,16},{32,40},{40,32},{48,56},{56,48},{64,72... | collective-permute-start | bytes 393224 | tf_op jit(solution)/shard_map/ppermute | solution.py:792
  23.5 7.7 %collective-permute-start.2 = (f32[2,16,512]{2,1,0:T(8,128)S(1)}, f32[2,16,512]{2,1,0:T(8,128)S(1)}, u32[]{:S(2)}, u32[]{:S(2)}) collective-permute-start(f32[2,16,512]{2,1,0:T(8,128)S(1)} %get-tuple-element.60), channel_id=1, source_target_pairs={{0,7},{1,2},{2,1},{3,4},{4,3},{5,6},{6,5},{7,0},{8,15},{9,10},{10,... | collective-permute-start | bytes 196616 | tf_op jit(solution)/shard_map/ppermute | solution.py:792
  25.5 5.7 %collective-permute-start.3 = (f32[2,16,512]{2,1,0:T(8,128)S(1)}, f32[2,16,512]{2,1,0:T(8,128)S(1)}, u32[]{:S(2)}, u32[]{:S(2)}) collective-permute-start(f32[2,16,512]{2,1,0:T(8,128)S(1)} %get-tuple-element.61), channel_id=1, source_target_pairs={{0,1},{1,0},{2,3},{3,2},{4,5},{5,4},{6,7},{7,6},{8,9},{9,8},{10,11... | collective-permute-start | bytes 196616 | tf_op jit(solution)/shard_map/ppermute | solution.py:792
  33.9 8.5 %collective-permute-start.4 = (f32[2,4,32,128]{3,2,1,0:T(8,128)S(1)}, f32[2,4,32,128]{3,2,1,0:T(8,128)S(1)}, u32[]{:S(2)}, u32[]{:S(2)}) collective-permute-start(f32[2,4,32,128]{3,2,1,0:T(8,128)S(1)} %get-tuple-element.70), channel_id=1, source_target_pairs={{0,120},{8,16},{16,8},{24,32},{32,24},{40,48},{48,40},{56,64},{64,... | collective-permute-start | bytes 393224 | tf_op jit(solution)/shard_map/ppermute | solution.py:792
  34.7 7.7 %collective-permute-start.5 = (f32[2,4,32,128]{3,2,1,0:T(8,128)S(1)}, f32[2,4,32,128]{3,2,1,0:T(8,128)S(1)}, u32[]{:S(2)}, u32[]{:S(2)}) collective-permute-start(f32[2,4,32,128]{3,2,1,0:T(8,128)S(1)} %get-tuple-element.71), channel_id=1, source_target_pairs={{0,8},{8,0},{16,24},{24,16},{32,40},{40,32},{48,56},{56,48},{64,72... | collective-permute-start | bytes 393224 | tf_op jit(solution)/shard_map/ppermute | solution.py:792
  35.5 6.1 %collective-permute-start.6 = (f32[2,16,512]{2,1,0:T(8,128)S(1)}, f32[2,16,512]{2,1,0:T(8,128)S(1)}, u32[]{:S(2)}, u32[]{:S(2)}) collective-permute-start(f32[2,16,512]{2,1,0:T(8,128)S(1)} %get-tuple-element.72), channel_id=1, source_target_pairs={{0,7},{1,2},{2,1},{3,4},{4,3},{5,6},{6,5},{7,0},{8,15},{9,10},{10,... | collective-permute-start | bytes 196616 | tf_op jit(solution)/shard_map/ppermute | solution.py:792
  37.1 4.5 %collective-permute-start.7 = (f32[2,16,512]{2,1,0:T(8,128)S(1)}, f32[2,16,512]{2,1,0:T(8,128)S(1)}, u32[]{:S(2)}, u32[]{:S(2)}) collective-permute-start(f32[2,16,512]{2,1,0:T(8,128)S(1)} %get-tuple-element.73), channel_id=1, source_target_pairs={{0,1},{1,0},{2,3},{3,2},{4,5},{5,4},{6,7},{7,6},{8,9},{9,8},{10,11... | collective-permute-start | bytes 196616 | tf_op jit(solution)/shard_map/ppermute | solution.py:792
  43.2 7.6 %collective-permute-start.8 = (f32[2,4,32,128]{3,2,1,0:T(8,128)S(1)}, f32[2,4,32,128]{3,2,1,0:T(8,128)S(1)}, u32[]{:S(2)}, u32[]{:S(2)}) collective-permute-start(f32[2,4,32,128]{3,2,1,0:T(8,128)S(1)} %get-tuple-element.80), channel_id=1, source_target_pairs={{0,120},{8,16},{16,8},{24,32},{32,24},{40,48},{48,40},{56,64},{64,... | collective-permute-start | bytes 393224 | tf_op jit(solution)/shard_map/ppermute | solution.py:792
  44.7 6.1 %collective-permute-start.9 = (f32[2,4,32,128]{3,2,1,0:T(8,128)S(1)}, f32[2,4,32,128]{3,2,1,0:T(8,128)S(1)}, u32[]{:S(2)}, u32[]{:S(2)}) collective-permute-start(f32[2,4,32,128]{3,2,1,0:T(8,128)S(1)} %get-tuple-element.81), channel_id=1, source_target_pairs={{0,8},{8,0},{16,24},{24,16},{32,40},{40,32},{48,56},{56,48},{64,72... | collective-permute-start | bytes 393224 | tf_op jit(solution)/shard_map/ppermute | solution.py:792
  44.7 5.6 %collective-permute-start.10 = (f32[2,16,512]{2,1,0:T(8,128)S(1)}, f32[2,16,512]{2,1,0:T(8,128)S(1)}, u32[]{:S(2)}, u32[]{:S(2)}) collective-permute-start(f32[2,16,512]{2,1,0:T(8,128)S(1)} %get-tuple-element.82), channel_id=1, source_target_pairs={{0,7},{1,2},{2,1},{3,4},{4,3},{5,6},{6,5},{7,0},{8,15},{9,10},{10,... | collective-permute-start | bytes 196616 | tf_op jit(solution)/shard_map/ppermute | solution.py:792
  46.2 4.1 %collective-permute-start.11 = (f32[2,16,512]{2,1,0:T(8,128)S(1)}, f32[2,16,512]{2,1,0:T(8,128)S(1)}, u32[]{:S(2)}, u32[]{:S(2)}) collective-permute-start(f32[2,16,512]{2,1,0:T(8,128)S(1)} %get-tuple-element.83), channel_id=1, source_target_pairs={{0,1},{1,0},{2,3},{3,2},{4,5},{5,4},{6,7},{7,6},{8,9},{9,8},{10,11... | collective-permute-start | bytes 196616 | tf_op jit(solution)/shard_map/ppermute | solution.py:792
  54.4 22.4 %all-to-all-start.1 = ((f32[128,8,128]{2,1,0:T(8,128)}), f32[128,8,128]{2,1,0:T(8,128)S(1)}, u32[]{:S(2)}, u32[]{:S(2)}) async-start(f32[128,8,128]{2,1,0:T(8,128)} %bitcast.17), calls=%async_computation.1 | async-start | bytes 1048576 | tf_op jit(solution)/shard_map/all_to_all | solution.py:841
  61.8 13.5 %collective-permute-start.12 = (f32[2,4,32,128]{3,2,1,0:T(8,128)S(1)}, f32[2,4,32,128]{3,2,1,0:T(8,128)S(1)}, u32[]{:S(2)}, u32[]{:S(2)}) collective-permute-start(f32[2,4,32,128]{3,2,1,0:T(8,128)S(1)} %get-tuple-element.98), channel_id=1, source_target_pairs={{0,120},{8,16},{16,8},{24,32},{32,24},{40,48},{48,40},{56,64},{64,... | collective-permute-start | bytes 393224 | tf_op jit(solution)/shard_map/ppermute | solution.py:792
  66.9 8.4 %collective-permute-start.13 = (f32[2,4,32,128]{3,2,1,0:T(8,128)S(1)}, f32[2,4,32,128]{3,2,1,0:T(8,128)S(1)}, u32[]{:S(2)}, u32[]{:S(2)}) collective-permute-start(f32[2,4,32,128]{3,2,1,0:T(8,128)S(1)} %get-tuple-element.99), channel_id=1, source_target_pairs={{0,8},{8,0},{16,24},{24,16},{32,40},{40,32},{48,56},{56,48},{64,72... | collective-permute-start | bytes 393224 | tf_op jit(solution)/shard_map/ppermute | solution.py:792
  66.9 7.8 %collective-permute-start.14 = (f32[2,16,512]{2,1,0:T(8,128)S(1)}, f32[2,16,512]{2,1,0:T(8,128)S(1)}, u32[]{:S(2)}, u32[]{:S(2)}) collective-permute-start(f32[2,16,512]{2,1,0:T(8,128)S(1)} %get-tuple-element.100), channel_id=1, source_target_pairs={{0,7},{1,2},{2,1},{3,4},{4,3},{5,6},{6,5},{7,0},{8,15},{9,10},{10,... | collective-permute-start | bytes 196616 | tf_op jit(solution)/shard_map/ppermute | solution.py:792
  68.9 5.8 %collective-permute-start.15 = (f32[2,16,512]{2,1,0:T(8,128)S(1)}, f32[2,16,512]{2,1,0:T(8,128)S(1)}, u32[]{:S(2)}, u32[]{:S(2)}) collective-permute-start(f32[2,16,512]{2,1,0:T(8,128)S(1)} %get-tuple-element.101), channel_id=1, source_target_pairs={{0,1},{1,0},{2,3},{3,2},{4,5},{5,4},{6,7},{7,6},{8,9},{9,8},{10,11... | collective-permute-start | bytes 196616 | tf_op jit(solution)/shard_map/ppermute | solution.py:792

commit v6 on v5

--- a/solution.py
+++ b/solution.py
@@ -267,7 +267,7 @@
     coupling[:, :heights] = jnp.zeros((coupling.shape[0], heights, *coupling.shape[2:]), jnp.float32)
 
 
-def local_planes(fields, befores, outs, speed2, extra, sends=None):
+def local_planes(fields, befores, outs, speed2, extra, sends=None, arrivals=None, lag=0):
     cells_z = speed2.shape[0]
 
     def plane(z, below, above):
@@ -281,13 +281,18 @@
         plane(z, lambda now: now[z - 1], lambda now: now[z + 1])
         return carry
 
-    plane(0, lambda now: 0.0, lambda now: now[1])
-    plane(cells_z - 1, lambda now: now[cells_z - 2], lambda now: 0.0)
-    shares = len(sends) if sends else 1
+    shares = len(sends or arrivals or ((),))
     share = cells_z // shares
     for i in range(shares):
-        start, stop = max(i * share, 1), min((i + 1) * share, cells_z - 1)
-        lax.fori_loop(start, stop, inner, 0, unroll=(stop - start) // -(-(stop - start) // UNROLL))
+        for copy in arrivals[i] if arrivals else ():
+            copy.wait()
+        start, stop = max(i * share - lag, 1), (i + 1) * share - lag
+        if i == 0:
+            plane(0, lambda now: 0.0, lambda now: now[1])
+        if i == shares - 1:
+            plane(cells_z - 1, lambda now: now[cells_z - 2], lambda now: 0.0)
+            stop = cells_z - 1
+        lax.fori_loop(start, stop, inner, 0, unroll=min(stop - start, UNROLL))
         for send in sends[i] if sends else ():
             send.start()
 
@@ -311,6 +316,18 @@
         )
         for i in range(count)
     ]
+
+
+def arrivals_of(pairs, sems, first, count):
+    loads = [
+        shares_of(source, target, sems, first + i * count, count)
+        for i, (source, target) in enumerate(pairs)
+    ]
+    arrivals = [[copies[i] for copies in loads] for i in range(count)]
+    for copies in arrivals:
+        for copy in copies:
+            copy.start()
+    return arrivals
 
 
 class Lines:
@@ -391,24 +408,14 @@
 
 
 def first_local_kernel(rows_hbm, field_prev_hbm, adjoint_prev_hbm, speed2_hbm, field, adjoint, out_hbm, adjoint_out_hbm, push, picked, rows_ref, field_prev, adjoint_prev, speed2, out, adjoint_out, tiles, sems):
-    loads = [
-        pltpu.make_async_copy(source, target, sems.at[i])
-        for i, (source, target) in enumerate(
-            (
-                (rows_hbm, rows_ref),
-                (speed2_hbm, speed2),
-                (field_prev_hbm, field_prev),
-                (adjoint_prev_hbm, adjoint_prev),
-            )
-        )
-    ]
-    for copy in loads:
-        copy.start()
-    loads[0].wait()
+    shares = 4
+    rows_load = pltpu.make_async_copy(rows_hbm, rows_ref, sems.at[0])
+    rows_load.start()
+    pairs = ((speed2_hbm, speed2), (field_prev_hbm, field_prev), (adjoint_prev_hbm, adjoint_prev))
+    arrivals = arrivals_of(pairs, sems, 14, shares)
+    rows_load.wait()
     pick(rows_ref, (field, adjoint), picked, tiles)
     push[...] = KAPPA * picked[...]
-    for copy in loads[1:]:
-        copy.wait()
     sends = list(
         zip(
             shares_of(out, out_hbm, sems, 6, 4), shares_of(adjoint_out, adjoint_out_hbm, sems, 10, 4)
@@ -421,6 +428,7 @@
         speed2,
         lambda side, z: 0.0,
         sends,
+        arrivals,
     )
     for pair in sends:
         for send in pair:
@@ -436,7 +444,7 @@
         out_shape=[HBM(field.shape, jnp.float32)] * 2 + [rows_shape] * 2,
         scratch_shapes=[pltpu.SMEM((slots,), jnp.int32)]
         + [pltpu.VMEM(field.shape, jnp.float32)] * 5
-        + [pltpu.VMEM((2, 8 * slots, width), jnp.float32), pltpu.SemaphoreType.DMA((14,))],
+        + [pltpu.VMEM((2, 8 * slots, width), jnp.float32), pltpu.SemaphoreType.DMA((26,))],
         compiler_params=params(16),
         cost_estimate=pl.CostEstimate(flops=8 << 20, bytes_accessed=12 << 20, transcendentals=0),
         name="local0",
@@ -667,42 +675,38 @@
 
 
 def last_local_kernel(rows_hbm, field_hbm, field_prev_hbm, adjoint_hbm, adjoint_prev_hbm, speed2_hbm, change, out, adjoint_out, speed_first, speed_last, speed_ends, rows_ref, field, field_prev, adjoint, adjoint_prev, speed2, coupling, sems):
-    loads = [
-        pltpu.make_async_copy(source, target, sems.at[i])
-        for i, (source, target) in enumerate(
-            (
-                (rows_hbm, rows_ref),
-                (speed2_hbm, speed2),
-                (field_hbm, field),
-                (adjoint_hbm, adjoint),
-                (field_prev_hbm, field_prev),
-                (adjoint_prev_hbm, adjoint_prev),
-            )
-        )
-    ]
-    for copy in loads:
-        copy.start()
+    shares = 4
+    rows_load = pltpu.make_async_copy(rows_hbm, rows_ref, sems.at[0])
+    rows_load.start()
+    pairs = (
+        (speed2_hbm, speed2),
+        (field_hbm, field),
+        (adjoint_hbm, adjoint),
+        (field_prev_hbm, field_prev),
+        (adjoint_prev_hbm, adjoint_prev),
+    )
+    arrivals = arrivals_of(pairs, sems, 1, shares)
     clear(coupling)
-    loads[0].wait()
+    rows_load.wait()
     couple(rows_ref, change, coupling)
-    loads[1].wait()
-    cells_z = speed2.shape[0]
-    speed_ends[0], speed_ends[1] = speed2[0], speed2[cells_z - 1]
-
-    def sides(z, carry):
-        keep_side(speed2[z], z, speed_first, speed_last)
-        return carry
-
-    lax.fori_loop(0, cells_z, sides, 0, unroll=8)
-    for copy in loads[2:]:
-        copy.wait()
     local_planes(
         (field, adjoint),
         (field_prev, adjoint_prev),
         (out, adjoint_out),
         speed2,
         functools.partial(extra_of, coupling),
-    )
+        None,
+        arrivals,
+        1,
+    )
+    cells_z = speed2.shape[0]
+    speed_ends[0], speed_ends[1] = speed2[0], speed2[cells_z - 1]
+
+    def sides(z, carry):
+        keep_side(speed2[z], z, speed_first, speed_last)
+        return carry
+
+    lax.fori_loop(0, cells_z, sides, 0, unroll=8)
 
 
 def last_local(rows, field, field_prev, adjoint, adjoint_prev, speed2, change):
@@ -719,7 +723,7 @@
         scratch_shapes=[pltpu.SMEM((slots,), jnp.int32)]
         + [pltpu.VMEM(field.shape, jnp.float32)] * 5
         + coupling_scratch(field, slots, width)[:1]
-        + [pltpu.SemaphoreType.DMA((6,))],
+        + [pltpu.SemaphoreType.DMA((21,))],
         compiler_params=params(16),
         cost_estimate=pl.CostEstimate(flops=8 << 20, bytes_accessed=12 << 20, transcendentals=0),
         name=f"local{STEPS - 1}",

time: 77.8 us -> 77.8 us (level)
  waiting for transfers between devices: 1.97 us -> 3.14 us
  Pallas kernels: 30.4 us -> 29.4 us
    ppermute x16, waiting for transfers between devices: 1.97 us -> 3.14 us  [exchange(): lax.ppermute(edge, axis, swaps(axis, first))]
    pallas_call x1, Pallas kernels: 4.15 us -> 3.13 us  [last_local(): pl.pallas_call(last_local_kernel, in_specs=[pl.BlockSpec(memory_space=HBM...]
  transfers between devices with their start and end apart: 18 -> 18, of which waited for: 3 -> 3; matrix products, arithmetic and copies ran while one was open for 0% -> 0% of each run, Pallas kernels for 24% -> 23%
where the time goes in v6:
time: 77.8 us; the launch traced here: 77.5 us
  starting transfers between devices  43.4 us (56%)
  Pallas kernels  29.4 us (38%)
  waiting for transfers between devices  3.14 us (4%)
  between operations  0.86 us (1%)
    ppermute x16, starting transfers between devices, exchange(): lax.ppermute(edge, axis, swaps(axis, first))  24.4 us
    all_to_all x1, starting transfers between devices, body(): lax.all_to_all(lines, ('gx', 'gz'), split_axis=0, concat_axis=0, tiled=True)  11.5 us
    all_to_all x1, starting transfers between devices, body(): lax.all_to_all(parts, ('gx', 'gz'), split_axis=0, concat_axis=0, tiled=True)  7.45 us
    pallas_call x2, Pallas kernels, local_step(): pl.pallas_call(functools.partial(local_kernel, step), in_specs=[pl.BlockS...  7.4 us
    pallas_call x1, Pallas kernels, surface_rows(): pl.pallas_call(surface_kernel, in_specs=[pl.BlockSpec(memory_space=HBM)]...  4.73 us
    pallas_call x1, Pallas kernels, first_local(): pl.pallas_call(first_local_kernel, in_specs=[pl.BlockSpec(memory_space=HB...  4.03 us
    ppermute x16, waiting for transfers between devices, exchange(): lax.ppermute(edge, axis, swaps(axis, first))  3.14 us
    pallas_call x1, Pallas kernels, last_local(): pl.pallas_call(last_local_kernel, in_specs=[pl.BlockSpec(memory_space=HBM...  3.13 us
  transfers between devices with their start and end apart: 18, of which 3 were waited for; matrix products, arithmetic and copies ran while one was open for 0% of the time, Pallas kernels for 23%

profile of v6, /device:TPU:1, one launch (start us, length us, event | category | flops | bytes accessed | tf_op | source)
XLA Modules:
  0.0 77.5 jit_solution(15167393395213958169)
XLA Ops:
  0.6 4.7 %surface_rows.1 = f32[768,128]{1,0:T(8,128)} custom-call(f32[8,64,64]{2,1,0:T(8,128)} %maps_hbm.1, s32[128]{0:T(128)} %patch_hbm.1, s32[1024]{0:T(1024)} %material_hbm.1, f32[128,64,128]{2,1,0:T(8,128)} %layer_hbm.1), custom_call_target="tpu_custom_call" | custom-call | tf_op jit(solution)/shard_map/surface_rows/pallas_call | solution.py:101
  5.4 11.5 %all-to-all-start = ((f32[128,1,768]{2,1,0:T(1,128)}), f32[128,1,768]{2,1,0:T(1,128)S(1)}, u32[]{:S(2)}, u32[]{:S(2)}) async-start(f32[128,1,768]{2,1,0:T(1,128)} %bitcast.16), calls=%async_computation | async-start | bytes 786432 | tf_op jit(solution)/shard_map/all_to_all | solution.py:820
  16.9 1.7 %edges.1 = (f32[32,16,512]{2,1,0:T(8,128)S(1)}, f32[32,16,512]{2,1,0:T(8,128)S(1)}, f32[2,4,32,128]{3,2,1,0:T(8,128)S(1)}, f32[2,4,32,128]{3,2,1,0:T(8,128)S(1)}...) custom-call(f32[32,16,512]{2,1,0:T(8,128)} %field_prev.1, f32[32,16,512]{2,1,0:T(8,128)} %adjoint_prev.1), custom_call_target="tpu_custom_call" | custom-call | tf_op jit(solution)/shard_map/edges/pallas_call | solution.py:240
  18.6 4.9 %collective-permute-start = (f32[2,4,32,128]{3,2,1,0:T(8,128)S(1)}, f32[2,4,32,128]{3,2,1,0:T(8,128)S(1)}, u32[]{:S(2)}, u32[]{:S(2)}) collective-permute-start(f32[2,4,32,128]{3,2,1,0:T(8,128)S(1)} %get-tuple-element.58), channel_id=1, source_target_pairs={{0,120},{8,16},{16,8},{24,32},{32,24},{40,48},{48,40},{56,64},{64,... | collective-permute-start | bytes 393224 | tf_op jit(solution)/shard_map/ppermute | solution.py:796
  23.5 2.0 %collective-permute-start.2 = (f32[2,16,512]{2,1,0:T(8,128)S(1)}, f32[2,16,512]{2,1,0:T(8,128)S(1)}, u32[]{:S(2)}, u32[]{:S(2)}) collective-permute-start(f32[2,16,512]{2,1,0:T(8,128)S(1)} %get-tuple-element.60), channel_id=1, source_target_pairs={{0,7},{1,2},{2,1},{3,4},{4,3},{5,6},{6,5},{7,0},{8,15},{9,10},{10,... | collective-permute-start | bytes 196616 | tf_op jit(solution)/shard_map/ppermute | solution.py:796
  25.5 1.6 %collective-permute-start.3 = (f32[2,16,512]{2,1,0:T(8,128)S(1)}, f32[2,16,512]{2,1,0:T(8,128)S(1)}, u32[]{:S(2)}, u32[]{:S(2)}) collective-permute-start(f32[2,16,512]{2,1,0:T(8,128)S(1)} %get-tuple-element.61), channel_id=1, source_target_pairs={{0,1},{1,0},{2,3},{3,2},{4,5},{5,4},{6,7},{7,6},{8,9},{9,8},{10,11... | collective-permute-start | bytes 196616 | tf_op jit(solution)/shard_map/ppermute | solution.py:796
  27.1 4.0 %local0.1 = (f32[32,16,512]{2,1,0:T(8,128)}, f32[32,16,512]{2,1,0:T(8,128)}, f32[2,128,128]{2,1,0:T(8,128)S(1)}, f32[2,128,128]{2,1,0:T(8,128)S(1)}) custom-call(s32[128]{0:T(128)} %bitcast.9, f32[32,16,512]{2,1,0:T(8,128)} %field_prev_hbm.1, f32[32,16,512]{2,1,0:T(8,128)} %adjoint_prev_hbm.1, f32[32,16,512]{2,1,0:T(8,128)} %speed2_hbm.5, ...), custom_call_target="tpu_custom_call" | custom-call | flops 8388608 | bytes 12582912 | tf_op jit(solution)/shard_map/local0/pallas_call | solution.py:440
  31.2 2.7 %border0.1 = (f32[32,16,512]{2,1,0:T(8,128)S(1)}, f32[32,16,512]{2,1,0:T(8,128)S(1)}, f32[32,16,512]{2,1,0:T(8,128)S(1)}, f32[2,4,32,128]{3,2,1,0:T(8,128)S(1)},...) custom-call(s32[128]{0:T(128)S(1)} %bitcast.11, ...), custom_call_target="tpu_custom_call" | custom-call | tf_op jit(solution)/shard_map/border0/pallas_call | solution.py:493
  33.9 0.8 %collective-permute-start.4 = (f32[2,4,32,128]{3,2,1,0:T(8,128)S(1)}, f32[2,4,32,128]{3,2,1,0:T(8,128)S(1)}, u32[]{:S(2)}, u32[]{:S(2)}) collective-permute-start(f32[2,4,32,128]{3,2,1,0:T(8,128)S(1)} %get-tuple-element.70), channel_id=1, source_target_pairs={{0,120},{8,16},{16,8},{24,32},{32,24},{40,48},{48,40},{56,64},{64,... | collective-permute-start | bytes 393224 | tf_op jit(solution)/shard_map/ppermute | solution.py:796
  34.7 0.8 %collective-permute-start.5 = (f32[2,4,32,128]{3,2,1,0:T(8,128)S(1)}, f32[2,4,32,128]{3,2,1,0:T(8,128)S(1)}, u32[]{:S(2)}, u32[]{:S(2)}) collective-permute-start(f32[2,4,32,128]{3,2,1,0:T(8,128)S(1)} %get-tuple-element.71), channel_id=1, source_target_pairs={{0,8},{8,0},{16,24},{24,16},{32,40},{40,32},{48,56},{56,48},{64,72... | collective-permute-start | bytes 393224 | tf_op jit(solution)/shard_map/ppermute | solution.py:796
  35.5 1.6 %collective-permute-start.6 = (f32[2,16,512]{2,1,0:T(8,128)S(1)}, f32[2,16,512]{2,1,0:T(8,128)S(1)}, u32[]{:S(2)}, u32[]{:S(2)}) collective-permute-start(f32[2,16,512]{2,1,0:T(8,128)S(1)} %get-tuple-element.72), channel_id=1, source_target_pairs={{0,7},{1,2},{2,1},{3,4},{4,3},{5,6},{6,5},{7,0},{8,15},{9,10},{10,... | collective-permute-start | bytes 196616 | tf_op jit(solution)/shard_map/ppermute | solution.py:796
  37.1 0.8 %collective-permute-start.7 = (f32[2,16,512]{2,1,0:T(8,128)S(1)}, f32[2,16,512]{2,1,0:T(8,128)S(1)}, u32[]{:S(2)}, u32[]{:S(2)}) collective-permute-start(f32[2,16,512]{2,1,0:T(8,128)S(1)} %get-tuple-element.73), channel_id=1, source_target_pairs={{0,1},{1,0},{2,3},{3,2},{4,5},{5,4},{6,7},{7,6},{8,9},{9,8},{10,11... | collective-permute-start | bytes 196616 | tf_op jit(solution)/shard_map/ppermute | solution.py:796
  37.9 3.7 %local1.1 = (f32[32,16,512]{2,1,0:T(8,128)S(1)}, f32[32,16,512]{2,1,0:T(8,128)S(1)}, f32[2,128,128]{2,1,0:T(8,128)S(1)}, f32[2,128,128]{2,1,0:T(8,128)S(1)}) custom-call(s32[128]{0:T(128)S(1)} %bitcast.12, f32[32,16,512]{2,1,0:T(8,128)S(1)} %get-tuple-element.64.field.field_prev, f32[32,16,512]{2,1,0:T(8,128)} %field_prev.1, ...), custom_call_target="tpu_custom_call" | custom-call | flops 8388608 | bytes 12582912 | tf_op jit(solution)/shard_map/local1/pallas_call | solution.py:564
  43.1 1.5 %collective-permute-start.8 = (f32[2,4,32,128]{3,2,1,0:T(8,128)S(1)}, f32[2,4,32,128]{3,2,1,0:T(8,128)S(1)}, u32[]{:S(2)}, u32[]{:S(2)}) collective-permute-start(f32[2,4,32,128]{3,2,1,0:T(8,128)S(1)} %get-tuple-element.80), channel_id=1, source_target_pairs={{0,120},{8,16},{16,8},{24,32},{32,24},{40,48},{48,40},{56,64},{64,... | collective-permute-start | bytes 393224 | tf_op jit(solution)/shard_map/ppermute | solution.py:796
  44.7 1.6 %collective-permute-start.10 = (f32[2,16,512]{2,1,0:T(8,128)S(1)}, f32[2,16,512]{2,1,0:T(8,128)S(1)}, u32[]{:S(2)}, u32[]{:S(2)}) collective-permute-start(f32[2,16,512]{2,1,0:T(8,128)S(1)} %get-tuple-element.82), channel_id=1, source_target_pairs={{0,7},{1,2},{2,1},{3,4},{4,3},{5,6},{6,5},{7,0},{8,15},{9,10},{10,... | collective-permute-start | bytes 196616 | tf_op jit(solution)/shard_map/ppermute | solution.py:796
  46.6 3.7 %local2.1 = (f32[32,16,512]{2,1,0:T(8,128)S(1)}, f32[32,16,512]{2,1,0:T(8,128)S(1)}, f32[2,128,128]{2,1,0:T(8,128)S(1)}, f32[2,128,128]{2,1,0:T(8,128)S(1)}, f32...) custom-call(s32[128]{0:T(128)S(1)} %bitcast.13, f32[32,16,512]{2,1,0:T(8,128)S(1)} %get-tuple-element.74.field, ...), custom_call_target="tpu_custom_call" | custom-call | flops 8388608 | bytes 12582912 | tf_op jit(solution)/shard_map/local2/pallas_call | solution.py:564
  51.5 2.8 %correlation.1 = (f32[1024,128]{1,0:T(8,128)}, f32[2,128,128]{2,1,0:T(8,128)S(1)}, f32[32,16,512]{2,1,0:T(8,128)}, f32[32,16,512]{2,1,0:T(8,128)}) custom-call(s32[128]{0:T(128)S(1)} %bitcast.14, s32[1,128]{1,0:T(1,128)S(1)} %bitcast.15, f32[32,16,512]{2,1,0:T(8,128)S(1)} %get-tuple-element.84.field, f32[32,16,512]{2,1,0:T(8,128)S(1)} %get-tuple-element.85.adjoint, ...), custom_call_target="tpu_custom_call" | custom-call | tf_op jit(solution)/shard_map/correlation/pallas_call | solution.py:657
  54.4 7.5 %all-to-all-start.1 = ((f32[128,8,128]{2,1,0:T(8,128)}), f32[128,8,128]{2,1,0:T(8,128)S(1)}, u32[]{:S(2)}, u32[]{:S(2)}) async-start(f32[128,8,128]{2,1,0:T(8,128)} %bitcast.17), calls=%async_computation.1 | async-start | bytes 1048576 | tf_op jit(solution)/shard_map/all_to_all | solution.py:845
  61.8 4.9 %collective-permute-start.12 = (f32[2,4,32,128]{3,2,1,0:T(8,128)S(1)}, f32[2,4,32,128]{3,2,1,0:T(8,128)S(1)}, u32[]{:S(2)}, u32[]{:S(2)}) collective-permute-start(f32[2,4,32,128]{3,2,1,0:T(8,128)S(1)} %get-tuple-element.98), channel_id=1, source_target_pairs={{0,120},{8,16},{16,8},{24,32},{32,24},{40,48},{48,40},{56,64},{64,... | collective-permute-start | bytes 393224 | tf_op jit(solution)/shard_map/ppermute | solution.py:796
  66.7 2.0 %collective-permute-start.14 = (f32[2,16,512]{2,1,0:T(8,128)S(1)}, f32[2,16,512]{2,1,0:T(8,128)S(1)}, u32[]{:S(2)}, u32[]{:S(2)}) collective-permute-start(f32[2,16,512]{2,1,0:T(8,128)S(1)} %get-tuple-element.100), channel_id=1, source_target_pairs={{0,7},{1,2},{2,1},{3,4},{4,3},{5,6},{6,5},{7,0},{8,15},{9,10},{10,... | collective-permute-start | bytes 196616 | tf_op jit(solution)/shard_map/ppermute | solution.py:796
  68.7 1.6 %collective-permute-start.15 = (f32[2,16,512]{2,1,0:T(8,128)S(1)}, f32[2,16,512]{2,1,0:T(8,128)S(1)}, u32[]{:S(2)}, u32[]{:S(2)}) collective-permute-start(f32[2,16,512]{2,1,0:T(8,128)S(1)} %get-tuple-element.101), channel_id=1, source_target_pairs={{0,1},{1,0},{2,3},{3,2},{4,5},{5,4},{6,7},{7,6},{8,9},{9,8},{10,11... | collective-permute-start | bytes 196616 | tf_op jit(solution)/shard_map/ppermute | solution.py:796
  70.3 3.1 %local3.1 = (f32[32,16,512]{2,1,0:T(8,128)S(1)}, f32[32,16,512]{2,1,0:T(8,128)S(1)}, f32[4,32,128]{2,1,0:T(8,128)S(1)}, f32[4,32,128]{2,1,0:T(8,128)S(1)}, f32[2,16,512]{2,1,0:T(8,128)S(1)}) custom-call(s32[128]{0:T(128)} %bitcast.10, f32[32,16,512]{2,1,0:T(8,128)} %get-tuple-element.88.field_hbm, f32[32,16,512]{2,1,0:T(8,128)} %get-tuple-element.89.field_prev_hbm, ...), custom_call_target="tpu_custom_call" | custom-call | flops 8388608 | bytes 12582912 | tf_op jit(solution)/shard_map/local3/pallas_call | solution.py:717
  73.5 1.9 %collective-permute-done.12.x_from_outer = f32[2,4,32,128]{3,2,1,0:T(8,128)S(1)} collective-permute-done((f32[2,4,32,128]{3,2,1,0:T(8,128)S(1)}, f32[2,4,32,128]{3,2,1,0:T(8,128)S(1)}, u32[]{:S(2)}, u32[]{:S(2)}) %collective-permute-start.12) | collective-permute-done | bytes 131104 | tf_op jit(solution)/shard_map/ppermute | solution.py:796
  75.3 1.5 %finish.1 = (f32[32,16,512]{2,1,0:T(8,128)}, f32[32,16,512]{2,1,0:T(8,128)}) custom-call(f32[32,16,512]{2,1,0:T(8,128)S(1)} %get-tuple-element.93.field_in, f32[32,16,512]{2,1,0:T(8,128)S(1)} %get-tuple-element.94.adjoint_in, f32[4,32,128]{2,1,0:T(8,128)S(1)} %get-tuple-element.95.speed_first, f32[4,32,128]{2,1,0:T(8,128)S(1)} %get-tuple-element.96.speed_last, ...), custom_call_target="tpu_custom_call" | custom-call | tf_op jit(solution)/shard_map/finish/pallas_call | solution.py:776
  (26 shorter events, 3.8 us)
Async XLA Ops:
  5.4 25.8 %copy-start = (s32[1,128,1]{1,2,0:T(1,128)S(1)}, s32[1,128,1]{1,2,0:T(1,128)}, u32[]{:S(2)}) copy-start(s32[1,128,1]{1,2,0:T(1,128)} %param.17) | copy-start | bytes 1540
  5.4 25.8 %all-to-all-start = ((f32[128,1,768]{2,1,0:T(1,128)}), f32[128,1,768]{2,1,0:T(1,128)S(1)}, u32[]{:S(2)}, u32[]{:S(2)}) async-start(f32[128,1,768]{2,1,0:T(1,128)} %bitcast.16), calls=%async_computation | async-start | bytes 786432 | tf_op jit(solution)/shard_map/all_to_all | solution.py:820
  18.6 12.6 %collective-permute-start = (f32[2,4,32,128]{3,2,1,0:T(8,128)S(1)}, f32[2,4,32,128]{3,2,1,0:T(8,128)S(1)}, u32[]{:S(2)}, u32[]{:S(2)}) collective-permute-start(f32[2,4,32,128]{3,2,1,0:T(8,128)S(1)} %get-tuple-element.58), channel_id=1, source_target_pairs={{0,120},{8,16},{16,8},{24,32},{32,24},{40,48},{48,40},{56,64},{64,... | collective-permute-start | bytes 393224 | tf_op jit(solution)/shard_map/ppermute | solution.py:796
  23.5 7.7 %collective-permute-start.1 = (f32[2,4,32,128]{3,2,1,0:T(8,128)S(1)}, f32[2,4,32,128]{3,2,1,0:T(8,128)S(1)}, u32[]{:S(2)}, u32[]{:S(2)}) collective-permute-start(f32[2,4,32,128]{3,2,1,0:T(8,128)S(1)} %get-tuple-element.59), channel_id=1, source_target_pairs={{0,8},{8,0},{16,24},{24,16},{32,40},{40,32},{48,56},{56,48},{64,72... | collective-permute-start | bytes 393224 | tf_op jit(solution)/shard_map/ppermute | solution.py:796
  23.5 7.6 %collective-permute-start.2 = (f32[2,16,512]{2,1,0:T(8,128)S(1)}, f32[2,16,512]{2,1,0:T(8,128)S(1)}, u32[]{:S(2)}, u32[]{:S(2)}) collective-permute-start(f32[2,16,512]{2,1,0:T(8,128)S(1)} %get-tuple-element.60), channel_id=1, source_target_pairs={{0,7},{1,2},{2,1},{3,4},{4,3},{5,6},{6,5},{7,0},{8,15},{9,10},{10,... | collective-permute-start | bytes 196616 | tf_op jit(solution)/shard_map/ppermute | solution.py:796
  25.5 5.7 %collective-permute-start.3 = (f32[2,16,512]{2,1,0:T(8,128)S(1)}, f32[2,16,512]{2,1,0:T(8,128)S(1)}, u32[]{:S(2)}, u32[]{:S(2)}) collective-permute-start(f32[2,16,512]{2,1,0:T(8,128)S(1)} %get-tuple-element.61), channel_id=1, source_target_pairs={{0,1},{1,0},{2,3},{3,2},{4,5},{5,4},{6,7},{7,6},{8,9},{9,8},{10,11... | collective-permute-start | bytes 196616 | tf_op jit(solution)/shard_map/ppermute | solution.py:796
  33.9 8.5 %collective-permute-start.4 = (f32[2,4,32,128]{3,2,1,0:T(8,128)S(1)}, f32[2,4,32,128]{3,2,1,0:T(8,128)S(1)}, u32[]{:S(2)}, u32[]{:S(2)}) collective-permute-start(f32[2,4,32,128]{3,2,1,0:T(8,128)S(1)} %get-tuple-element.70), channel_id=1, source_target_pairs={{0,120},{8,16},{16,8},{24,32},{32,24},{40,48},{48,40},{56,64},{64,... | collective-permute-start | bytes 393224 | tf_op jit(solution)/shard_map/ppermute | solution.py:796
  34.7 7.7 %collective-permute-start.5 = (f32[2,4,32,128]{3,2,1,0:T(8,128)S(1)}, f32[2,4,32,128]{3,2,1,0:T(8,128)S(1)}, u32[]{:S(2)}, u32[]{:S(2)}) collective-permute-start(f32[2,4,32,128]{3,2,1,0:T(8,128)S(1)} %get-tuple-element.71), channel_id=1, source_target_pairs={{0,8},{8,0},{16,24},{24,16},{32,40},{40,32},{48,56},{56,48},{64,72... | collective-permute-start | bytes 393224 | tf_op jit(solution)/shard_map/ppermute | solution.py:796
  35.5 6.1 %collective-permute-start.6 = (f32[2,16,512]{2,1,0:T(8,128)S(1)}, f32[2,16,512]{2,1,0:T(8,128)S(1)}, u32[]{:S(2)}, u32[]{:S(2)}) collective-permute-start(f32[2,16,512]{2,1,0:T(8,128)S(1)} %get-tuple-element.72), channel_id=1, source_target_pairs={{0,7},{1,2},{2,1},{3,4},{4,3},{5,6},{6,5},{7,0},{8,15},{9,10},{10,... | collective-permute-start | bytes 196616 | tf_op jit(solution)/shard_map/ppermute | solution.py:796
  37.1 4.5 %collective-permute-start.7 = (f32[2,16,512]{2,1,0:T(8,128)S(1)}, f32[2,16,512]{2,1,0:T(8,128)S(1)}, u32[]{:S(2)}, u32[]{:S(2)}) collective-permute-start(f32[2,16,512]{2,1,0:T(8,128)S(1)} %get-tuple-element.73), channel_id=1, source_target_pairs={{0,1},{1,0},{2,3},{3,2},{4,5},{5,4},{6,7},{7,6},{8,9},{9,8},{10,11... | collective-permute-start | bytes 196616 | tf_op jit(solution)/shard_map/ppermute | solution.py:796
  43.1 7.6 %collective-permute-start.8 = (f32[2,4,32,128]{3,2,1,0:T(8,128)S(1)}, f32[2,4,32,128]{3,2,1,0:T(8,128)S(1)}, u32[]{:S(2)}, u32[]{:S(2)}) collective-permute-start(f32[2,4,32,128]{3,2,1,0:T(8,128)S(1)} %get-tuple-element.80), channel_id=1, source_target_pairs={{0,120},{8,16},{16,8},{24,32},{32,24},{40,48},{48,40},{56,64},{64,... | collective-permute-start | bytes 393224 | tf_op jit(solution)/shard_map/ppermute | solution.py:796
  44.7 6.1 %collective-permute-start.9 = (f32[2,4,32,128]{3,2,1,0:T(8,128)S(1)}, f32[2,4,32,128]{3,2,1,0:T(8,128)S(1)}, u32[]{:S(2)}, u32[]{:S(2)}) collective-permute-start(f32[2,4,32,128]{3,2,1,0:T(8,128)S(1)} %get-tuple-element.81), channel_id=1, source_target_pairs={{0,8},{8,0},{16,24},{24,16},{32,40},{40,32},{48,56},{56,48},{64,72... | collective-permute-start | bytes 393224 | tf_op jit(solution)/shard_map/ppermute | solution.py:796
  44.7 5.6 %collective-permute-start.10 = (f32[2,16,512]{2,1,0:T(8,128)S(1)}, f32[2,16,512]{2,1,0:T(8,128)S(1)}, u32[]{:S(2)}, u32[]{:S(2)}) collective-permute-start(f32[2,16,512]{2,1,0:T(8,128)S(1)} %get-tuple-element.82), channel_id=1, source_target_pairs={{0,7},{1,2},{2,1},{3,4},{4,3},{5,6},{6,5},{7,0},{8,15},{9,10},{10,... | collective-permute-start | bytes 196616 | tf_op jit(solution)/shard_map/ppermute | solution.py:796
  46.2 4.1 %collective-permute-start.11 = (f32[2,16,512]{2,1,0:T(8,128)S(1)}, f32[2,16,512]{2,1,0:T(8,128)S(1)}, u32[]{:S(2)}, u32[]{:S(2)}) collective-permute-start(f32[2,16,512]{2,1,0:T(8,128)S(1)} %get-tuple-element.83), channel_id=1, source_target_pairs={{0,1},{1,0},{2,3},{3,2},{4,5},{5,4},{6,7},{7,6},{8,9},{9,8},{10,11... | collective-permute-start | bytes 196616 | tf_op jit(solution)/shard_map/ppermute | solution.py:796
  54.4 22.4 %all-to-all-start.1 = ((f32[128,8,128]{2,1,0:T(8,128)}), f32[128,8,128]{2,1,0:T(8,128)S(1)}, u32[]{:S(2)}, u32[]{:S(2)}) async-start(f32[128,8,128]{2,1,0:T(8,128)} %bitcast.17), calls=%async_computation.1 | async-start | bytes 1048576 | tf_op jit(solution)/shard_map/all_to_all | solution.py:845
  61.8 13.5 %collective-permute-start.12 = (f32[2,4,32,128]{3,2,1,0:T(8,128)S(1)}, f32[2,4,32,128]{3,2,1,0:T(8,128)S(1)}, u32[]{:S(2)}, u32[]{:S(2)}) collective-permute-start(f32[2,4,32,128]{3,2,1,0:T(8,128)S(1)} %get-tuple-element.98), channel_id=1, source_target_pairs={{0,120},{8,16},{16,8},{24,32},{32,24},{40,48},{48,40},{56,64},{64,... | collective-permute-start | bytes 393224 | tf_op jit(solution)/shard_map/ppermute | solution.py:796
  66.7 8.6 %collective-permute-start.13 = (f32[2,4,32,128]{3,2,1,0:T(8,128)S(1)}, f32[2,4,32,128]{3,2,1,0:T(8,128)S(1)}, u32[]{:S(2)}, u32[]{:S(2)}) collective-permute-start(f32[2,4,32,128]{3,2,1,0:T(8,128)S(1)} %get-tuple-element.99), channel_id=1, source_target_pairs={{0,8},{8,0},{16,24},{24,16},{32,40},{40,32},{48,56},{56,48},{64,72... | collective-permute-start | bytes 393224 | tf_op jit(solution)/shard_map/ppermute | solution.py:796
  66.7 6.7 %collective-permute-start.14 = (f32[2,16,512]{2,1,0:T(8,128)S(1)}, f32[2,16,512]{2,1,0:T(8,128)S(1)}, u32[]{:S(2)}, u32[]{:S(2)}) collective-permute-start(f32[2,16,512]{2,1,0:T(8,128)S(1)} %get-tuple-element.100), channel_id=1, source_target_pairs={{0,7},{1,2},{2,1},{3,4},{4,3},{5,6},{6,5},{7,0},{8,15},{9,10},{10,... | collective-permute-start | bytes 196616 | tf_op jit(solution)/shard_map/ppermute | solution.py:796
  68.7 4.8 %collective-permute-start.15 = (f32[2,16,512]{2,1,0:T(8,128)S(1)}, f32[2,16,512]{2,1,0:T(8,128)S(1)}, u32[]{:S(2)}, u32[]{:S(2)}) collective-permute-start(f32[2,16,512]{2,1,0:T(8,128)S(1)} %get-tuple-element.101), channel_id=1, source_target_pairs={{0,1},{1,0},{2,3},{3,2},{4,5},{5,4},{6,7},{7,6},{8,9},{9,8},{10,11... | collective-permute-start | bytes 196616 | tf_op jit(solution)/shard_map/ppermute | solution.py:796

commit v7 on v6

--- a/solution.py
+++ b/solution.py
@@ -17,7 +17,7 @@
 VMEM = pltpu.VMEM
 SMEM = pltpu.SMEM
 HBM = pltpu.HBM
-UNROLL = 10
+UNROLL = 30
 
 
 def in_hbm(*arrays):

time: 77.8 us -> 77.5 us (level)
  transfers between devices with their start and end apart: 18 -> 18, of which waited for: 3 -> 3; matrix products, arithmetic and copies ran while one was open for 0% -> 0% of each run, Pallas kernels for 23% -> 22%
where the time goes in v7:
time: 77.5 us; the launch traced here: 77.2 us
  starting transfers between devices  42.9 us (55%)
  Pallas kernels  28.9 us (37%)
  waiting for transfers between devices  3.8 us (5%)
  between operations  0.86 us (1%)
    ppermute x16, starting transfers between devices, exchange(): lax.ppermute(edge, axis, swaps(axis, first))  24.2 us
    all_to_all x1, starting transfers between devices, body(): lax.all_to_all(lines, ('gx', 'gz'), split_axis=0, concat_axis=0, tiled=True)  11.5 us
    all_to_all x1, starting transfers between devices, body(): lax.all_to_all(parts, ('gx', 'gz'), split_axis=0, concat_axis=0, tiled=True)  7.24 us
    pallas_call x2, Pallas kernels, local_step(): pl.pallas_call(functools.partial(local_kernel, step), in_specs=[pl.BlockS...  6.96 us
    pallas_call x1, Pallas kernels, surface_rows(): pl.pallas_call(surface_kernel, in_specs=[pl.BlockSpec(memory_space=HBM)]...  4.73 us
    pallas_call x1, Pallas kernels, first_local(): pl.pallas_call(first_local_kernel, in_specs=[pl.BlockSpec(memory_space=HB...  4.03 us
    ppermute x16, waiting for transfers between devices, exchange(): lax.ppermute(edge, axis, swaps(axis, first))  3.8 us
    pallas_call x1, Pallas kernels, last_local(): pl.pallas_call(last_local_kernel, in_specs=[pl.BlockSpec(memory_space=HBM...  3.13 us
  transfers between devices with their start and end apart: 18, of which 3 were waited for; matrix products, arithmetic and copies ran while one was open for 0% of the time, Pallas kernels for 22%

profile of v7, /device:TPU:1, one launch (start us, length us, event | category | flops | bytes accessed | tf_op | source)
XLA Modules:
  0.0 77.2 jit_solution(2511390672136106626)
XLA Ops:
  0.6 4.7 %surface_rows.1 = f32[768,128]{1,0:T(8,128)} custom-call(f32[8,64,64]{2,1,0:T(8,128)} %maps_hbm.1, s32[128]{0:T(128)} %patch_hbm.1, s32[1024]{0:T(1024)} %material_hbm.1, f32[128,64,128]{2,1,0:T(8,128)} %layer_hbm.1), custom_call_target="tpu_custom_call" | custom-call | tf_op jit(solution)/shard_map/surface_rows/pallas_call | solution.py:101
  5.4 11.5 %all-to-all-start = ((f32[128,1,768]{2,1,0:T(1,128)}), f32[128,1,768]{2,1,0:T(1,128)S(1)}, u32[]{:S(2)}, u32[]{:S(2)}) async-start(f32[128,1,768]{2,1,0:T(1,128)} %bitcast.16), calls=%async_computation | async-start | bytes 786432 | tf_op jit(solution)/shard_map/all_to_all | solution.py:820
  16.9 1.7 %edges.1 = (f32[32,16,512]{2,1,0:T(8,128)S(1)}, f32[32,16,512]{2,1,0:T(8,128)S(1)}, f32[2,4,32,128]{3,2,1,0:T(8,128)S(1)}, f32[2,4,32,128]{3,2,1,0:T(8,128)S(1)}...) custom-call(f32[32,16,512]{2,1,0:T(8,128)} %field_prev.1, f32[32,16,512]{2,1,0:T(8,128)} %adjoint_prev.1), custom_call_target="tpu_custom_call" | custom-call | tf_op jit(solution)/shard_map/edges/pallas_call | solution.py:240
  18.6 4.9 %collective-permute-start = (f32[2,4,32,128]{3,2,1,0:T(8,128)S(1)}, f32[2,4,32,128]{3,2,1,0:T(8,128)S(1)}, u32[]{:S(2)}, u32[]{:S(2)}) collective-permute-start(f32[2,4,32,128]{3,2,1,0:T(8,128)S(1)} %get-tuple-element.58), channel_id=1, source_target_pairs={{0,120},{8,16},{16,8},{24,32},{32,24},{40,48},{48,40},{56,64},{64,... | collective-permute-start | bytes 393224 | tf_op jit(solution)/shard_map/ppermute | solution.py:796
  23.5 2.0 %collective-permute-start.2 = (f32[2,16,512]{2,1,0:T(8,128)S(1)}, f32[2,16,512]{2,1,0:T(8,128)S(1)}, u32[]{:S(2)}, u32[]{:S(2)}) collective-permute-start(f32[2,16,512]{2,1,0:T(8,128)S(1)} %get-tuple-element.60), channel_id=1, source_target_pairs={{0,7},{1,2},{2,1},{3,4},{4,3},{5,6},{6,5},{7,0},{8,15},{9,10},{10,... | collective-permute-start | bytes 196616 | tf_op jit(solution)/shard_map/ppermute | solution.py:796
  25.5 1.6 %collective-permute-start.3 = (f32[2,16,512]{2,1,0:T(8,128)S(1)}, f32[2,16,512]{2,1,0:T(8,128)S(1)}, u32[]{:S(2)}, u32[]{:S(2)}) collective-permute-start(f32[2,16,512]{2,1,0:T(8,128)S(1)} %get-tuple-element.61), channel_id=1, source_target_pairs={{0,1},{1,0},{2,3},{3,2},{4,5},{5,4},{6,7},{7,6},{8,9},{9,8},{10,11... | collective-permute-start | bytes 196616 | tf_op jit(solution)/shard_map/ppermute | solution.py:796
  27.1 4.0 %local0.1 = (f32[32,16,512]{2,1,0:T(8,128)}, f32[32,16,512]{2,1,0:T(8,128)}, f32[2,128,128]{2,1,0:T(8,128)S(1)}, f32[2,128,128]{2,1,0:T(8,128)S(1)}) custom-call(s32[128]{0:T(128)} %bitcast.9, f32[32,16,512]{2,1,0:T(8,128)} %field_prev_hbm.1, f32[32,16,512]{2,1,0:T(8,128)} %adjoint_prev_hbm.1, f32[32,16,512]{2,1,0:T(8,128)} %speed2_hbm.5, ...), custom_call_target="tpu_custom_call" | custom-call | flops 8388608 | bytes 12582912 | tf_op jit(solution)/shard_map/local0/pallas_call | solution.py:440
  31.2 2.7 %border0.1 = (f32[32,16,512]{2,1,0:T(8,128)S(1)}, f32[32,16,512]{2,1,0:T(8,128)S(1)}, f32[32,16,512]{2,1,0:T(8,128)S(1)}, f32[2,4,32,128]{3,2,1,0:T(8,128)S(1)},...) custom-call(s32[128]{0:T(128)S(1)} %bitcast.11, ...), custom_call_target="tpu_custom_call" | custom-call | tf_op jit(solution)/shard_map/border0/pallas_call | solution.py:493
  34.7 0.8 %collective-permute-start.5 = (f32[2,4,32,128]{3,2,1,0:T(8,128)S(1)}, f32[2,4,32,128]{3,2,1,0:T(8,128)S(1)}, u32[]{:S(2)}, u32[]{:S(2)}) collective-permute-start(f32[2,4,32,128]{3,2,1,0:T(8,128)S(1)} %get-tuple-element.71), channel_id=1, source_target_pairs={{0,8},{8,0},{16,24},{24,16},{32,40},{40,32},{48,56},{56,48},{64,72... | collective-permute-start | bytes 393224 | tf_op jit(solution)/shard_map/ppermute | solution.py:796
  35.5 1.6 %collective-permute-start.6 = (f32[2,16,512]{2,1,0:T(8,128)S(1)}, f32[2,16,512]{2,1,0:T(8,128)S(1)}, u32[]{:S(2)}, u32[]{:S(2)}) collective-permute-start(f32[2,16,512]{2,1,0:T(8,128)S(1)} %get-tuple-element.72), channel_id=1, source_target_pairs={{0,7},{1,2},{2,1},{3,4},{4,3},{5,6},{6,5},{7,0},{8,15},{9,10},{10,... | collective-permute-start | bytes 196616 | tf_op jit(solution)/shard_map/ppermute | solution.py:796
  37.9 3.5 %local1.1 = (f32[32,16,512]{2,1,0:T(8,128)S(1)}, f32[32,16,512]{2,1,0:T(8,128)S(1)}, f32[2,128,128]{2,1,0:T(8,128)S(1)}, f32[2,128,128]{2,1,0:T(8,128)S(1)}) custom-call(s32[128]{0:T(128)S(1)} %bitcast.12, f32[32,16,512]{2,1,0:T(8,128)S(1)} %get-tuple-element.64.field.field_prev, f32[32,16,512]{2,1,0:T(8,128)} %field_prev.1, ...), custom_call_target="tpu_custom_call" | custom-call | flops 8388608 | bytes 12582912 | tf_op jit(solution)/shard_map/local1/pallas_call | solution.py:564
  41.4 1.0 %collective-permute-done.4.x_from_outer = f32[2,4,32,128]{3,2,1,0:T(8,128)S(1)} collective-permute-done((f32[2,4,32,128]{3,2,1,0:T(8,128)S(1)}, f32[2,4,32,128]{3,2,1,0:T(8,128)S(1)}, u32[]{:S(2)}, u32[]{:S(2)}) %collective-permute-start.4) | collective-permute-done | bytes 131104 | tf_op jit(solution)/shard_map/ppermute | solution.py:796
  43.1 1.3 %collective-permute-start.8 = (f32[2,4,32,128]{3,2,1,0:T(8,128)S(1)}, f32[2,4,32,128]{3,2,1,0:T(8,128)S(1)}, u32[]{:S(2)}, u32[]{:S(2)}) collective-permute-start(f32[2,4,32,128]{3,2,1,0:T(8,128)S(1)} %get-tuple-element.80), channel_id=1, source_target_pairs={{0,120},{8,16},{16,8},{24,32},{32,24},{40,48},{48,40},{56,64},{64,... | collective-permute-start | bytes 393224 | tf_op jit(solution)/shard_map/ppermute | solution.py:796
  44.4 1.8 %collective-permute-start.10 = (f32[2,16,512]{2,1,0:T(8,128)S(1)}, f32[2,16,512]{2,1,0:T(8,128)S(1)}, u32[]{:S(2)}, u32[]{:S(2)}) collective-permute-start(f32[2,16,512]{2,1,0:T(8,128)S(1)} %get-tuple-element.82), channel_id=1, source_target_pairs={{0,7},{1,2},{2,1},{3,4},{4,3},{5,6},{6,5},{7,0},{8,15},{9,10},{10,... | collective-permute-start | bytes 196616 | tf_op jit(solution)/shard_map/ppermute | solution.py:796
  46.3 3.5 %local2.1 = (f32[32,16,512]{2,1,0:T(8,128)S(1)}, f32[32,16,512]{2,1,0:T(8,128)S(1)}, f32[2,128,128]{2,1,0:T(8,128)S(1)}, f32[2,128,128]{2,1,0:T(8,128)S(1)}, f32...) custom-call(s32[128]{0:T(128)S(1)} %bitcast.13, f32[32,16,512]{2,1,0:T(8,128)S(1)} %get-tuple-element.74.field, ...), custom_call_target="tpu_custom_call" | custom-call | flops 8388608 | bytes 12582912 | tf_op jit(solution)/shard_map/local2/pallas_call | solution.py:564
  49.8 0.9 %collective-permute-done.8.x_from_outer = f32[2,4,32,128]{3,2,1,0:T(8,128)S(1)} collective-permute-done((f32[2,4,32,128]{3,2,1,0:T(8,128)S(1)}, f32[2,4,32,128]{3,2,1,0:T(8,128)S(1)}, u32[]{:S(2)}, u32[]{:S(2)}) %collective-permute-start.8) | collective-permute-done | bytes 131104 | tf_op jit(solution)/shard_map/ppermute | solution.py:796
  51.4 2.8 %correlation.1 = (f32[1024,128]{1,0:T(8,128)}, f32[2,128,128]{2,1,0:T(8,128)S(1)}, f32[32,16,512]{2,1,0:T(8,128)}, f32[32,16,512]{2,1,0:T(8,128)}) custom-call(s32[128]{0:T(128)S(1)} %bitcast.14, s32[1,128]{1,0:T(1,128)S(1)} %bitcast.15, f32[32,16,512]{2,1,0:T(8,128)S(1)} %get-tuple-element.84.field, f32[32,16,512]{2,1,0:T(8,128)S(1)} %get-tuple-element.85.adjoint, ...), custom_call_target="tpu_custom_call" | custom-call | tf_op jit(solution)/shard_map/correlation/pallas_call | solution.py:657
  54.3 7.2 %all-to-all-start.1 = ((f32[128,8,128]{2,1,0:T(8,128)}), f32[128,8,128]{2,1,0:T(8,128)S(1)}, u32[]{:S(2)}, u32[]{:S(2)}) async-start(f32[128,8,128]{2,1,0:T(8,128)} %bitcast.17), calls=%async_computation.1 | async-start | bytes 1048576 | tf_op jit(solution)/shard_map/all_to_all | solution.py:845
  61.5 4.9 %collective-permute-start.12 = (f32[2,4,32,128]{3,2,1,0:T(8,128)S(1)}, f32[2,4,32,128]{3,2,1,0:T(8,128)S(1)}, u32[]{:S(2)}, u32[]{:S(2)}) collective-permute-start(f32[2,4,32,128]{3,2,1,0:T(8,128)S(1)} %get-tuple-element.98), channel_id=1, source_target_pairs={{0,120},{8,16},{16,8},{24,32},{32,24},{40,48},{48,40},{56,64},{64,... | collective-permute-start | bytes 393224 | tf_op jit(solution)/shard_map/ppermute | solution.py:796
  66.4 2.0 %collective-permute-start.14 = (f32[2,16,512]{2,1,0:T(8,128)S(1)}, f32[2,16,512]{2,1,0:T(8,128)S(1)}, u32[]{:S(2)}, u32[]{:S(2)}) collective-permute-start(f32[2,16,512]{2,1,0:T(8,128)S(1)} %get-tuple-element.100), channel_id=1, source_target_pairs={{0,7},{1,2},{2,1},{3,4},{4,3},{5,6},{6,5},{7,0},{8,15},{9,10},{10,... | collective-permute-start | bytes 196616 | tf_op jit(solution)/shard_map/ppermute | solution.py:796
  68.4 1.6 %collective-permute-start.15 = (f32[2,16,512]{2,1,0:T(8,128)S(1)}, f32[2,16,512]{2,1,0:T(8,128)S(1)}, u32[]{:S(2)}, u32[]{:S(2)}) collective-permute-start(f32[2,16,512]{2,1,0:T(8,128)S(1)} %get-tuple-element.101), channel_id=1, source_target_pairs={{0,1},{1,0},{2,3},{3,2},{4,5},{5,4},{6,7},{7,6},{8,9},{9,8},{10,11... | collective-permute-start | bytes 196616 | tf_op jit(solution)/shard_map/ppermute | solution.py:796
  70.0 3.1 %local3.1 = (f32[32,16,512]{2,1,0:T(8,128)S(1)}, f32[32,16,512]{2,1,0:T(8,128)S(1)}, f32[4,32,128]{2,1,0:T(8,128)S(1)}, f32[4,32,128]{2,1,0:T(8,128)S(1)}, f32[2,16,512]{2,1,0:T(8,128)S(1)}) custom-call(s32[128]{0:T(128)} %bitcast.10, f32[32,16,512]{2,1,0:T(8,128)} %get-tuple-element.88.field_hbm, f32[32,16,512]{2,1,0:T(8,128)} %get-tuple-element.89.field_prev_hbm, ...), custom_call_target="tpu_custom_call" | custom-call | flops 8388608 | bytes 12582912 | tf_op jit(solution)/shard_map/local3/pallas_call | solution.py:717
  73.2 1.9 %collective-permute-done.12.x_from_outer = f32[2,4,32,128]{3,2,1,0:T(8,128)S(1)} collective-permute-done((f32[2,4,32,128]{3,2,1,0:T(8,128)S(1)}, f32[2,4,32,128]{3,2,1,0:T(8,128)S(1)}, u32[]{:S(2)}, u32[]{:S(2)}) %collective-permute-start.12) | collective-permute-done | bytes 131104 | tf_op jit(solution)/shard_map/ppermute | solution.py:796
  75.0 1.5 %finish.1 = (f32[32,16,512]{2,1,0:T(8,128)}, f32[32,16,512]{2,1,0:T(8,128)}) custom-call(f32[32,16,512]{2,1,0:T(8,128)S(1)} %get-tuple-element.93.field_in, f32[32,16,512]{2,1,0:T(8,128)S(1)} %get-tuple-element.94.adjoint_in, f32[4,32,128]{2,1,0:T(8,128)S(1)} %get-tuple-element.95.speed_first, f32[4,32,128]{2,1,0:T(8,128)S(1)} %get-tuple-element.96.speed_last, ...), custom_call_target="tpu_custom_call" | custom-call | tf_op jit(solution)/shard_map/finish/pallas_call | solution.py:776
  (26 shorter events, 3.9 us)
Async XLA Ops:
  5.4 25.8 %copy-start = (s32[1,128,1]{1,2,0:T(1,128)S(1)}, s32[1,128,1]{1,2,0:T(1,128)}, u32[]{:S(2)}) copy-start(s32[1,128,1]{1,2,0:T(1,128)} %param.17) | copy-start | bytes 1540
  5.4 25.8 %all-to-all-start = ((f32[128,1,768]{2,1,0:T(1,128)}), f32[128,1,768]{2,1,0:T(1,128)S(1)}, u32[]{:S(2)}, u32[]{:S(2)}) async-start(f32[128,1,768]{2,1,0:T(1,128)} %bitcast.16), calls=%async_computation | async-start | bytes 786432 | tf_op jit(solution)/shard_map/all_to_all | solution.py:820
  18.6 12.6 %collective-permute-start = (f32[2,4,32,128]{3,2,1,0:T(8,128)S(1)}, f32[2,4,32,128]{3,2,1,0:T(8,128)S(1)}, u32[]{:S(2)}, u32[]{:S(2)}) collective-permute-start(f32[2,4,32,128]{3,2,1,0:T(8,128)S(1)} %get-tuple-element.58), channel_id=1, source_target_pairs={{0,120},{8,16},{16,8},{24,32},{32,24},{40,48},{48,40},{56,64},{64,... | collective-permute-start | bytes 393224 | tf_op jit(solution)/shard_map/ppermute | solution.py:796
  23.5 7.7 %collective-permute-start.1 = (f32[2,4,32,128]{3,2,1,0:T(8,128)S(1)}, f32[2,4,32,128]{3,2,1,0:T(8,128)S(1)}, u32[]{:S(2)}, u32[]{:S(2)}) collective-permute-start(f32[2,4,32,128]{3,2,1,0:T(8,128)S(1)} %get-tuple-element.59), channel_id=1, source_target_pairs={{0,8},{8,0},{16,24},{24,16},{32,40},{40,32},{48,56},{56,48},{64,72... | collective-permute-start | bytes 393224 | tf_op jit(solution)/shard_map/ppermute | solution.py:796
  23.5 7.6 %collective-permute-start.2 = (f32[2,16,512]{2,1,0:T(8,128)S(1)}, f32[2,16,512]{2,1,0:T(8,128)S(1)}, u32[]{:S(2)}, u32[]{:S(2)}) collective-permute-start(f32[2,16,512]{2,1,0:T(8,128)S(1)} %get-tuple-element.60), channel_id=1, source_target_pairs={{0,7},{1,2},{2,1},{3,4},{4,3},{5,6},{6,5},{7,0},{8,15},{9,10},{10,... | collective-permute-start | bytes 196616 | tf_op jit(solution)/shard_map/ppermute | solution.py:796
  25.5 5.7 %collective-permute-start.3 = (f32[2,16,512]{2,1,0:T(8,128)S(1)}, f32[2,16,512]{2,1,0:T(8,128)S(1)}, u32[]{:S(2)}, u32[]{:S(2)}) collective-permute-start(f32[2,16,512]{2,1,0:T(8,128)S(1)} %get-tuple-element.61), channel_id=1, source_target_pairs={{0,1},{1,0},{2,3},{3,2},{4,5},{5,4},{6,7},{7,6},{8,9},{9,8},{10,11... | collective-permute-start | bytes 196616 | tf_op jit(solution)/shard_map/ppermute | solution.py:796
  33.9 8.5 %collective-permute-start.4 = (f32[2,4,32,128]{3,2,1,0:T(8,128)S(1)}, f32[2,4,32,128]{3,2,1,0:T(8,128)S(1)}, u32[]{:S(2)}, u32[]{:S(2)}) collective-permute-start(f32[2,4,32,128]{3,2,1,0:T(8,128)S(1)} %get-tuple-element.70), channel_id=1, source_target_pairs={{0,120},{8,16},{16,8},{24,32},{32,24},{40,48},{48,40},{56,64},{64,... | collective-permute-start | bytes 393224 | tf_op jit(solution)/shard_map/ppermute | solution.py:796
  34.7 7.7 %collective-permute-start.5 = (f32[2,4,32,128]{3,2,1,0:T(8,128)S(1)}, f32[2,4,32,128]{3,2,1,0:T(8,128)S(1)}, u32[]{:S(2)}, u32[]{:S(2)}) collective-permute-start(f32[2,4,32,128]{3,2,1,0:T(8,128)S(1)} %get-tuple-element.71), channel_id=1, source_target_pairs={{0,8},{8,0},{16,24},{24,16},{32,40},{40,32},{48,56},{56,48},{64,72... | collective-permute-start | bytes 393224 | tf_op jit(solution)/shard_map/ppermute | solution.py:796
  35.5 5.9 %collective-permute-start.6 = (f32[2,16,512]{2,1,0:T(8,128)S(1)}, f32[2,16,512]{2,1,0:T(8,128)S(1)}, u32[]{:S(2)}, u32[]{:S(2)}) collective-permute-start(f32[2,16,512]{2,1,0:T(8,128)S(1)} %get-tuple-element.72), channel_id=1, source_target_pairs={{0,7},{1,2},{2,1},{3,4},{4,3},{5,6},{6,5},{7,0},{8,15},{9,10},{10,... | collective-permute-start | bytes 196616 | tf_op jit(solution)/shard_map/ppermute | solution.py:796
  37.1 4.3 %collective-permute-start.7 = (f32[2,16,512]{2,1,0:T(8,128)S(1)}, f32[2,16,512]{2,1,0:T(8,128)S(1)}, u32[]{:S(2)}, u32[]{:S(2)}) collective-permute-start(f32[2,16,512]{2,1,0:T(8,128)S(1)} %get-tuple-element.73), channel_id=1, source_target_pairs={{0,1},{1,0},{2,3},{3,2},{4,5},{5,4},{6,7},{7,6},{8,9},{9,8},{10,11... | collective-permute-start | bytes 196616 | tf_op jit(solution)/shard_map/ppermute | solution.py:796
  43.1 7.6 %collective-permute-start.8 = (f32[2,4,32,128]{3,2,1,0:T(8,128)S(1)}, f32[2,4,32,128]{3,2,1,0:T(8,128)S(1)}, u32[]{:S(2)}, u32[]{:S(2)}) collective-permute-start(f32[2,4,32,128]{3,2,1,0:T(8,128)S(1)} %get-tuple-element.80), channel_id=1, source_target_pairs={{0,120},{8,16},{16,8},{24,32},{32,24},{40,48},{48,40},{56,64},{64,... | collective-permute-start | bytes 393224 | tf_op jit(solution)/shard_map/ppermute | solution.py:796
  44.4 6.3 %collective-permute-start.9 = (f32[2,4,32,128]{3,2,1,0:T(8,128)S(1)}, f32[2,4,32,128]{3,2,1,0:T(8,128)S(1)}, u32[]{:S(2)}, u32[]{:S(2)}) collective-permute-start(f32[2,4,32,128]{3,2,1,0:T(8,128)S(1)} %get-tuple-element.81), channel_id=1, source_target_pairs={{0,8},{8,0},{16,24},{24,16},{32,40},{40,32},{48,56},{56,48},{64,72... | collective-permute-start | bytes 393224 | tf_op jit(solution)/shard_map/ppermute | solution.py:796
  44.4 5.4 %collective-permute-start.10 = (f32[2,16,512]{2,1,0:T(8,128)S(1)}, f32[2,16,512]{2,1,0:T(8,128)S(1)}, u32[]{:S(2)}, u32[]{:S(2)}) collective-permute-start(f32[2,16,512]{2,1,0:T(8,128)S(1)} %get-tuple-element.82), channel_id=1, source_target_pairs={{0,7},{1,2},{2,1},{3,4},{4,3},{5,6},{6,5},{7,0},{8,15},{9,10},{10,... | collective-permute-start | bytes 196616 | tf_op jit(solution)/shard_map/ppermute | solution.py:796
  46.2 3.6 %collective-permute-start.11 = (f32[2,16,512]{2,1,0:T(8,128)S(1)}, f32[2,16,512]{2,1,0:T(8,128)S(1)}, u32[]{:S(2)}, u32[]{:S(2)}) collective-permute-start(f32[2,16,512]{2,1,0:T(8,128)S(1)} %get-tuple-element.83), channel_id=1, source_target_pairs={{0,1},{1,0},{2,3},{3,2},{4,5},{5,4},{6,7},{7,6},{8,9},{9,8},{10,11... | collective-permute-start | bytes 196616 | tf_op jit(solution)/shard_map/ppermute | solution.py:796
  54.3 22.2 %all-to-all-start.1 = ((f32[128,8,128]{2,1,0:T(8,128)}), f32[128,8,128]{2,1,0:T(8,128)S(1)}, u32[]{:S(2)}, u32[]{:S(2)}) async-start(f32[128,8,128]{2,1,0:T(8,128)} %bitcast.17), calls=%async_computation.1 | async-start | bytes 1048576 | tf_op jit(solution)/shard_map/all_to_all | solution.py:845
  61.5 13.5 %collective-permute-start.12 = (f32[2,4,32,128]{3,2,1,0:T(8,128)S(1)}, f32[2,4,32,128]{3,2,1,0:T(8,128)S(1)}, u32[]{:S(2)}, u32[]{:S(2)}) collective-permute-start(f32[2,4,32,128]{3,2,1,0:T(8,128)S(1)} %get-tuple-element.98), channel_id=1, source_target_pairs={{0,120},{8,16},{16,8},{24,32},{32,24},{40,48},{48,40},{56,64},{64,... | collective-permute-start | bytes 393224 | tf_op jit(solution)/shard_map/ppermute | solution.py:796
  66.4 8.6 %collective-permute-start.13 = (f32[2,4,32,128]{3,2,1,0:T(8,128)S(1)}, f32[2,4,32,128]{3,2,1,0:T(8,128)S(1)}, u32[]{:S(2)}, u32[]{:S(2)}) collective-permute-start(f32[2,4,32,128]{3,2,1,0:T(8,128)S(1)} %get-tuple-element.99), channel_id=1, source_target_pairs={{0,8},{8,0},{16,24},{24,16},{32,40},{40,32},{48,56},{56,48},{64,72... | collective-permute-start | bytes 393224 | tf_op jit(solution)/shard_map/ppermute | solution.py:796
  66.4 6.7 %collective-permute-start.14 = (f32[2,16,512]{2,1,0:T(8,128)S(1)}, f32[2,16,512]{2,1,0:T(8,128)S(1)}, u32[]{:S(2)}, u32[]{:S(2)}) collective-permute-start(f32[2,16,512]{2,1,0:T(8,128)S(1)} %get-tuple-element.100), channel_id=1, source_target_pairs={{0,7},{1,2},{2,1},{3,4},{4,3},{5,6},{6,5},{7,0},{8,15},{9,10},{10,... | collective-permute-start | bytes 196616 | tf_op jit(solution)/shard_map/ppermute | solution.py:796
  68.4 4.8 %collective-permute-start.15 = (f32[2,16,512]{2,1,0:T(8,128)S(1)}, f32[2,16,512]{2,1,0:T(8,128)S(1)}, u32[]{:S(2)}, u32[]{:S(2)}) collective-permute-start(f32[2,16,512]{2,1,0:T(8,128)S(1)} %get-tuple-element.101), channel_id=1, source_target_pairs={{0,1},{1,0},{2,3},{3,2},{4,5},{5,4},{6,7},{7,6},{8,9},{9,8},{10,11... | collective-permute-start | bytes 196616 | tf_op jit(solution)/shard_map/ppermute | solution.py:796
